TPU v7x, 32 devices: a whole 2x2x4 slice. The times are simulated.
32 devices in a mesh: blk: 8 (over y, x, core), sub: 4 (over z).
Axes of the slice: x: 2, y: 2, z: 4, core: 2. Of those that a mesh axis runs over, the one named last changes fastest.
Arguments:
- vorticity: float32 [3, 8, 32, 1024], P(None, 'blk', 'sub'), may hold values from -6 to 6
- velocity: float32 [3, 8, 32, 1024], P(None, 'blk', 'sub'), may hold values from -0.9 to 0.9
- gradient: float32 [9, 8, 32, 1024], P(None, 'blk', 'sub'), may hold values from -3 to 3
- neighbour: int32 [8, 6], P('blk'), may hold values from 0 to 7, as said below
Outputs:
- new_vorticity: float32 [3, 8, 32, 1024], P(None, 'blk', 'sub')
Inputs may be any that keep to these rules, and one draw needn't show every extreme that they name: The blocks form a periodic grid of blocks numbered along a space-filling curve; neighbour[b, 2a] and neighbour[b, 2a + 1] are the blocks beside block b below and above it along dimension a, so neighbour[neighbour[b, 2a], 2a + 1] = b and neighbour[neighbour[b, 2a + 1], 2a] = b.
All inputs are finite; a program needn't handle non-finite values.
Results may differ from a plain program's by a relative error of at most 0.0003.
Values sent between devices are 32-bit elements; how exact they have to be, the bound alone decides.
No kernel may reach another device: no remote copies, remote signals or barrier semaphores. Data moves between devices by JAX's collectives and lax.ppermute only.
A program may use at most 64 MiB of HBM per device.

v0:
```python
import jax
import jax.numpy as jnp
from jax import lax
from jax.sharding import PartitionSpec as P

B = 32


stretch_step = 0.25


def kernel(offset):
    a = jnp.abs(offset)
    near_part = 1.0 - 2.5 * a * a + 1.5 * a * a * a
    far_part = 0.5 * (2.0 - a) * (2.0 - a) * (1.0 - a)
    return jnp.where(a < 1.0, near_part, jnp.where(a < 2.0, far_part, 0.0))


def stretch(w, g):
    return jnp.stack(
        [
            w[i] + stretch_step * (g[3 * i] * w[0] + g[3 * i + 1] * w[1] + g[3 * i + 2] * w[2])
            for i in range(3)
        ]
    )


def pull_rows(wanted, summed_in, pieces_in):
    row_count = pieces_in[0].shape[1]
    block_ids = jnp.arange(row_count, dtype=jnp.int32)
    results = []
    for running, pieces, chosen in zip(summed_in, pieces_in, wanted):
        select_rows = (chosen[:, None] == block_ids[None, :]).astype(jnp.float32)
        picked = jnp.einsum("bm,cmxyz->cbxyz", select_rows, pieces, precision=lax.Precision.HIGHEST)
        results.append(picked)
    return tuple(results)


def block_pass(values, displace, neighbour, dim):
    length = values.shape[dim]
    face_id = 2 * (dim - 2)
    below_ids = neighbour[:, face_id]
    above_ids = neighbour[:, face_id + 1]
    stacked = jnp.concatenate([values, displace[None]], axis=0)
    low_cells = lax.slice_in_dim(stacked, 0, 2, axis=dim)
    high_cells = lax.slice_in_dim(stacked, length - 2, length, axis=dim)
    empty = jnp.zeros_like(low_cells)
    below_cells, above_cells = pull_rows(
        (below_ids, above_ids),
        (empty, empty),
        (
            lax.all_gather(high_cells, "blk", axis=1, tiled=True),
            lax.all_gather(low_cells, "blk", axis=1, tiled=True),
        ),
    )
    widened = jnp.concatenate([below_cells, stacked, above_cells], axis=dim)
    sources = widened[:3]
    shifts = widened[3]
    result = None
    for k in range(-2, 3):
        weighted = sources * kernel(k - shifts)[None]
        landed = lax.slice_in_dim(weighted, 2 - k, 2 - k + length, axis=dim)
        result = landed if result is None else result + landed
    return result


def shards(vorticity, velocity, gradient, neighbour):
    blocks_here = vorticity.shape[1]
    slab_cells = vorticity.shape[2]
    block_shape = (blocks_here, slab_cells, B, B)
    w = vorticity.reshape((3,) + block_shape)
    u = velocity.reshape((3,) + block_shape)
    g = gradient.reshape((9,) + block_shape)
    values = stretch(w, g)
    stacked = jnp.concatenate([values, u[0][None]], axis=0)
    pencils = lax.all_to_all(stacked, "sub", split_axis=3, concat_axis=2, tiled=True)
    after_x = block_pass(pencils[:3], pencils[3], neighbour, 2)
    values = lax.all_to_all(after_x, "sub", split_axis=2, concat_axis=3, tiled=True)
    values = block_pass(values, u[1], neighbour, 3)
    values = block_pass(values, u[2], neighbour, 4)
    return values.reshape(vorticity.shape)


def solution(mesh):
    return jax.shard_map(
        shards,
        mesh=mesh,
        in_specs=(
            P(None, "blk", "sub", None),
            P(None, "blk", "sub", None),
            P(None, "blk", "sub", None),
            P("blk", None),
        ),
        out_specs=P(None, "blk", "sub", None),
        check_vma=False,
    )
```

profile of v0, /device:TPU:0, one launch (start us, length us, event | category | flops | bytes accessed | tf_op | source)
XLA Modules:
  0.0 101.8 jit_solution(10625267584770468083)
XLA Ops:
  4.1 0.9 reshape.699
  5.0 6.4 %all-to-all-start = ((f32[4,1,8192]{2,1,0:T(1,128)}), f32[4,1,8192]{2,1,0:T(1,128)S(1)}, u32[]{:S(2)}, u32[]{:S(2)}) async-start(f32[4,1,8192]{2,1,0:T(1,128)} %reshape.699), calls=%async_computation | async-start | bytes 262144 | tf_op jit(solution)/shard_map/all_to_all | solution.py:76
  12.1 5.4 %all-to-all-done = f32[4,1,8192]{2,1,0:T(1,128)S(1)} async-done(((f32[4,1,8192]{2,1,0:T(1,128)}), f32[4,1,8192]{2,1,0:T(1,128)S(1)}, u32[]{:S(2)}, u32[]{:S(2)}) %all-to-all-start) | async-done | bytes 131104 | tf_op jit(solution)/shard_map/all_to_all | solution.py:76
  18.1 1.0 %reduce = f32[4,8192]{1,0:T(4,128)S(1)} reduce(f32[4,1,8192]{2,1,0:T(1,128)S(1)} %all-to-all-done, f32[]{:T(128)} %broadcast.658), dimensions={1}, to_apply=%all_to_all.24.reduce_sub_computation | reduce | bytes 262148 | tf_op jit(solution)/shard_map/all_to_all | solution.py:76
  19.7 9.3 %all_gather.18 = f32[4,8,2,8,32]{4,3,2,0,1:T(8,128)S(1)} all-gather(f32[4,1,2,8,32]{4,3,2,0,1:T(8,128)S(1)} %get-tuple-element.15), channel_id=1, replica_groups=mesh['blk'=8,'sub'=4] {'blk'}, dimensions={1}, use_global_device_ids=true | all-gather | bytes 73728 | tf_op jit(solution)/shard_map/all_gather | solution.py:52
  29.1 9.3 %all_gather.19 = f32[4,8,2,8,32]{4,3,2,0,1:T(8,128)S(1)} all-gather(f32[4,1,2,8,32]{4,3,2,0,1:T(8,128)S(1)} %get-tuple-element.16), channel_id=1, replica_groups=mesh['blk'=8,'sub'=4] {'blk'}, dimensions={1}, use_global_device_ids=true | all-gather | bytes 73728 | tf_op jit(solution)/shard_map/all_gather | solution.py:53
  38.3 1.1 %fusion.22 = f32[1,4,2,8,32]{4,0,3,2,1:T(1,128)S(1)} fusion(f32[4,8,2,8,32]{4,3,2,0,1:T(8,128)S(1)} %all_gather.18, s32[]{:T(128)} %bitcast.6), kind=kOutput, calls=%fused_computation.45 | convolution fusion | flops 196616 | bytes 73732 | tf_op jit(solution)/shard_map/bm,cmxyz->cbxyz/dot_general | solution.py:34
  39.4 1.0 %fusion.20 = f32[1,4,2,8,32]{4,0,3,2,1:T(1,128)S(1)} fusion(f32[4,8,2,8,32]{4,3,2,0,1:T(8,128)S(1)} %all_gather.19, s32[]{:T(128)} %bitcast.12), kind=kOutput, calls=%fused_computation.43 | convolution fusion | flops 196616 | bytes 73732 | tf_op jit(solution)/shard_map/bm,cmxyz->cbxyz/dot_general | solution.py:34
  40.6 0.8 copy-done.1
  41.9 0.9 slice-done.1
  43.0 0.8 reshape.701
  43.8 3.3 %all-to-all-start.1 = ((f32[4,1,6144]{2,1,0:T(1,128)}), f32[4,1,6144]{2,1,0:T(1,128)S(1)}, u32[]{:S(2)}, u32[]{:S(2)}) async-start(f32[4,1,6144]{2,1,0:T(1,128)} %reshape.701), calls=%async_computation.1 | async-start | bytes 196608 | tf_op jit(solution)/shard_map/all_to_all | solution.py:78
  47.3 5.8 %all-to-all-done.1 = f32[4,1,6144]{2,1,0:T(1,128)S(1)} async-done(((f32[4,1,6144]{2,1,0:T(1,128)}), f32[4,1,6144]{2,1,0:T(1,128)S(1)}, u32[]{:S(2)}, u32[]{:S(2)}) %all-to-all-start.1) | async-done | bytes 98336 | tf_op jit(solution)/shard_map/all_to_all | solution.py:78
  53.1 0.9 reduce.1
  54.4 8.3 %all_gather.21 = f32[4,8,8,2,32]{4,2,3,0,1:T(8,128)S(1)} all-gather(f32[4,1,8,2,32]{4,2,3,0,1:T(8,128)S(1)} %copy.36), channel_id=1, replica_groups=mesh['blk'=8,'sub'=4] {'blk'}, dimensions={1}, use_global_device_ids=true | all-gather | bytes 73728 | tf_op jit(solution)/shard_map/all_gather | solution.py:53
  62.7 9.3 %all_gather.20 = f32[4,8,8,2,32]{4,2,3,0,1:T(8,128)S(1)} all-gather(f32[4,1,8,2,32]{4,2,3,0,1:T(8,128)S(1)} %copy.35), channel_id=1, replica_groups=mesh['blk'=8,'sub'=4] {'blk'}, dimensions={1}, use_global_device_ids=true | all-gather | bytes 73728 | tf_op jit(solution)/shard_map/all_gather | solution.py:52
  72.0 0.9 fusion.16
  72.9 1.0 fusion.18
  74.2 0.8 copy-done.2
  75.5 0.9 slice-done.2
  77.4 8.3 %all_gather.23 = f32[4,8,8,32,2]{3,2,4,0,1:T(8,128)S(1)} all-gather(f32[4,1,8,32,2]{3,2,4,0,1:T(8,128)S(1)} %copy.38), channel_id=1, replica_groups=mesh['blk'=8,'sub'=4] {'blk'}, dimensions={1}, use_global_device_ids=true | all-gather | bytes 73728 | tf_op jit(solution)/shard_map/all_gather | solution.py:53
  85.7 9.5 %all_gather.22 = f32[4,8,8,32,2]{3,2,4,0,1:T(8,128)S(1)} all-gather(f32[4,1,8,32,2]{3,2,4,0,1:T(8,128)S(1)} %copy.37), channel_id=1, replica_groups=mesh['blk'=8,'sub'=4] {'blk'}, dimensions={1}, use_global_device_ids=true | all-gather | bytes 73728 | tf_op jit(solution)/shard_map/all_gather | solution.py:52
  95.2 0.9 fusion.14
  96.4 1.0 %fusion.12 = f32[1,4,8,32,2]{3,0,4,2,1:T(1,128)S(1)} fusion(f32[4,8,8,32,2]{3,2,4,0,1:T(8,128)S(1)} %all_gather.23, s32[]{:T(128)} %bitcast.48), kind=kOutput, calls=%fused_computation.35 | convolution fusion | flops 196616 | bytes 73732 | tf_op jit(solution)/shard_map/bm,cmxyz->cbxyz/dot_general | solution.py:34
  (82 shorter events, 13.2 us)
Async XLA Ops:
  0.8 0.9 copy-start.4
  1.7 1.0 copy-start.3
  5.0 6.5 %copy-start.5 = (s32[1,6]{1,0:T(1,128)S(1)}, s32[1,6]{1,0:T(1,128)}, u32[]{:S(2)}) copy-start(s32[1,6]{1,0:T(1,128)} %param.7) | copy-start | bytes 76
  5.0 12.5 %all-to-all-start = ((f32[4,1,8192]{2,1,0:T(1,128)}), f32[4,1,8192]{2,1,0:T(1,128)S(1)}, u32[]{:S(2)}, u32[]{:S(2)}) async-start(f32[4,1,8192]{2,1,0:T(1,128)} %reshape.699), calls=%async_computation | async-start | bytes 262144 | tf_op jit(solution)/shard_map/all_to_all | solution.py:76
  40.6 0.8 copy-start.1
  41.8 1.0 slice-start.1
  43.8 9.3 %all-to-all-start.1 = ((f32[4,1,6144]{2,1,0:T(1,128)}), f32[4,1,6144]{2,1,0:T(1,128)S(1)}, u32[]{:S(2)}, u32[]{:S(2)}) async-start(f32[4,1,6144]{2,1,0:T(1,128)} %reshape.701), calls=%async_computation.1 | async-start | bytes 196608 | tf_op jit(solution)/shard_map/all_to_all | solution.py:78
  74.1 0.9 copy-start.2
  75.4 1.0 %slice-start.2 = ((f32[4,1,8,36,32]{4,3,2,0,1:T(8,128)}), f32[3,1,8,36,32]{4,3,2,0,1:T(8,128)S(1)}, s32[]{:S(2)}) async-start(f32[4,1,8,36,32]{4,3,2,0,1:T(8,128)} %copy-done.2), calls=%async_computation.4 | async-start | bytes 983040 | tf_op jit(solution)/shard_map/slice | solution.py:57
  98.2 0.8 copy-start
  99.5 1.0 slice-start
where the time goes:
time: 103 us; the launch traced here: 102 us
  blocking collectives  54 us (52%)
  local copies, waits for them, and re-layouts  15.2 us (15%)
  waiting for transfers between devices  11.2 us (11%)
  starting transfers between devices  9.75 us (9%)
  matrix products  5.99 us (6%)
  other arithmetic  5.21 us (5%)
    all_gather x3, blocking collectives, block_pass(): lax.all_gather(high_cells, 'blk', axis=1, tiled=True)  28.1 us
    all_gather x3, blocking collectives, block_pass(): lax.all_gather(low_cells, 'blk', axis=1, tiled=True)  25.9 us
    all_to_all x1, starting transfers between devices, shards(): lax.all_to_all(stacked, 'sub', split_axis=3, concat_axis=2, tiled=True)  6.45 us
    unnamed x16, local copies, waits for them, and re-layouts  6.01 us
    dot_general x6, matrix products, pull_rows(): jnp.einsum('bm,cmxyz->cbxyz', select_rows, pieces, precision=lax.Precisio...  5.99 us
    all_to_all x1, waiting for transfers between devices, shards(): lax.all_to_all(after_x, 'sub', split_axis=2, concat_axis=3, tiled=True)  5.78 us
    all_to_all x1, waiting for transfers between devices, shards(): lax.all_to_all(stacked, 'sub', split_axis=3, concat_axis=2, tiled=True)  5.39 us
    all_to_all x1, starting transfers between devices, shards(): lax.all_to_all(after_x, 'sub', split_axis=2, concat_axis=3, tiled=True)  3.3 us
  transfers between devices with their start and end apart: 2, of which 2 were waited for; matrix products, arithmetic and copies ran while one was open for 1% of the time, Pallas kernels for 0%

commit v1 on v0

v1 whole, which is shorter than its diff:
```python
import functools

import jax
import jax.numpy as jnp
from jax import lax
from jax.experimental import pallas as pl
from jax.experimental.pallas import tpu as pltpu
from jax.sharding import PartitionSpec as P

B = 32
TILES = B * B // 128
stretch_step = 0.25

AFTER_Y, AFTER_Z, U1_Y, U1_Z, U2_Z = 0, 3, 6, 7, 8
FACES = 9
NEAR_Y, NEAR_Z = 9, 10
FAR, FAR_Y, FAR_Z = 11, 19, 20
SENT = 21


def iotas():
    return (
        lax.broadcasted_iota(jnp.int32, (8, 128), 0),
        lax.broadcasted_iota(jnp.int32, (8, 128), 1),
    )


def weights(u):
    a = jnp.abs(u)
    rest = 1.0 - a
    centre = 1.0 + a * a * (1.5 * a - 2.5)
    toward = a * (0.5 + a * (2.0 - 1.5 * a))
    away = -0.5 * a * rest * rest
    far = -0.5 * a * a * rest
    up = u >= 0.0
    return {
        0: centre,
        1: jnp.where(up, toward, away),
        -1: jnp.where(up, away, toward),
        2: jnp.where(up, far, 0.0),
        -2: jnp.where(up, 0.0, far),
    }


def lane(tile):
    return pl.ds(128 * tile, 128)


def y_face(tiles, lanes):
    return jnp.where(lanes < 64, tiles[0], tiles[TILES - 1])


def z_face(tiles, lanes):
    m = lanes & 3
    index = 32 * ((lanes >> 2) & 3) + jnp.where(m < 2, m, 28 + m)
    face = None
    for t, tile in enumerate(tiles):
        picked = jnp.take_along_axis(tile, index, axis=1)
        face = picked if face is None else jnp.where((lanes >> 4) == t, picked, face)
    return face


def first_kernel(slab, nb_ref, w_ref, u_ref, g_ref, after_ref, face_ref, near_ref, far_ref):
    rows, lanes = iotas()
    odd = lax.axis_index("sub") % 2 == 1
    meta = jnp.zeros((8, 128), jnp.float32)
    for j in range(6):
        meta = jnp.where(lanes == j, nb_ref[0, j].astype(jnp.float32), meta)
    after = [[], [], []]
    near, far = [], []
    for t in range(TILES):
        w = [w_ref[c, 0, :, lane(t)] for c in range(3)]
        weight = weights(u_ref[0, 0, :, lane(t)])
        ups, downs = [], []
        for c in range(3):
            q = w[c] + stretch_step * (
                g_ref[3 * c, 0, :, lane(t)] * w[0]
                + g_ref[3 * c + 1, 0, :, lane(t)] * w[1]
                + g_ref[3 * c + 2, 0, :, lane(t)] * w[2]
            )
            inside, up, down = q * weight[0], 0.0, 0.0
            for k in (1, 2):
                moved = pltpu.roll(q * weight[k], k, 0)
                spilt = rows < k if slab == 8 else rows >= slab
                inside = inside + jnp.where(spilt, 0.0, moved)
                up = up + jnp.where(spilt, moved, 0.0)
                moved = pltpu.roll(q * weight[-k], 8 - k, 0)
                spilt = rows >= 8 - k
                inside = inside + jnp.where(spilt, 0.0, moved)
                down = down + jnp.where(spilt, moved, 0.0)
            after[c].append(inside)
            after_ref[c, :, lane(t)] = inside
            ups.append(up)
            downs.append(down)
        rest = meta if t == 0 else 0.0
        packed_up, packed_down = rest, rest
        for c in (2, 1, 0):
            here = rows < 2 * c + 2
            shift = (2 * c - slab) % 8
            packed_up = jnp.where(here, pltpu.roll(ups[c], shift, 0) if shift else ups[c], packed_up)
            packed_down = jnp.where(here, pltpu.roll(downs[c], 2 * c + 2, 0), packed_down)
        near.append(jnp.where(odd, packed_down, packed_up))
        far.append(jnp.where(odd, packed_up, packed_down))
    for tiles, ref in ((near, near_ref), (far, far_ref)):
        for t in range(TILES):
            ref[t] = tiles[t]
        ref[TILES] = y_face(tiles, lanes)
        ref[TILES + 1] = z_face(tiles, lanes)
    for c in range(3):
        face_ref[AFTER_Y + c] = y_face(after[c], lanes)
        face_ref[AFTER_Z + c] = z_face(after[c], lanes)
    u1 = [u_ref[1, 0, :, lane(t)] for t in range(TILES)]
    u2 = [u_ref[2, 0, :, lane(t)] for t in range(TILES)]
    face_ref[U1_Y] = y_face(u1, lanes)
    face_ref[U1_Z] = z_face(u1, lanes)
    face_ref[U2_Z] = z_face(u2, lanes)


def last_kernel(slab, slabs, nb_ref, after_ref, u_ref, near_ref, all_ref, out_ref):
    rows, lanes = iotas()
    here = lax.axis_index("blk")
    place_in = lax.axis_index("sub")
    odd = place_in % 2 == 1
    near_row = jnp.where(odd, 0, slab - 2)
    far_row = jnp.where(odd, slab - 2, 0)

    def beside(block, face):
        tile = all_ref[block, FAR]
        only = jnp.where((rows == 6) & (lanes == face), tile, -1.0)
        return jnp.max(only).astype(jnp.int32)

    below_x = place_in == 0
    above_x = place_in == slabs - 1
    x_face = jnp.where(above_x, 1, 0)

    def far_block(block):
        return jnp.where(below_x | above_x, beside(block, x_face), block)

    def placed(tile, c, row):
        moved = pltpu.roll(tile, (row - 2 * c + 8) % 8, 0)
        return jnp.where((rows >= row) & (rows < row + 2), moved, 0.0)

    outer = far_block(here)
    after = [[], [], []]
    for t in range(TILES):
        near, far = near_ref[t], all_ref[outer, FAR + t]
        for c in range(3):
            after[c].append(
                after_ref[c, :, lane(t)] + placed(near, c, near_row) + placed(far, c, far_row)
            )

    ym, yp = nb_ref[0, 2], nb_ref[0, 3]
    zm, zp = nb_ref[0, 4], nb_ref[0, 5]
    from_above = lanes < 64

    def mixed(tile, far=False):
        if far:
            a, b = far_block(yp), far_block(ym)
        else:
            a, b = yp, ym
        return jnp.where(from_above, all_ref[a, tile], all_ref[b, tile])

    near, far = mixed(NEAR_Y), mixed(FAR_Y, True)
    weight = weights(mixed(U1_Y))
    one = jnp.where(from_above, weight[-1], weight[1])
    two = jnp.where(from_above, weight[-2], weight[2])
    y_spill = []
    for c in range(3):
        q = mixed(AFTER_Y + c) + placed(near, c, near_row) + placed(far, c, far_row)
        q1, q2 = q * one, q * two
        edge = jnp.where(lanes < 32, pltpu.roll(q1, 32, 1), pltpu.roll(q1, 96, 1))
        y_spill.append(
            pltpu.roll(q2, 64, 1) + jnp.where((lanes < 32) | (lanes >= 96), edge, 0.0)
        )
    after_y = [[None] * TILES for c in range(3)]
    moved = {}
    for t in range(TILES):
        weight = weights(u_ref[1, 0, :, lane(t)])
        for c in range(3):
            q = after[c][t]
            after_y[c][t] = q * weight[0]
            for k in (-2, -1, 1, 2):
                moved[c, t, k] = pltpu.roll(q * weight[k], (32 * k) % 128, 1)
    for t in range(TILES):
        for c in range(3):
            total = after_y[c][t]
            for k in (1, 2):
                cut = lanes < 32 * k
                other = moved[c, t - 1, k] if t > 0 else 0.0
                total = total + jnp.where(cut, other, moved[c, t, k])
                cut = lanes >= 128 - 32 * k
                other = moved[c, t + 1, -k] if t < TILES - 1 else 0.0
                total = total + jnp.where(cut, other, moved[c, t, -k])
            if t == 0:
                total = total + jnp.where(lanes < 64, y_spill[c], 0.0)
            if t == TILES - 1:
                total = total + jnp.where(lanes >= 64, y_spill[c], 0.0)
            after_y[c][t] = total

    place_z = lanes & 3
    y_cell = lanes >> 2
    from_above = place_z < 2
    upper = y_cell < 16
    zpp, zpm = beside(zp, 3), beside(zp, 2)
    zmp, zmm = beside(zm, 3), beside(zm, 2)
    far_zp, far_zm = far_block(zp), far_block(zm)
    far_zpp, far_zpm = far_block(zpp), far_block(zpm)
    far_zmp, far_zmm = far_block(zmp), far_block(zmm)

    def face(tile, a, b):
        return jnp.where(from_above, all_ref[a, tile], all_ref[b, tile])

    def corner(tile, a, b, c, d):
        return jnp.where(upper, face(tile, a, b), face(tile, c, d))

    near, far = face(NEAR_Z, zp, zm), face(FAR_Z, far_zp, far_zm)
    u1 = face(U1_Z, zp, zm)
    u2 = face(U2_Z, zp, zm)
    corner_near = corner(NEAR_Z, zpp, zmp, zpm, zmm)
    corner_far = corner(FAR_Z, far_zpp, far_zmp, far_zpm, far_zmm)
    corner_u1 = corner(U1_Z, zpp, zmp, zpm, zmm)
    own_weight = weights(u1)
    corner_weight = weights(corner_u1)
    weight = weights(u2)
    one = jnp.where(from_above, weight[-1], weight[1])
    two = jnp.where(from_above, weight[-2], weight[2])
    z_spill = []
    for c in range(3):
        q = face(AFTER_Z + c, zp, zm) + placed(near, c, near_row) + placed(far, c, far_row)
        qc = (
            corner(AFTER_Z + c, zpp, zmp, zpm, zmm)
            + placed(corner_near, c, near_row)
            + placed(corner_far, c, far_row)
        )
        total = q * own_weight[0]
        for k in (-2, -1, 1, 2):
            outside = y_cell >= B - k if k > 0 else y_cell < -k
            source = jnp.where(outside, qc * corner_weight[k], q * own_weight[k])
            total = total + pltpu.roll(source, (4 * k) % 128, 1)
        q1, q2 = total * one, total * two
        spill = jnp.where(from_above, pltpu.roll(q2, 126, 1), pltpu.roll(q2, 2, 1))
        edge = jnp.where(place_z == 0, pltpu.roll(q1, 125, 1), pltpu.roll(q1, 3, 1))
        z_spill.append(spill + jnp.where((place_z == 0) | (place_z == 3), edge, 0.0))

    z_cell = lanes & 31
    at_face = (z_cell < 2) | (z_cell >= 30)
    slot = jnp.where(z_cell < 2, z_cell, jnp.where(z_cell >= 30, z_cell - 28, 0))
    for t in range(TILES):
        weight = weights(u_ref[2, 0, :, lane(t)])
        index = 16 * t + 4 * (lanes >> 5) + slot
        for c in range(3):
            q = after_y[c][t]
            total = q * weight[0]
            for k in (1, 2):
                moved = pltpu.roll(q * weight[k], k, 1)
                total = total + jnp.where(z_cell >= k, moved, 0.0)
                moved = pltpu.roll(q * weight[-k], 128 - k, 1)
                total = total + jnp.where(z_cell < B - k, moved, 0.0)
            spill = jnp.take_along_axis(z_spill[c], index, axis=1)
            out_ref[c, 0, :, lane(t)] = total + jnp.where(at_face, spill, 0.0)


def shards(slabs, vorticity, velocity, gradient, neighbour):
    slab = vorticity.shape[2]
    if slab < 8:
        room = ((0, 0), (0, 0), (0, 8 - slab), (0, 0))
        vorticity, velocity, gradient = (
            jnp.pad(a, room) for a in (vorticity, velocity, gradient)
        )
    vmem = pl.BlockSpec(memory_space=pltpu.VMEM)
    smem = pl.BlockSpec(memory_space=pltpu.SMEM)

    def tiles(count):
        return jax.ShapeDtypeStruct((count, 8, 128), jnp.float32)

    after, faces, near, far = pl.pallas_call(
        functools.partial(first_kernel, slab),
        out_shape=(
            jax.ShapeDtypeStruct((3, 8, B * B), jnp.float32),
            tiles(FACES),
            tiles(TILES + 2),
            tiles(TILES + 2),
        ),
        in_specs=[smem, vmem, vmem, vmem],
        out_specs=(vmem, vmem, vmem, vmem),
    )(neighbour, vorticity, velocity, gradient)
    far = lax.ppermute(
        far,
        "sub",
        [p for i in range(1, slabs, 2) for p in ((i, (i + 1) % slabs), ((i + 1) % slabs, i))],
    )
    near = lax.ppermute(
        near, "sub", [p for i in range(0, slabs, 2) for p in ((i, i + 1), (i + 1, i))]
    )
    sent = jnp.concatenate([faces, near[TILES:], far], axis=0)
    everything = lax.all_gather(sent, "blk")
    room = everything.size * 4 + (8 << 20)
    out = pl.pallas_call(
        functools.partial(last_kernel, slab, slabs),
        out_shape=jax.ShapeDtypeStruct((3, 1, 8, B * B), jnp.float32),
        in_specs=[smem, vmem, vmem, vmem, vmem],
        out_specs=vmem,
        compiler_params=pltpu.CompilerParams(vmem_limit_bytes=room),
    )(neighbour, after, velocity, near, everything)
    return out[:, :, :slab]


def solution(mesh):
    return jax.shard_map(
        functools.partial(shards, mesh.shape["sub"]),
        mesh=mesh,
        in_specs=(
            P(None, "blk", "sub", None),
            P(None, "blk", "sub", None),
            P(None, "blk", "sub", None),
            P("blk", None),
        ),
        out_specs=P(None, "blk", "sub", None),
        check_vma=False,
    )
```

time: 103 us -> 24.9 us (0.24)
  blocking collectives: 54 us -> 10.4 us
  local copies, waits for them, and re-layouts: 15.2 us -> 0.66 us
  waiting for transfers between devices: 11.2 us -> 3.53 us
  matrix products: 5.99 us -> 0 us
  other arithmetic: 5.21 us -> 0.77 us
  starting transfers between devices: 9.75 us -> 5.5 us
  Pallas kernels: 0 us -> 3.78 us
    all_gather x6 -> x1, blocking collectives: 54 us -> 10.4 us  [shards(): everything = lax.all_gather(sent, 'blk')]
    all_to_all x2 -> x0, waiting for transfers between devices: 11.2 us -> none  [the longest x1 5.78 us: shards(): lax.all_to_all(after_x, 'sub', split_axis=2, concat_axis=3, tiled=True)]
    all_to_all x2 -> x0, starting transfers between devices: 9.75 us -> none  [the longest x1 6.45 us: shards(): lax.all_to_all(stacked, 'sub', split_axis=3, concat_axis=2, tiled=True)]
    dot_general x6 -> x0, matrix products: 5.99 us -> none  [pull_rows(): jnp.einsum('bm,cmxyz->cbxyz', select_rows, pieces, precision=lax.Precisio...]
    ppermute x0 -> x2, starting transfers between devices: none -> 5.5 us  [the longest x1 3.02 us: shards(): lax.ppermute(near, 'sub', [p for i in range(0, slabs, 2) for p in ((i, i...]
    slice x35 -> x1, local copies, waits for them, and re-layouts: 5.45 us -> 0.01 us  [shards(): sent = jnp.concatenate([faces, near[TILES:], far], axis=0)]
    unnamed x16 -> x6, local copies, waits for them, and re-layouts: 6.01 us -> 0.66 us
    pallas_call x0 -> x2, Pallas kernels: none -> 3.78 us  [the longest x1 1.94 us: shards(): pl.pallas_call(functools.partial(first_kernel, slab), out_shape=(jax.Shap...]
  transfers between devices with their start and end apart: 2 -> 2, of which waited for: 2 -> 1; matrix products, arithmetic and copies ran while one was open for 1% -> 0% of each run, Pallas kernels for 0% -> 0%
where the time goes in v1:
time: 24.9 us; the launch traced here: 24.7 us
  blocking collectives  10.4 us (42%)
  starting transfers between devices  5.5 us (22%)
  Pallas kernels  3.78 us (15%)
  waiting for transfers between devices  3.53 us (14%)
  other arithmetic  0.77 us (3%)
  local copies, waits for them, and re-layouts  0.66 us (3%)
    all_gather x1, blocking collectives, shards(): everything = lax.all_gather(sent, 'blk')  10.4 us
    ppermute x1, waiting for transfers between devices, shards(): lax.ppermute(far, 'sub', [p for i in range(1, slabs, 2) for p in ((i, (i...  3.53 us
    ppermute x1, starting transfers between devices, shards(): lax.ppermute(near, 'sub', [p for i in range(0, slabs, 2) for p in ((i, i...  3.02 us
    ppermute x1, starting transfers between devices, shards(): lax.ppermute(far, 'sub', [p for i in range(1, slabs, 2) for p in ((i, (i...  2.47 us
    pallas_call x1, Pallas kernels, shards(): pl.pallas_call(functools.partial(first_kernel, slab), out_shape=(jax.Shap...  1.94 us
    pallas_call x1, Pallas kernels, shards(): pl.pallas_call(functools.partial(last_kernel, slab, slabs), out_shape=jax...  1.84 us
    concatenate x1, other arithmetic, shards(): sent = jnp.concatenate([faces, near[TILES:], far], axis=0)  0.77 us
    unnamed x6, local copies, waits for them, and re-layouts  0.66 us
  transfers between devices with their start and end apart: 2, of which 1 were waited for; matrix products, arithmetic and copies ran while one was open for 0% of the time, Pallas kernels for 0%

profile of v1, /device:TPU:0, one launch (start us, length us, event | category | flops | bytes accessed | tf_op | source)
XLA Modules:
  0.0 24.7 jit_solution(11389459810731991893)
XLA Ops:
  0.0 1.9 %shard_map.46 = (f32[3,8,1024]{2,1,0:T(8,128)}, f32[9,8,128]{2,1,0:T(8,128)}, f32[10,8,128]{2,1,0:T(8,128)}, f32[10,8,128]{2,1,0:T(8,128)}) custom-call(s32[1,6]{1,0:T(1,128)} %nb_ref.3, f32[3,1,8,1024]{3,2,1,0:T(8,128)} %w_ref.1, f32[3,1,8,1024]{3,2,1,0:T(8,128)} %u_ref.3, f32[9,1,8,1024]{3,2,1,0:T(8,128)} %g_ref.1), custom_call_target="tpu_custom_call" | custom-call | tf_op jit(solution)/shard_map/pallas_call | solution.py:276
  1.9 3.0 %collective-permute-start = (f32[10,8,128]{2,1,0:T(8,128)}, f32[10,8,128]{2,1,0:T(8,128)S(1)}, u32[]{:S(2)}, u32[]{:S(2)}) collective-permute-start(f32[10,8,128]{2,1,0:T(8,128)} %get-tuple-element.10), channel_id=1, source_target_pairs={{0,1},{1,0},{2,3},{3,2},{4,5},{5,4},{6,7},{7,6},{8,9},{9,8},{10,11... | collective-permute-start | bytes 122888 | tf_op jit(solution)/shard_map/ppermute | solution.py:292
  5.0 2.5 %collective-permute-start.1 = (f32[10,8,128]{2,1,0:T(8,128)}, f32[10,8,128]{2,1,0:T(8,128)S(1)}, u32[]{:S(2)}, u32[]{:S(2)}) collective-permute-start(f32[10,8,128]{2,1,0:T(8,128)} %get-tuple-element.12), channel_id=1, source_target_pairs={{1,2},{2,1},{3,0},{0,3},{5,6},{6,5},{7,4},{4,7},{9,10},{10,9},{11,... | collective-permute-start | bytes 122888 | tf_op jit(solution)/shard_map/ppermute | solution.py:287
  7.4 0.0 collective-permute-done.near_ref
  7.4 3.5 %collective-permute-done.1 = f32[10,8,128]{2,1,0:T(8,128)S(1)} collective-permute-done((f32[10,8,128]{2,1,0:T(8,128)}, f32[10,8,128]{2,1,0:T(8,128)S(1)}, u32[]{:S(2)}, u32[]{:S(2)}) %collective-permute-start.1) | collective-permute-done | bytes 40992 | tf_op jit(solution)/shard_map/ppermute | solution.py:287
  11.0 0.8 %pad_maximum_fusion = f32[21,8,128]{2,1,0:T(8,128)S(1)} fusion(f32[10,8,128]{2,1,0:T(8,128)S(1)} %collective-permute-done.1, f32[2,8,128]{2,1,0:T(8,128)S(1)} %slice.4, f32[9,8,128]{2,1,0:T(8,128)} %get-tuple-element.11), kind=kLoop, calls=%fused_computation | loop fusion | flops 43008 | bytes 172032 | tf_op jit(solution)/shard_map/concatenate | solution.py:295
  11.7 0.0 copy-start
  11.8 0.0 copy-start.1
  11.8 10.4 %all-gather = f32[168,8,128]{2,1,0:T(8,128)S(1)} all-gather(f32[21,8,128]{2,1,0:T(8,128)S(1)} %pad_maximum_fusion), channel_id=2, replica_groups=mesh['blk'=8,'sub'=4] {'blk'}, dimensions={0}, use_global_device_ids=true | all-gather | bytes 774144 | tf_op jit(solution)/shard_map/all_gather | solution.py:296
  22.2 0.0 copy-start.2
  22.2 0.0 copy-done
  22.2 0.0 copy-done.1
  22.2 0.6 %copy-done.2 = s32[1,6]{1,0:T(1,128)S(1)} copy-done((s32[1,6]{1,0:T(1,128)S(1)}, s32[1,6]{1,0:T(1,128)}, u32[]{:S(2)}) %copy-start.2) | copy-done | bytes 48
  22.8 1.8 %shard_map.47 = f32[3,1,8,1024]{3,2,1,0:T(8,128)} custom-call(s32[1,6]{1,0:T(1,128)S(1)} %copy-done.2, f32[3,8,1024]{2,1,0:T(8,128)S(1)} %copy-done.1, f32[3,1,8,1024]{3,2,1,0:T(8,128)S(1)} %copy-done, f32[10,8,128]{2,1,0:T(8,128)S(1)} %collective-permute-done.near_ref, f32[8,21,8,128]{3,2,1,0:T(8,128)S(1)} %bitcast.1), custom_call_target="tpu_custom_call" | custom-call | tf_op jit(solution)/shard_map/pallas_call | solution.py:298
  (1 shorter events, 0.0 us)
Async XLA Ops:
  1.9 5.5 %collective-permute-start = (f32[10,8,128]{2,1,0:T(8,128)}, f32[10,8,128]{2,1,0:T(8,128)S(1)}, u32[]{:S(2)}, u32[]{:S(2)}) collective-permute-start(f32[10,8,128]{2,1,0:T(8,128)} %get-tuple-element.10), channel_id=1, source_target_pairs={{0,1},{1,0},{2,3},{3,2},{4,5},{5,4},{6,7},{7,6},{8,9},{9,8},{10,11... | collective-permute-start | bytes 122888 | tf_op jit(solution)/shard_map/ppermute | solution.py:292
  5.0 6.0 %collective-permute-start.1 = (f32[10,8,128]{2,1,0:T(8,128)}, f32[10,8,128]{2,1,0:T(8,128)S(1)}, u32[]{:S(2)}, u32[]{:S(2)}) collective-permute-start(f32[10,8,128]{2,1,0:T(8,128)} %get-tuple-element.12), channel_id=1, source_target_pairs={{1,2},{2,1},{3,0},{0,3},{5,6},{6,5},{7,4},{4,7},{9,10},{10,9},{11,... | collective-permute-start | bytes 122888 | tf_op jit(solution)/shard_map/ppermute | solution.py:287
  11.7 10.4 %copy-start = (f32[3,1,8,1024]{3,2,1,0:T(8,128)S(1)}, f32[3,1,8,1024]{3,2,1,0:T(8,128)}, u32[]{:S(2)}) copy-start(f32[3,1,8,1024]{3,2,1,0:T(8,128)} %u_ref.3) | copy-start | bytes 294916
  11.8 10.4 %copy-start.1 = (f32[3,8,1024]{2,1,0:T(8,128)S(1)}, f32[3,8,1024]{2,1,0:T(8,128)}, u32[]{:S(2)}) copy-start(f32[3,8,1024]{2,1,0:T(8,128)} %get-tuple-element.9.after_ref) | copy-start | bytes 294916
  22.2 0.7 %copy-start.2 = (s32[1,6]{1,0:T(1,128)S(1)}, s32[1,6]{1,0:T(1,128)}, u32[]{:S(2)}) copy-start(s32[1,6]{1,0:T(1,128)} %nb_ref.3) | copy-start | bytes 76

commit v2 on v1

--- a/solution.py
+++ b/solution.py
@@ -60,7 +60,17 @@
     return face
 
 
-def first_kernel(slab, nb_ref, w_ref, u_ref, g_ref, after_ref, face_ref, near_ref, far_ref):
+def first_kernel(slab, *refs):
+    here, (u_ref, after_ref, face_ref, near_ref, far_ref) = refs[:4], refs[4:9]
+    nb_ref, w_ref, g_ref, sems = refs[9:]
+    copies = [
+        pltpu.make_async_copy(source, target, sems.at[n])
+        for n, (source, target) in enumerate(zip(here, (nb_ref, w_ref, u_ref, g_ref)))
+    ]
+    for copy in copies:
+        copy.start()
+    for copy in copies:
+        copy.wait()
     rows, lanes = iotas()
     odd = lax.axis_index("sub") % 2 == 1
     meta = jnp.zeros((8, 128), jnp.float32)
@@ -116,57 +126,99 @@
     face_ref[U2_Z] = z_face(u2, lanes)
 
 
-def last_kernel(slab, slabs, nb_ref, after_ref, u_ref, near_ref, all_ref, out_ref):
+def last_kernel(slab, slabs, relative, after_ref, u_ref, near_ref, *refs):
+    block_refs, out_ref = refs[:-1], refs[-1]
     rows, lanes = iotas()
     here = lax.axis_index("blk")
     place_in = lax.axis_index("sub")
     odd = place_in % 2 == 1
     near_row = jnp.where(odd, 0, slab - 2)
     far_row = jnp.where(odd, slab - 2, 0)
-
-    def beside(block, face):
-        tile = all_ref[block, FAR]
-        only = jnp.where((rows == 6) & (lanes == face), tile, -1.0)
-        return jnp.max(only).astype(jnp.int32)
-
     below_x = place_in == 0
     above_x = place_in == slabs - 1
+    at_end = below_x | above_x
     x_face = jnp.where(above_x, 1, 0)
-
-    def far_block(block):
-        return jnp.where(below_x | above_x, beside(block, x_face), block)
+    base = here if relative else 0
+
+    def over_blocks(step, carry):
+        if relative:
+            for slot, ref in enumerate(block_refs):
+                carry = step(slot, lambda tile, ref=ref: ref[tile], carry)
+            return carry
+        (ref,) = block_refs
+        return lax.fori_loop(
+            0, ref.shape[0], lambda slot, c: step(slot, lambda tile: ref[slot, tile], c), carry
+        )
 
     def placed(tile, c, row):
         moved = pltpu.roll(tile, (row - 2 * c + 8) % 8, 0)
         return jnp.where((rows >= row) & (rows < row + 2), moved, 0.0)
 
-    outer = far_block(here)
+    from_above_y = lanes < 64
+    place_z = lanes & 3
+    y_cell = lanes >> 2
+    from_above_z = place_z < 2
+    y_face_id = jnp.where(y_cell < 16, 3, 2)
+    x_face_id = jnp.full((8, 128), x_face, jnp.int32)
+
+    def beside(tile, face_id):
+        row = jnp.broadcast_to(tile[6:7], (8, 128))
+        return jnp.take_along_axis(row, face_id, axis=1).astype(jnp.int32) ^ base
+
+    slot_y = beside(near_ref[0], jnp.where(from_above_y, 3, 2))
+    slot_z = beside(near_ref[0], jnp.where(from_above_z, 5, 4))
+    outer = jnp.where(at_end, beside(near_ref[0], x_face_id), here ^ base)
+
+    def find_corner(slot, tile_at, found):
+        return jnp.where(slot_z == slot, beside(tile_at(FAR), y_face_id), found)
+
+    slot_c = over_blocks(find_corner, slot_z)
+    slots = (slot_y, slot_z, slot_c)
+
+    def find_far(slot, tile_at, found):
+        there = beside(tile_at(FAR), x_face_id)
+        return tuple(
+            jnp.where(at_end & (start == slot), there, f) for start, f in zip(slots, found)
+        )
+
+    far_y, far_z, far_c = over_blocks(find_far, slots)
+
+    wanted = (
+        [(slot_y, t) for t in (AFTER_Y, AFTER_Y + 1, AFTER_Y + 2, U1_Y, NEAR_Y)]
+        + [(far_y, FAR_Y)]
+        + [(slot_z, t) for t in (AFTER_Z, AFTER_Z + 1, AFTER_Z + 2, U1_Z, U2_Z, NEAR_Z)]
+        + [(far_z, FAR_Z)]
+        + [(slot_c, t) for t in (AFTER_Z, AFTER_Z + 1, AFTER_Z + 2, U1_Z, NEAR_Z)]
+        + [(far_c, FAR_Z)]
+        + [(outer, FAR + t) for t in range(TILES)]
+    )
+
+    def pick(slot, tile_at, picked):
+        return tuple(
+            jnp.where(which == slot, tile_at(tile), p) for (which, tile), p in zip(wanted, picked)
+        )
+
+    zero = jnp.zeros((8, 128), jnp.float32)
+    picked = over_blocks(pick, (zero,) * len(wanted))
+    y_after, (y_u1, y_near, y_far) = picked[0:3], picked[3:6]
+    z_after, (z_u1, z_u2, z_near, z_far) = picked[6:9], picked[9:13]
+    c_after, (c_u1, c_near, c_far) = picked[13:16], picked[16:19]
+    far_tiles = picked[19:]
+
     after = [[], [], []]
     for t in range(TILES):
-        near, far = near_ref[t], all_ref[outer, FAR + t]
+        near, far = near_ref[t], far_tiles[t]
         for c in range(3):
             after[c].append(
                 after_ref[c, :, lane(t)] + placed(near, c, near_row) + placed(far, c, far_row)
             )
 
-    ym, yp = nb_ref[0, 2], nb_ref[0, 3]
-    zm, zp = nb_ref[0, 4], nb_ref[0, 5]
-    from_above = lanes < 64
-
-    def mixed(tile, far=False):
-        if far:
-            a, b = far_block(yp), far_block(ym)
-        else:
-            a, b = yp, ym
-        return jnp.where(from_above, all_ref[a, tile], all_ref[b, tile])
-
-    near, far = mixed(NEAR_Y), mixed(FAR_Y, True)
-    weight = weights(mixed(U1_Y))
-    one = jnp.where(from_above, weight[-1], weight[1])
-    two = jnp.where(from_above, weight[-2], weight[2])
+    weight = weights(y_u1)
+    one = jnp.where(from_above_y, weight[-1], weight[1])
+    two = jnp.where(from_above_y, weight[-2], weight[2])
     y_spill = []
     for c in range(3):
-        q = mixed(AFTER_Y + c) + placed(near, c, near_row) + placed(far, c, far_row)
+        q = y_after[c] + placed(y_near, c, near_row) + placed(y_far, c, far_row)
         q1, q2 = q * one, q * two
         edge = jnp.where(lanes < 32, pltpu.roll(q1, 32, 1), pltpu.roll(q1, 96, 1))
         y_spill.append(
@@ -197,67 +249,45 @@
                 total = total + jnp.where(lanes >= 64, y_spill[c], 0.0)
             after_y[c][t] = total
 
-    place_z = lanes & 3
-    y_cell = lanes >> 2
-    from_above = place_z < 2
-    upper = y_cell < 16
-    zpp, zpm = beside(zp, 3), beside(zp, 2)
-    zmp, zmm = beside(zm, 3), beside(zm, 2)
-    far_zp, far_zm = far_block(zp), far_block(zm)
-    far_zpp, far_zpm = far_block(zpp), far_block(zpm)
-    far_zmp, far_zmm = far_block(zmp), far_block(zmm)
-
-    def face(tile, a, b):
-        return jnp.where(from_above, all_ref[a, tile], all_ref[b, tile])
-
-    def corner(tile, a, b, c, d):
-        return jnp.where(upper, face(tile, a, b), face(tile, c, d))
-
-    near, far = face(NEAR_Z, zp, zm), face(FAR_Z, far_zp, far_zm)
-    u1 = face(U1_Z, zp, zm)
-    u2 = face(U2_Z, zp, zm)
-    corner_near = corner(NEAR_Z, zpp, zmp, zpm, zmm)
-    corner_far = corner(FAR_Z, far_zpp, far_zmp, far_zpm, far_zmm)
-    corner_u1 = corner(U1_Z, zpp, zmp, zpm, zmm)
-    own_weight = weights(u1)
-    corner_weight = weights(corner_u1)
-    weight = weights(u2)
-    one = jnp.where(from_above, weight[-1], weight[1])
-    two = jnp.where(from_above, weight[-2], weight[2])
+    own_weight = weights(z_u1)
+    corner_weight = weights(c_u1)
+    weight = weights(z_u2)
+    one = jnp.where(from_above_z, weight[-1], weight[1])
+    two = jnp.where(from_above_z, weight[-2], weight[2])
     z_spill = []
     for c in range(3):
-        q = face(AFTER_Z + c, zp, zm) + placed(near, c, near_row) + placed(far, c, far_row)
-        qc = (
-            corner(AFTER_Z + c, zpp, zmp, zpm, zmm)
-            + placed(corner_near, c, near_row)
-            + placed(corner_far, c, far_row)
-        )
+        q = z_after[c] + placed(z_near, c, near_row) + placed(z_far, c, far_row)
+        qc = c_after[c] + placed(c_near, c, near_row) + placed(c_far, c, far_row)
         total = q * own_weight[0]
         for k in (-2, -1, 1, 2):
             outside = y_cell >= B - k if k > 0 else y_cell < -k
             source = jnp.where(outside, qc * corner_weight[k], q * own_weight[k])
             total = total + pltpu.roll(source, (4 * k) % 128, 1)
         q1, q2 = total * one, total * two
-        spill = jnp.where(from_above, pltpu.roll(q2, 126, 1), pltpu.roll(q2, 2, 1))
+        spill = jnp.where(from_above_z, pltpu.roll(q2, 126, 1), pltpu.roll(q2, 2, 1))
         edge = jnp.where(place_z == 0, pltpu.roll(q1, 125, 1), pltpu.roll(q1, 3, 1))
         z_spill.append(spill + jnp.where((place_z == 0) | (place_z == 3), edge, 0.0))
 
     z_cell = lanes & 31
     at_face = (z_cell < 2) | (z_cell >= 30)
-    slot = jnp.where(z_cell < 2, z_cell, jnp.where(z_cell >= 30, z_cell - 28, 0))
+    place = jnp.where(z_cell < 2, z_cell, jnp.where(z_cell >= 30, z_cell - 28, 0))
     for t in range(TILES):
         weight = weights(u_ref[2, 0, :, lane(t)])
-        index = 16 * t + 4 * (lanes >> 5) + slot
+        index = 16 * t + 4 * (lanes >> 5) + place
         for c in range(3):
             q = after_y[c][t]
             total = q * weight[0]
             for k in (1, 2):
-                moved = pltpu.roll(q * weight[k], k, 1)
-                total = total + jnp.where(z_cell >= k, moved, 0.0)
-                moved = pltpu.roll(q * weight[-k], 128 - k, 1)
-                total = total + jnp.where(z_cell < B - k, moved, 0.0)
+                shifted = pltpu.roll(q * weight[k], k, 1)
+                total = total + jnp.where(z_cell >= k, shifted, 0.0)
+                shifted = pltpu.roll(q * weight[-k], 128 - k, 1)
+                total = total + jnp.where(z_cell < B - k, shifted, 0.0)
             spill = jnp.take_along_axis(z_spill[c], index, axis=1)
             out_ref[c, 0, :, lane(t)] = total + jnp.where(at_face, spill, 0.0)
+
+
+def swapped(array, d, blocks):
+    return lax.ppermute(array, "blk", [(i, i ^ d) for i in range(blocks)])
 
 
 def shards(slabs, vorticity, velocity, gradient, neighbour):
@@ -268,22 +298,30 @@
             jnp.pad(a, room) for a in (vorticity, velocity, gradient)
         )
     vmem = pl.BlockSpec(memory_space=pltpu.VMEM)
-    smem = pl.BlockSpec(memory_space=pltpu.SMEM)
+    hbm = pl.BlockSpec(memory_space=pltpu.HBM)
 
     def tiles(count):
         return jax.ShapeDtypeStruct((count, 8, 128), jnp.float32)
 
-    after, faces, near, far = pl.pallas_call(
+    velocity, after, faces, near, far = pl.pallas_call(
         functools.partial(first_kernel, slab),
         out_shape=(
+            jax.ShapeDtypeStruct(velocity.shape, jnp.float32),
             jax.ShapeDtypeStruct((3, 8, B * B), jnp.float32),
             tiles(FACES),
             tiles(TILES + 2),
             tiles(TILES + 2),
         ),
-        in_specs=[smem, vmem, vmem, vmem],
-        out_specs=(vmem, vmem, vmem, vmem),
-    )(neighbour, vorticity, velocity, gradient)
+        in_specs=[hbm] * 4,
+        out_specs=(vmem,) * 5,
+        scratch_shapes=[
+            pltpu.SMEM(neighbour.shape, jnp.int32),
+            pltpu.VMEM(vorticity.shape, jnp.float32),
+            pltpu.VMEM(gradient.shape, jnp.float32),
+            pltpu.SemaphoreType.DMA((4,)),
+        ],
+        compiler_params=pltpu.CompilerParams(vmem_limit_bytes=16 << 20),
+    )(*(pltpu.with_memory_space_constraint(a, pltpu.HBM) for a in (neighbour, vorticity, velocity, gradient)))
     far = lax.ppermute(
         far,
         "sub",
@@ -293,15 +331,25 @@
         near, "sub", [p for i in range(0, slabs, 2) for p in ((i, i + 1), (i + 1, i))]
     )
     sent = jnp.concatenate([faces, near[TILES:], far], axis=0)
-    everything = lax.all_gather(sent, "blk")
-    room = everything.size * 4 + (8 << 20)
+    blocks = lax.axis_size("blk")
+    relative = blocks in (2, 4, 8)
+    if relative:
+        held = {0: sent}
+        for d in range(2, blocks, 2):
+            held[d] = swapped(sent, d, blocks)
+        for d in range(0, blocks, 2):
+            held[d + 1] = swapped(held[d], 1, blocks)
+        arrays = [held[d] for d in range(blocks)]
+    else:
+        arrays = [lax.all_gather(sent, "blk")]
+    room = (16 << 20) + (0 if relative else arrays[0].size * 4)
     out = pl.pallas_call(
-        functools.partial(last_kernel, slab, slabs),
+        functools.partial(last_kernel, slab, slabs, relative),
         out_shape=jax.ShapeDtypeStruct((3, 1, 8, B * B), jnp.float32),
-        in_specs=[smem, vmem, vmem, vmem, vmem],
+        in_specs=[vmem] * (3 + len(arrays)),
         out_specs=vmem,
         compiler_params=pltpu.CompilerParams(vmem_limit_bytes=room),
-    )(neighbour, after, velocity, near, everything)
+    )(after, velocity, near, *arrays)
     return out[:, :, :slab]
 
 

time: 24.9 us -> 20.4 us (0.82)
  blocking collectives: 10.4 us -> 0 us
  waiting for transfers between devices: 3.53 us -> 8.52 us
  starting transfers between devices: 5.5 us -> 9.14 us
  Pallas kernels: 3.78 us -> 2.52 us
  other arithmetic: 0.77 us -> 0.01 us
  local copies, waits for them, and re-layouts: 0.66 us -> 0.01 us
    all_gather x1 -> x0, blocking collectives: 10.4 us -> none  [shards(): everything = lax.all_gather(sent, 'blk')]
    ppermute x0 -> x7, waiting for transfers between devices: none -> 5.2 us  [swapped(): return lax.ppermute(array, 'blk', [(i, i ^ d) for i in range(blocks)])]
    ppermute x0 -> x7, starting transfers between devices: none -> 3.58 us  [swapped(): return lax.ppermute(array, 'blk', [(i, i ^ d) for i in range(blocks)])]
    concatenate x1, other arithmetic: 0.77 us -> 0.01 us  [shards(): sent = jnp.concatenate([faces, near[TILES:], far], axis=0)]
    pallas_call x1, Pallas kernels: 1.84 us -> 1.18 us  [shards(): pl.pallas_call(functools.partial(last_kernel, slab, slabs, relative), out...]
    unnamed x6 -> x0, local copies, waits for them, and re-layouts: 0.66 us -> none
    pallas_call x1, Pallas kernels: 1.94 us -> 1.34 us  [shards(): pl.pallas_call(functools.partial(first_kernel, slab), out_shape=(jax.Shap...]
  transfers between devices with their start and end apart: 2 -> 9, of which waited for: 1 -> 6; matrix products, arithmetic and copies ran while one was open for 0% -> 0% of each run, Pallas kernels for 0% -> 0%
where the time goes in v2:
time: 20.4 us; the launch traced here: 20.2 us
  starting transfers between devices  9.14 us (45%)
  waiting for transfers between devices  8.52 us (42%)
  Pallas kernels  2.52 us (12%)
    ppermute x7, waiting for transfers between devices, swapped(): return lax.ppermute(array, 'blk', [(i, i ^ d) for i in range(blocks)])  5.2 us
    ppermute x7, starting transfers between devices, swapped(): return lax.ppermute(array, 'blk', [(i, i ^ d) for i in range(blocks)])  3.58 us
    ppermute x1, waiting for transfers between devices, shards(): lax.ppermute(far, 'sub', [p for i in range(1, slabs, 2) for p in ((i, (i...  3.32 us
    ppermute x1, starting transfers between devices, shards(): lax.ppermute(near, 'sub', [p for i in range(0, slabs, 2) for p in ((i, i...  3.09 us
    ppermute x1, starting transfers between devices, shards(): lax.ppermute(far, 'sub', [p for i in range(1, slabs, 2) for p in ((i, (i...  2.47 us
    pallas_call x1, Pallas kernels, shards(): pl.pallas_call(functools.partial(first_kernel, slab), out_shape=(jax.Shap...  1.34 us
    pallas_call x1, Pallas kernels, shards(): pl.pallas_call(functools.partial(last_kernel, slab, slabs, relative), out...  1.18 us
  transfers between devices with their start and end apart: 9, of which 6 were waited for; matrix products, arithmetic and copies ran while one was open for 0% of the time, Pallas kernels for 0%

profile of v2, /device:TPU:0, one launch (start us, length us, event | category | flops | bytes accessed | tf_op | source)
XLA Modules:
  0.0 20.2 jit_solution(13477961882632582435)
XLA Ops:
  0.0 1.3 %shard_map.46 = (f32[3,1,8,1024]{3,2,1,0:T(8,128)S(1)}, f32[3,8,1024]{2,1,0:T(8,128)S(1)}, f32[9,8,128]{2,1,0:T(8,128)S(1)}, f32[10,8,128]{2,1,0:T(8,128)S(1)}, f32[10,8,128]{2,1,0:T(8,128)S(1)}) custom-call(s32[1,6]{1,0:T(1,128)} %refs_0_.1, f32[3,1,8,1024]{3,2,1,0:T(8,128)} %refs_1_.1, f32[3,1,8,1024]{3,2,1,0:T(8,128)} %refs_2_.1, f32[9,1,8,1024]{3,2,1,0:T(8,128)} %refs_3_.1), custom_call_target="tpu_custom_call" | custom-call | tf_op jit(solution)/shard_map/pallas_call | solution.py:306
  1.3 3.1 %collective-permute-start = (f32[10,8,128]{2,1,0:T(8,128)S(1)}, f32[10,8,128]{2,1,0:T(8,128)S(1)}, u32[]{:S(2)}, u32[]{:S(2)}) collective-permute-start(f32[10,8,128]{2,1,0:T(8,128)S(1)} %get-tuple-element.12), channel_id=1, source_target_pairs={{0,1},{1,0},{2,3},{3,2},{4,5},{5,4},{6,7},{7,6},{8,9},{9,8},{10,11... | collective-permute-start | bytes 122888 | tf_op jit(solution)/shard_map/ppermute | solution.py:330
  4.4 2.5 %collective-permute-start.1 = (f32[10,8,128]{2,1,0:T(8,128)S(1)}, f32[10,8,128]{2,1,0:T(8,128)S(1)}, u32[]{:S(2)}, u32[]{:S(2)}) collective-permute-start(f32[10,8,128]{2,1,0:T(8,128)S(1)} %get-tuple-element.14), channel_id=1, source_target_pairs={{1,2},{2,1},{3,0},{0,3},{5,6},{6,5},{7,4},{4,7},{9,10},{10,9},{11,... | collective-permute-start | bytes 122888 | tf_op jit(solution)/shard_map/ppermute | solution.py:325
  6.9 0.0 collective-permute-done.near_ref
  6.9 3.3 %collective-permute-done.1 = f32[10,8,128]{2,1,0:T(8,128)S(1)} collective-permute-done((f32[10,8,128]{2,1,0:T(8,128)S(1)}, f32[10,8,128]{2,1,0:T(8,128)S(1)}, u32[]{:S(2)}, u32[]{:S(2)}) %collective-permute-start.1) | collective-permute-done | bytes 40992 | tf_op jit(solution)/shard_map/ppermute | solution.py:325
  10.2 2.5 %collective-permute-start.7 = (f32[21,8,128]{2,1,0:T(8,128)S(1)}, f32[21,8,128]{2,1,0:T(8,128)S(1)}, u32[]{:S(2)}, u32[]{:S(2)}) collective-permute-start(f32[21,8,128]{2,1,0:T(8,128)S(1)} %pad_maximum_fusion.refs_0_), channel_id=1, source_target_pairs={{0,24},{4,28},{8,16},{12,20},{16,8},{20,12},{24,0},{28,4},{1,25},{... | collective-permute-start | bytes 258056 | tf_op jit(solution)/shard_map/ppermute | solution.py:290
  12.8 0.5 %collective-permute-start.5 = (f32[21,8,128]{2,1,0:T(8,128)S(1)}, f32[21,8,128]{2,1,0:T(8,128)S(1)}, u32[]{:S(2)}, u32[]{:S(2)}) collective-permute-start(f32[21,8,128]{2,1,0:T(8,128)S(1)} %pad_maximum_fusion.refs_0_), channel_id=1, source_target_pairs={{0,16},{4,20},{8,24},{12,28},{16,0},{20,4},{24,8},{28,12},{1,17},{... | collective-permute-start | bytes 258056 | tf_op jit(solution)/shard_map/ppermute | solution.py:290
  13.3 0.5 %collective-permute-start.3 = (f32[21,8,128]{2,1,0:T(8,128)S(1)}, f32[21,8,128]{2,1,0:T(8,128)S(1)}, u32[]{:S(2)}, u32[]{:S(2)}) collective-permute-start(f32[21,8,128]{2,1,0:T(8,128)S(1)} %pad_maximum_fusion.refs_0_), channel_id=1, source_target_pairs={{0,8},{4,12},{8,0},{12,4},{16,24},{20,28},{24,16},{28,20},{1,9},{5... | collective-permute-start | bytes 258056 | tf_op jit(solution)/shard_map/ppermute | solution.py:290
  13.8 0.0 collective-permute-start.2
  13.8 2.6 %collective-permute-done.7.refs_6_ = f32[21,8,128]{2,1,0:T(8,128)S(1)} collective-permute-done((f32[21,8,128]{2,1,0:T(8,128)S(1)}, f32[21,8,128]{2,1,0:T(8,128)S(1)}, u32[]{:S(2)}, u32[]{:S(2)}) %collective-permute-start.7) | collective-permute-done | bytes 86048 | tf_op jit(solution)/shard_map/ppermute | solution.py:290
  16.3 0.0 collective-permute-start.8
  16.4 0.9 %collective-permute-done.5.refs_4_ = f32[21,8,128]{2,1,0:T(8,128)S(1)} collective-permute-done((f32[21,8,128]{2,1,0:T(8,128)S(1)}, f32[21,8,128]{2,1,0:T(8,128)S(1)}, u32[]{:S(2)}, u32[]{:S(2)}) %collective-permute-start.5) | collective-permute-done | bytes 86048 | tf_op jit(solution)/shard_map/ppermute | solution.py:290
  17.3 0.0 collective-permute-start.6
  17.3 0.5 %collective-permute-done.3.refs_2_ = f32[21,8,128]{2,1,0:T(8,128)S(1)} collective-permute-done((f32[21,8,128]{2,1,0:T(8,128)S(1)}, f32[21,8,128]{2,1,0:T(8,128)S(1)}, u32[]{:S(2)}, u32[]{:S(2)}) %collective-permute-start.3) | collective-permute-done | bytes 86048 | tf_op jit(solution)/shard_map/ppermute | solution.py:290
  17.7 0.0 collective-permute-start.4
  17.8 0.0 collective-permute-done.2.refs_1_
  17.8 0.0 collective-permute-done.8.refs_7_
  17.8 0.8 %collective-permute-done.6.refs_5_ = f32[21,8,128]{2,1,0:T(8,128)S(1)} collective-permute-done((f32[21,8,128]{2,1,0:T(8,128)S(1)}, f32[21,8,128]{2,1,0:T(8,128)S(1)}, u32[]{:S(2)}, u32[]{:S(2)}) %collective-permute-start.6) | collective-permute-done | bytes 86048 | tf_op jit(solution)/shard_map/ppermute | solution.py:290
  18.5 0.5 %collective-permute-done.4.refs_3_ = f32[21,8,128]{2,1,0:T(8,128)S(1)} collective-permute-done((f32[21,8,128]{2,1,0:T(8,128)S(1)}, f32[21,8,128]{2,1,0:T(8,128)S(1)}, u32[]{:S(2)}, u32[]{:S(2)}) %collective-permute-start.4) | collective-permute-done | bytes 86048 | tf_op jit(solution)/shard_map/ppermute | solution.py:290
  19.0 1.2 %shard_map.47 = f32[3,1,8,1024]{3,2,1,0:T(8,128)} custom-call(f32[3,8,1024]{2,1,0:T(8,128)S(1)} %get-tuple-element.10.after_ref, f32[3,1,8,1024]{3,2,1,0:T(8,128)S(1)} %get-tuple-element.11.u_ref, f32[10,8,128]{2,1,0:T(8,128)S(1)} %collective-permute-done.near_ref, f32[21,8,128]{2,1,0:T(8,128)S(1)} %pad_maximum_fusion.refs_0_, ...), custom_call_target="tpu_custom_call" | custom-call | tf_op jit(solution)/shard_map/pallas_call | solution.py:346
  (2 shorter events, 0.0 us)
Async XLA Ops:
  1.3 5.6 %collective-permute-start = (f32[10,8,128]{2,1,0:T(8,128)S(1)}, f32[10,8,128]{2,1,0:T(8,128)S(1)}, u32[]{:S(2)}, u32[]{:S(2)}) collective-permute-start(f32[10,8,128]{2,1,0:T(8,128)S(1)} %get-tuple-element.12), channel_id=1, source_target_pairs={{0,1},{1,0},{2,3},{3,2},{4,5},{5,4},{6,7},{7,6},{8,9},{9,8},{10,11... | collective-permute-start | bytes 122888 | tf_op jit(solution)/shard_map/ppermute | solution.py:330
  4.4 5.8 %collective-permute-start.1 = (f32[10,8,128]{2,1,0:T(8,128)S(1)}, f32[10,8,128]{2,1,0:T(8,128)S(1)}, u32[]{:S(2)}, u32[]{:S(2)}) collective-permute-start(f32[10,8,128]{2,1,0:T(8,128)S(1)} %get-tuple-element.14), channel_id=1, source_target_pairs={{1,2},{2,1},{3,0},{0,3},{5,6},{6,5},{7,4},{4,7},{9,10},{10,9},{11,... | collective-permute-start | bytes 122888 | tf_op jit(solution)/shard_map/ppermute | solution.py:325
  10.2 6.1 %collective-permute-start.7 = (f32[21,8,128]{2,1,0:T(8,128)S(1)}, f32[21,8,128]{2,1,0:T(8,128)S(1)}, u32[]{:S(2)}, u32[]{:S(2)}) collective-permute-start(f32[21,8,128]{2,1,0:T(8,128)S(1)} %pad_maximum_fusion.refs_0_), channel_id=1, source_target_pairs={{0,24},{4,28},{8,16},{12,20},{16,8},{20,12},{24,0},{28,4},{1,25},{... | collective-permute-start | bytes 258056 | tf_op jit(solution)/shard_map/ppermute | solution.py:290
  12.8 4.5 %collective-permute-start.5 = (f32[21,8,128]{2,1,0:T(8,128)S(1)}, f32[21,8,128]{2,1,0:T(8,128)S(1)}, u32[]{:S(2)}, u32[]{:S(2)}) collective-permute-start(f32[21,8,128]{2,1,0:T(8,128)S(1)} %pad_maximum_fusion.refs_0_), channel_id=1, source_target_pairs={{0,16},{4,20},{8,24},{12,28},{16,0},{20,4},{24,8},{28,12},{1,17},{... | collective-permute-start | bytes 258056 | tf_op jit(solution)/shard_map/ppermute | solution.py:290
  13.3 4.5 %collective-permute-start.3 = (f32[21,8,128]{2,1,0:T(8,128)S(1)}, f32[21,8,128]{2,1,0:T(8,128)S(1)}, u32[]{:S(2)}, u32[]{:S(2)}) collective-permute-start(f32[21,8,128]{2,1,0:T(8,128)S(1)} %pad_maximum_fusion.refs_0_), channel_id=1, source_target_pairs={{0,8},{4,12},{8,0},{12,4},{16,24},{20,28},{24,16},{28,20},{1,9},{5... | collective-permute-start | bytes 258056 | tf_op jit(solution)/shard_map/ppermute | solution.py:290
  13.8 4.0 %collective-permute-start.2 = (f32[21,8,128]{2,1,0:T(8,128)S(1)}, f32[21,8,128]{2,1,0:T(8,128)S(1)}, u32[]{:S(2)}, u32[]{:S(2)}) collective-permute-start(f32[21,8,128]{2,1,0:T(8,128)S(1)} %pad_maximum_fusion.refs_0_), channel_id=1, source_target_pairs={{0,4},{4,0},{8,12},{12,8},{16,20},{20,16},{24,28},{28,24},{1,5},{5... | collective-permute-start | bytes 258056 | tf_op jit(solution)/shard_map/ppermute | solution.py:290
  16.3 1.4 %collective-permute-start.8 = (f32[21,8,128]{2,1,0:T(8,128)S(1)}, f32[21,8,128]{2,1,0:T(8,128)S(1)}, u32[]{:S(2)}, u32[]{:S(2)}) collective-permute-start(f32[21,8,128]{2,1,0:T(8,128)S(1)} %collective-permute-done.7.refs_6_), channel_id=1, source_target_pairs={{0,4},{4,0},{8,12},{12,8},{16,20},{20,16},{24,28},{28,24},{1,5},{5... | collective-permute-start | bytes 258056 | tf_op jit(solution)/shard_map/ppermute | solution.py:290
  17.3 1.3 %collective-permute-start.6 = (f32[21,8,128]{2,1,0:T(8,128)S(1)}, f32[21,8,128]{2,1,0:T(8,128)S(1)}, u32[]{:S(2)}, u32[]{:S(2)}) collective-permute-start(f32[21,8,128]{2,1,0:T(8,128)S(1)} %collective-permute-done.5.refs_4_), channel_id=1, source_target_pairs={{0,4},{4,0},{8,12},{12,8},{16,20},{20,16},{24,28},{28,24},{1,5},{5... | collective-permute-start | bytes 258056 | tf_op jit(solution)/shard_map/ppermute | solution.py:290
  17.7 1.3 %collective-permute-start.4 = (f32[21,8,128]{2,1,0:T(8,128)S(1)}, f32[21,8,128]{2,1,0:T(8,128)S(1)}, u32[]{:S(2)}, u32[]{:S(2)}) collective-permute-start(f32[21,8,128]{2,1,0:T(8,128)S(1)} %collective-permute-done.3.refs_2_), channel_id=1, source_target_pairs={{0,4},{4,0},{8,12},{12,8},{16,20},{20,16},{24,28},{28,24},{1,5},{5... | collective-permute-start | bytes 258056 | tf_op jit(solution)/shard_map/ppermute | solution.py:290

commit v3 on v2

v3 whole, which is shorter than its diff:
```python
import functools

import jax
import jax.numpy as jnp
from jax import lax
from jax.experimental import pallas as pl
from jax.experimental.pallas import tpu as pltpu
from jax.sharding import PartitionSpec as P

B = 32
TILES = B * B // 128
stretch_step = 0.25

AFTER_Y, AFTER_Z, U1_Y, U1_Z, U2_Z = 0, 3, 6, 7, 8
FACES = 9
SPILLS = 6
KEPT = (0, 1, 2, 5, 6, 7)
PACKED = len(KEPT)
ROW_U1_Y, ROW_U1_Z, ROW_U2_Z, ROW_CORNER, ROW_BESIDE = 0, 2, 4, 6, 7
SENT = 2 * PACKED + 1


def iotas():
    return (
        lax.broadcasted_iota(jnp.int32, (8, 128), 0),
        lax.broadcasted_iota(jnp.int32, (8, 128), 1),
    )


def weights(u):
    a = jnp.abs(u)
    rest = 1.0 - a
    centre = 1.0 + a * a * (1.5 * a - 2.5)
    toward = a * (0.5 + a * (2.0 - 1.5 * a))
    away = -0.5 * a * rest * rest
    far = -0.5 * a * a * rest
    up = u >= 0.0
    return {
        0: centre,
        1: jnp.where(up, toward, away),
        -1: jnp.where(up, away, toward),
        2: jnp.where(up, far, 0.0),
        -2: jnp.where(up, 0.0, far),
    }


def lane(tile):
    return pl.ds(128 * tile, 128)


def gathered(tile, index):
    return jnp.take_along_axis(tile, index, axis=1)


def row_of(tile, row):
    return jnp.broadcast_to(tile[row : row + 1], (8, 128))


def pair_rows(tile, row):
    rows, _ = iotas()
    return jnp.where(rows & 1 == 0, row_of(tile, row), row_of(tile, row + 1))


def y_face(tiles):
    _, lanes = iotas()
    return jnp.where(lanes < 64, tiles[0], tiles[TILES - 1])


def z_of(n):
    return jnp.where(n < 2, n, B - 4 + n)


def z_face(tiles):
    _, lanes = iotas()
    index = 32 * ((lanes >> 2) & 3) + z_of(lanes & 3)
    face = None
    for t, tile in enumerate(tiles):
        if tile is not None:
            picked = gathered(tile, index)
            face = picked if face is None else jnp.where((lanes >> 4) == t, picked, face)
    return face


def y_edges(tile):
    _, lanes = iotas()
    y = lanes >> 2
    n = jnp.where(y < 2, y, jnp.where(y >= B - 2, y - (B - 4), 0))
    return gathered(tile, 32 * n + z_of(lanes & 3))


def pack(tiles):
    rows, _ = iotas()
    packed = []
    for j, t in enumerate(KEPT):
        last = jnp.where(rows == 6, pltpu.roll(tiles[3], 6 - j, 0), pltpu.roll(tiles[4], 7 - j, 0))
        packed.append(jnp.where(rows < 6, tiles[t], last))
    return packed


def unpack(packed):
    rows, _ = iotas()
    tiles = dict(zip(KEPT, packed))
    for t, row in ((3, 6), (4, 7)):
        tiles[t] = packed[0]
        for j, tile in enumerate(packed):
            tiles[t] = jnp.where(rows == j, pltpu.roll(tile, (j - row) % 8, 0), tiles[t])
    return [tiles[t] for t in range(TILES)]


def placed(tile, c, row):
    rows, _ = iotas()
    moved = pltpu.roll(tile, (row - 2 * c + 8) % 8, 0)
    return jnp.where((rows >= row) & (rows < row + 2), moved, 0.0)


def y_spill(fields, u):
    _, lanes = iotas()
    weight = weights(u)
    low = lanes < 64
    one = jnp.where(low, weight[-1], weight[1])
    two = jnp.where(low, weight[-2], weight[2])
    spilt = []
    for q in fields:
        q1, q2 = q * one, q * two
        edge = jnp.where(lanes < 32, pltpu.roll(q1, 32, 1), pltpu.roll(q1, 96, 1))
        edge = jnp.where((lanes < 32) | (lanes >= 96), edge, 0.0)
        spilt.append(pltpu.roll(q2, 64, 1) + edge)
    return spilt


def z_spill(fields, u):
    _, lanes = iotas()
    n = lanes & 3
    weight = weights(u)
    one = jnp.where(n < 2, weight[-1], weight[1])
    two = jnp.where(n < 2, weight[-2], weight[2])
    spilt = []
    for q in fields:
        q1, q2 = q * one, q * two
        edge = jnp.where(n == 0, pltpu.roll(q1, 125, 1), pltpu.roll(q1, 3, 1))
        edge = jnp.where((n == 0) | (n == 3), edge, 0.0)
        spilt.append(jnp.where(n < 2, pltpu.roll(q2, 126, 1), pltpu.roll(q2, 2, 1)) + edge)
    return spilt


def y_pass_of_z_face(q, weight, beside=None, beside_weight=None):
    _, lanes = iotas()
    y = lanes >> 2
    total = q * weight[0]
    for k in (-2, -1, 1, 2):
        outside = y >= B - k if k > 0 else y < -k
        other = 0.0 if beside is None else beside * beside_weight[k]
        total = total + pltpu.roll(jnp.where(outside, other, q * weight[k]), (4 * k) % 128, 1)
    return total


def stretched(w_ref, g_ref, t):
    w = [w_ref[c, 0, :, lane(t)] for c in range(3)]
    return [
        w[c]
        + stretch_step
        * (
            g_ref[3 * c, 0, :, lane(t)] * w[0]
            + g_ref[3 * c + 1, 0, :, lane(t)] * w[1]
            + g_ref[3 * c + 2, 0, :, lane(t)] * w[2]
        )
        for c in range(3)
    ]


def spill_kernel(slab, paired, *refs):
    here, (w_ref, u_ref, g_ref, give_ref, keep_ref, meta_ref) = refs[:4], refs[4:10]
    nb_ref, sems = refs[10:]
    copies = [
        pltpu.make_async_copy(source, target, sems.at[n])
        for n, (source, target) in enumerate(zip(here, (nb_ref, w_ref, u_ref, g_ref)))
    ]
    for copy in copies:
        copy.start()
    for copy in copies:
        copy.wait()
    rows, lanes = iotas()
    odd = lax.axis_index("sub") % 2 == 1
    near, far = [], []
    for t in range(TILES):
        q = stretched(w_ref, g_ref, t)
        u = u_ref[0, 0, :, lane(t)]
        top, bottom = q[2], q[2]
        for c in (2, 1, 0):
            mine = rows < 2 * c + 2
            shift = (2 * c + 2 - slab) % 8
            top = jnp.where(mine, pltpu.roll(q[c], shift, 0) if shift else q[c], top)
            bottom = jnp.where(mine, pltpu.roll(q[c], 2 * c, 0) if c else q[c], bottom)
        weight = weights(pair_rows(u, slab - 2))
        edge = jnp.where(rows & 1 == 0, pltpu.roll(top * weight[1], 7, 0), 0.0)
        up = top * weight[2] + edge
        weight = weights(pair_rows(u, 0))
        edge = jnp.where(rows & 1 == 1, pltpu.roll(bottom * weight[-1], 1, 0), 0.0)
        down = bottom * weight[-2] + edge
        near.append(jnp.where(odd, down, up))
        far.append(jnp.where(odd, up, down))
    second = lax.axis_index("blk") % 2 == 1
    for j, (n, f) in enumerate(zip(pack(near), pack(far))):
        give_ref[j] = jnp.where(second, n, f) if paired else f
        keep_ref[j] = jnp.where(second, f, n) if paired else n
    meta = jnp.zeros((8, 128), jnp.float32)
    for j in range(6):
        meta = jnp.where(lanes == j, nb_ref[0, j].astype(jnp.float32), meta)
    meta_ref[...] = meta


def inside_kernel(slab, w_ref, u_ref, g_ref, after_ref, face_ref):
    rows, lanes = iotas()
    after = [[], [], []]
    for t in range(TILES):
        weight = weights(u_ref[0, 0, :, lane(t)])
        for c, q in enumerate(stretched(w_ref, g_ref, t)):
            inside = q * weight[0]
            for k in (1, 2):
                spilt = rows < k if slab == 8 else rows >= slab
                inside = inside + jnp.where(spilt, 0.0, pltpu.roll(q * weight[k], k, 0))
                spilt = rows >= 8 - k
                inside = inside + jnp.where(spilt, 0.0, pltpu.roll(q * weight[-k], 8 - k, 0))
            after[c].append(inside)
            after_ref[c, :, lane(t)] = inside
    u1 = [u_ref[1, 0, :, lane(t)] for t in range(TILES)]
    u2 = [u_ref[2, 0, :, lane(t)] for t in range(TILES)]
    faces = [y_face(after[c]) for c in range(3)] + [z_face(after[c]) for c in range(3)]
    faces += [y_face(u1), z_face(u1), z_face(u2)]
    for n, face in enumerate(faces):
        face_ref[n] = face


def pair_kernel(keep_ref, got_ref, face_ref, both_ref):
    second = lax.axis_index("blk") % 2 == 1
    for j in range(PACKED):
        both_ref[j] = jnp.where(second, got_ref[j], keep_ref[j])
        both_ref[PACKED + j] = jnp.where(second, keep_ref[j], got_ref[j])


def spills_of(slab, face_ref, packed):
    near_row = jnp.where(lax.axis_index("sub") % 2 == 1, 0, slab - 2)
    near = unpack(packed)
    near_y, near_z = y_face(near), z_face(near)
    in_y = [face_ref[AFTER_Y + c] + placed(near_y, c, near_row) for c in range(3)]
    in_z = [face_ref[AFTER_Z + c] + placed(near_z, c, near_row) for c in range(3)]
    weight = weights(face_ref[U1_Z])
    in_z = [y_pass_of_z_face(q, weight) for q in in_z]
    return y_spill(in_y, face_ref[U1_Y]) + z_spill(in_z, face_ref[U2_Z])


def extra_of(slab, face_ref, meta):
    rows, lanes = iotas()
    far_row = jnp.where(lax.axis_index("sub") % 2 == 1, slab - 2, 0)
    extra = meta
    corner = gathered(face_ref[U2_Z], 4 * z_of((lanes >> 2) & 3) + (lanes & 3))
    corner = jnp.sum(jnp.where(rows == lanes >> 4, corner, 0.0), axis=0, keepdims=True)
    extra = jnp.where(rows < ROW_BESIDE, jnp.broadcast_to(corner, (8, 128)), extra)
    for tile, row in ((U2_Z, ROW_U2_Z), (U1_Z, ROW_U1_Z), (U1_Y, ROW_U1_Y)):
        moved = pltpu.roll(face_ref[tile], (row - far_row + 8) % 8, 0)
        extra = jnp.where(rows < row + 2, moved, extra)
    return extra


def middle_kernel(slab, own_ref, got_ref, spill_ref, meta_ref, sent_ref, own_sent_ref):
    second = lax.axis_index("blk") % 2 == 1
    for p, ref in enumerate((own_ref, got_ref)):
        packed = [spill_ref[PACKED * p + j] for j in range(PACKED)]
        for n, tile in enumerate(spills_of(slab, ref, packed)):
            tile = jnp.where(second, packed[n], tile)
            sent_ref[SPILLS * p + n] = tile
            own_sent_ref[SPILLS * p + n] = tile
            if p == 1:
                own_sent_ref[SENT + n] = packed[n]
    extra = extra_of(slab, own_ref, meta_ref[...])
    sent_ref[2 * PACKED] = extra
    own_sent_ref[2 * PACKED] = extra


def middle_kernel_alone(slab, face_ref, near_ref, far_ref, meta_ref, sent_ref):
    packed = [near_ref[j] for j in range(PACKED)]
    for n, tile in enumerate(spills_of(slab, face_ref, packed)):
        sent_ref[n] = tile
        sent_ref[SPILLS + n] = far_ref[n]
    sent_ref[2 * PACKED] = extra_of(slab, face_ref, meta_ref[...])


def last_kernel(slab, slabs, paired, after_ref, u_ref, spill_ref, *refs):
    block_refs, out_ref = refs[:-1], refs[-1]
    rows, lanes = iotas()
    here = lax.axis_index("blk")
    place_in = lax.axis_index("sub")
    odd = place_in % 2 == 1
    near_row = jnp.where(odd, 0, slab - 2)
    far_row = jnp.where(odd, slab - 2, 0)
    below_x = place_in == 0
    above_x = place_in == slabs - 1
    at_end = below_x | above_x
    x_face = jnp.where(above_x, 1, 0)
    second = here % 2 == 1
    base = here - here % 2 if paired else 0

    def over_blocks(step, carry):
        if not paired:
            (ref,) = block_refs
            return lax.fori_loop(
                0,
                ref.shape[0],
                lambda slot, c: step(
                    slot,
                    lambda n: ref[slot, n],
                    lambda j: ref[slot, SPILLS + j],
                    lambda: ref[slot, 2 * PACKED],
                    c,
                ),
                carry,
            )
        chips = len(block_refs) // 2
        for slot in range(2 * chips):
            held, other = block_refs[slot // 2], block_refs[chips + slot // 2]
            p = slot % 2

            def on_core(core, n, held=held, other=other):
                mine, theirs = held[n], other[n]
                return jnp.where(second, theirs, mine) if core == 0 else jnp.where(second, mine, theirs)

            carry = step(
                slot,
                lambda n, p=p, get=on_core: get(0, SPILLS * p + n),
                lambda j, p=p, get=on_core: get(1, PACKED * p + j),
                lambda p=p, get=on_core: get(p, 2 * PACKED),
                carry,
            )
        return carry

    packed = [spill_ref[j] for j in range(PACKED)]
    if paired:
        other = block_refs[len(block_refs) // 2]
        packed = [jnp.where(second, other[SENT + j], packed[j]) for j in range(PACKED)]
    near = unpack(packed)

    def beside(extra, face):
        index = jnp.full((8, 128), face, jnp.int32)
        return gathered(row_of(extra, ROW_BESIDE), index).astype(jnp.int32) ^ base

    own_extra = block_refs[0][2 * PACKED] if paired else block_refs[0][here, 2 * PACKED]
    ym, yp, zm, zp = (beside(own_extra, face) for face in (2, 3, 4, 5))
    outer = jnp.where(at_end, beside(own_extra, x_face), here ^ base)

    def find_corners(slot, spills, far, extra, found):
        tile = extra()
        below, above = (beside(tile, face) for face in (2, 3))
        at_m, at_p = zm == slot, zp == slot
        mm, mp, pm, pp = found
        return (
            jnp.where(at_m, below, mm),
            jnp.where(at_m, above, mp),
            jnp.where(at_p, below, pm),
            jnp.where(at_p, above, pp),
        )

    zmm, zmp, zpm, zpp = over_blocks(find_corners, (zm, zm, zp, zp))
    near_slots = (ym, yp, zm, zp, zmm, zmp, zpm, zpp)

    def find_far(slot, spills, far, extra, found):
        there = beside(extra(), x_face)
        return tuple(
            jnp.where(at_end & (start == slot), there, f) for start, f in zip(near_slots, found)
        )

    far_ym, far_yp, far_zm, far_zp, far_zmm, far_zmp, far_zpm, far_zpp = over_blocks(
        find_far, near_slots
    )

    y_low = lanes < 64
    n_low = lanes & 3 < 2
    z_cell = lanes & 31
    z_low = z_cell < 16
    corner_low, corner_high = jnp.where(z_low, zpm, zmm), jnp.where(z_low, zpp, zmp)
    wanted_spills = (
        [(jnp.where(y_low, ym, yp), n) for n in (0, 1, 2)]
        + [(jnp.where(n_low, zm, zp), n) for n in (3, 4, 5)]
        + [(jnp.where(y_low, corner_low, corner_high), n) for n in (0, 1, 2)]
    )
    wanted_extra = [
        jnp.where(y_low, yp, ym),
        jnp.where(n_low, zp, zm),
        jnp.where(y_low, corner_high, corner_low),
    ]
    far_z = jnp.where(z_low, far_zp, far_zm)
    wanted_far = (
        [(far_yp, 0), (far_ym, PACKED - 1)]
        + [(jnp.where(z_low, far_zpp, far_zmp), 0)]
        + [(jnp.where(z_low, far_zpm, far_zmm), PACKED - 1)]
        + [(far_z, j) for j in range(PACKED)]
        + [(outer, j) for j in range(PACKED)]
    )

    def pick(slot, spills, far, extra, picked):
        tile = extra()
        found = [(which, spills(n)) for which, n in wanted_spills]
        found += [(which, tile) for which in wanted_extra]
        found += [(which, far(j)) for which, j in wanted_far]
        return tuple(jnp.where(which == slot, t, p) for (which, t), p in zip(found, picked))

    count = len(wanted_spills) + len(wanted_extra) + len(wanted_far)
    picked = list(over_blocks(pick, (jnp.zeros((8, 128), jnp.float32),) * count))
    into_y, into_z, into_corner = picked[0:3], picked[3:6], picked[6:9]
    extra_y, extra_z, extra_c = picked[9:12]
    far_y = jnp.where(y_low, picked[12], picked[13])
    far_c = z_face([picked[14]] + [None] * (TILES - 2) + [picked[15]])
    far_z = z_face(unpack(picked[16 : 16 + PACKED]))
    far_own = unpack(picked[16 + PACKED :])

    (by_far,) = y_spill([far_y], pair_rows(extra_y, ROW_U1_Y))
    into_y = [into_y[c] + placed(by_far, c, far_row) for c in range(3)]

    (by_far,) = z_spill(
        [
            y_pass_of_z_face(
                far_z,
                weights(pair_rows(extra_z, ROW_U1_Z)),
                far_c,
                weights(y_edges(pair_rows(extra_c, ROW_U1_Y))),
            )
        ],
        pair_rows(extra_z, ROW_U2_Z),
    )
    y = lanes >> 2
    at_edge = (y < 2) | (y >= B - 2)
    n = jnp.where(y < 2, y, jnp.where(y >= B - 2, y - (B - 4), 0))
    u2 = gathered(row_of(extra_z, ROW_CORNER), 16 * rows + 4 * n + (lanes & 3))
    by_corner = z_spill([jnp.where(at_edge, y_edges(q), 0.0) for q in into_corner], u2)
    into_z = [into_z[c] + by_corner[c] + placed(by_far, c, far_row) for c in range(3)]

    after_y = [[None] * TILES for c in range(3)]
    moved = {}
    for t in range(TILES):
        weight = weights(u_ref[1, 0, :, lane(t)])
        for c in range(3):
            q = after_ref[c, :, lane(t)] + placed(near[t], c, near_row) + placed(far_own[t], c, far_row)
            after_y[c][t] = q * weight[0]
            for k in (-2, -1, 1, 2):
                moved[c, t, k] = pltpu.roll(q * weight[k], (32 * k) % 128, 1)
    for t in range(TILES):
        for c in range(3):
            total = after_y[c][t]
            for k in (1, 2):
                cut = lanes < 32 * k
                other = moved[c, t - 1, k] if t > 0 else 0.0
                total = total + jnp.where(cut, other, moved[c, t, k])
                cut = lanes >= 128 - 32 * k
                other = moved[c, t + 1, -k] if t < TILES - 1 else 0.0
                total = total + jnp.where(cut, other, moved[c, t, -k])
            if t == 0:
                total = total + jnp.where(y_low, into_y[c], 0.0)
            if t == TILES - 1:
                total = total + jnp.where(y_low, 0.0, into_y[c])
            after_y[c][t] = total

    at_face = (z_cell < 2) | (z_cell >= B - 2)
    place = jnp.where(z_cell < 2, z_cell, jnp.where(z_cell >= B - 2, z_cell - (B - 4), 0))
    for t in range(TILES):
        weight = weights(u_ref[2, 0, :, lane(t)])
        index = 16 * t + 4 * (lanes >> 5) + place
        for c in range(3):
            q = after_y[c][t]
            total = q * weight[0]
            for k in (1, 2):
                shifted = pltpu.roll(q * weight[k], k, 1)
                total = total + jnp.where(z_cell >= k, shifted, 0.0)
                shifted = pltpu.roll(q * weight[-k], 128 - k, 1)
                total = total + jnp.where(z_cell < B - k, shifted, 0.0)
            out_ref[c, 0, :, lane(t)] = total + jnp.where(at_face, gathered(into_z[c], index), 0.0)


def swapped(array, d, blocks):
    return lax.ppermute(array, "blk", [(i, i ^ d) for i in range(blocks)])


def near_slab(s, slabs):
    return s ^ 1


def far_slab(s, slabs):
    return (s + 1 if s % 2 else s - 1) % slabs


def shards(slabs, vorticity, velocity, gradient, neighbour):
    slab = vorticity.shape[2]
    if slab < 8:
        room = ((0, 0), (0, 0), (0, 8 - slab), (0, 0))
        vorticity, velocity, gradient = (
            jnp.pad(a, room) for a in (vorticity, velocity, gradient)
        )
    blocks = lax.axis_size("blk")
    paired = blocks in (2, 4, 8)
    vmem = pl.BlockSpec(memory_space=pltpu.VMEM)
    hbm = pl.BlockSpec(memory_space=pltpu.HBM)
    small = pltpu.CompilerParams(vmem_limit_bytes=16 << 20)

    def shape(*dims):
        return jax.ShapeDtypeStruct(dims, jnp.float32)

    def tiles(count):
        return shape(count, 8, 128)

    def call(kernel, out_shape, *args, params=small):
        return pl.pallas_call(
            kernel,
            out_shape=out_shape,
            in_specs=[vmem] * len(args),
            out_specs=(vmem,) * len(out_shape) if isinstance(out_shape, tuple) else vmem,
            compiler_params=params,
        )(*args)

    inputs = (neighbour, vorticity, velocity, gradient)
    vorticity, velocity, gradient, give, keep, meta = pl.pallas_call(
        functools.partial(spill_kernel, slab, paired),
        out_shape=(
            shape(*vorticity.shape),
            shape(*velocity.shape),
            shape(*gradient.shape),
            tiles(PACKED),
            tiles(PACKED),
            shape(8, 128),
        ),
        in_specs=[hbm] * 4,
        out_specs=(vmem,) * 6,
        scratch_shapes=[
            pltpu.SMEM(neighbour.shape, jnp.int32),
            pltpu.SemaphoreType.DMA((4,)),
        ],
        compiler_params=small,
    )(*(pltpu.with_memory_space_constraint(a, pltpu.HBM) for a in inputs))
    after, faces = call(
        functools.partial(inside_kernel, slab),
        (shape(3, 8, B * B), tiles(FACES)),
        vorticity,
        velocity,
        gradient,
    )
    if paired:
        got = swapped(give, 1, blocks)
        both = call(pair_kernel, tiles(2 * PACKED), keep, got, faces)
        spill = lax.ppermute(
            both,
            ("blk", "sub"),
            [
                (b * slabs + s, b * slabs + (far_slab if b % 2 else near_slab)(s, slabs))
                for b in range(blocks)
                for s in range(slabs)
            ],
        )
        got_faces = swapped(faces, 1, blocks)
        sent, own_sent = call(
            functools.partial(middle_kernel, slab),
            (tiles(SENT), tiles(SENT + PACKED)),
            faces,
            got_faces,
            spill,
            meta,
        )
        held = [sent] + [swapped(sent, d, blocks) for d in range(2, blocks, 2)]
        arrays = held + [swapped(array, 1, blocks) for array in [own_sent] + held[1:]]
    else:
        spill = lax.ppermute(keep, "sub", [(s, near_slab(s, slabs)) for s in range(slabs)])
        far = lax.ppermute(give, "sub", [(s, far_slab(s, slabs)) for s in range(slabs)])
        sent = call(
            functools.partial(middle_kernel_alone, slab), tiles(SENT), faces, spill, far, meta
        )
        arrays = [lax.all_gather(sent, "blk")]
    room = (16 << 20) + (0 if paired else arrays[0].size * 4)
    out = call(
        functools.partial(last_kernel, slab, slabs, paired),
        shape(3, 1, 8, B * B),
        after,
        velocity,
        spill,
        *arrays,
        params=pltpu.CompilerParams(vmem_limit_bytes=room),
    )
    return out[:, :, :slab]


def solution(mesh):
    return jax.shard_map(
        functools.partial(shards, mesh.shape["sub"]),
        mesh=mesh,
        in_specs=(
            P(None, "blk", "sub", None),
            P(None, "blk", "sub", None),
            P(None, "blk", "sub", None),
            P("blk", None),
        ),
        out_specs=P(None, "blk", "sub", None),
        check_vma=False,
    )
```

time: 20.4 us -> 18.3 us (0.90)
  waiting for transfers between devices: 8.52 us -> 6.34 us
  Pallas kernels: 2.52 us -> 2.85 us
  starting transfers between devices: 9.14 us -> 8.93 us
    ppermute x2 -> x1, waiting for transfers between devices: 3.32 us -> 0.01 us  [shards(): lax.ppermute(both, ('blk', 'sub'), [(b * slabs + s, b * slabs + (far_slab...]
    ppermute x2 -> x1, starting transfers between devices: 5.56 us -> 2.98 us  [shards(): lax.ppermute(both, ('blk', 'sub'), [(b * slabs + s, b * slabs + (far_slab...]
    ppermute x7 -> x9, starting transfers between devices: 3.58 us -> 5.95 us  [swapped(): return lax.ppermute(array, 'blk', [(i, i ^ d) for i in range(blocks)])]
    ppermute x7 -> x9, waiting for transfers between devices: 5.2 us -> 6.34 us  [swapped(): return lax.ppermute(array, 'blk', [(i, i ^ d) for i in range(blocks)])]
    pallas_call x2 -> x5, Pallas kernels: 2.52 us -> 2.85 us  [the longest x4 1.65 us: call(): pl.pallas_call(kernel, out_shape=out_shape, in_specs=[vmem] * len(args),...]
  transfers between devices with their start and end apart: 9 -> 10, of which waited for: 6 -> 7; matrix products, arithmetic and copies ran while one was open for 0% -> 0% of each run, Pallas kernels for 0% -> 1%
where the time goes in v3:
time: 18.3 us; the launch traced here: 18.2 us
  starting transfers between devices  8.93 us (49%)
  waiting for transfers between devices  6.34 us (35%)
  Pallas kernels  2.85 us (16%)
    ppermute x9, waiting for transfers between devices, swapped(): return lax.ppermute(array, 'blk', [(i, i ^ d) for i in range(blocks)])  6.34 us
    ppermute x9, starting transfers between devices, swapped(): return lax.ppermute(array, 'blk', [(i, i ^ d) for i in range(blocks)])  5.95 us
    ppermute x1, starting transfers between devices, shards(): lax.ppermute(both, ('blk', 'sub'), [(b * slabs + s, b * slabs + (far_slab...  2.98 us
    pallas_call x4, Pallas kernels, call(): pl.pallas_call(kernel, out_shape=out_shape, in_specs=[vmem] * len(args),...  1.65 us
    pallas_call x1, Pallas kernels, shards(): pl.pallas_call(functools.partial(spill_kernel, slab, paired), out_shape=(...  1.19 us
  transfers between devices with their start and end apart: 10, of which 7 were waited for; matrix products, arithmetic and copies ran while one was open for 0% of the time, Pallas kernels for 1%

profile of v3, /device:TPU:0, one launch (start us, length us, event | category | flops | bytes accessed | tf_op | source)
XLA Modules:
  0.0 18.2 jit_solution(658622018105161373)
XLA Ops:
  0.0 1.2 %shard_map.46 = (f32[3,1,8,1024]{3,2,1,0:T(8,128)S(1)}, f32[3,1,8,1024]{3,2,1,0:T(8,128)S(1)}, f32[9,1,8,1024]{3,2,1,0:T(8,128)S(1)}, f32[6,8,128]{2,1,0:T(8,128...) custom-call(s32[1,6]{1,0:T(1,128)} %refs_0_.1, f32[3,1,8,1024]{3,2,1,0:T(8,128)} %refs_1_.1, ...), custom_call_target="tpu_custom_call" | custom-call | tf_op jit(solution)/shard_map/pallas_call | solution.py:518
  1.2 0.5 %collective-permute-start = (f32[6,8,128]{2,1,0:T(8,128)S(1)}, f32[6,8,128]{2,1,0:T(8,128)S(1)}, u32[]{:S(2)}, u32[]{:S(2)}) collective-permute-start(f32[6,8,128]{2,1,0:T(8,128)S(1)} %get-tuple-element.20), channel_id=1, source_target_pairs={{0,4},{4,0},{8,12},{12,8},{16,20},{20,16},{24,28},{28,24},{1,5},{5... | collective-permute-start | bytes 73736 | tf_op jit(solution)/shard_map/ppermute | solution.py:478
  1.7 0.2 %shard_map.47 = (f32[3,8,1024]{2,1,0:T(8,128)S(1)}, f32[9,8,128]{2,1,0:T(8,128)S(1)}) custom-call(f32[3,1,8,1024]{3,2,1,0:T(8,128)S(1)} %get-tuple-element.15.w_ref, f32[3,1,8,1024]{3,2,1,0:T(8,128)S(1)} %get-tuple-element.16.u_ref, f32[9,1,8,1024]{3,2,1,0:T(8,128)S(1)} %get-tuple-element.17.g_ref), custom_call_target="tpu_custom_call" | custom-call | tf_op jit(solution)/shard_map/pallas_call | solution.py:509
  1.9 0.7 %collective-permute-done.got_ref = f32[6,8,128]{2,1,0:T(8,128)S(1)} collective-permute-done((f32[6,8,128]{2,1,0:T(8,128)S(1)}, f32[6,8,128]{2,1,0:T(8,128)S(1)}, u32[]{:S(2)}, u32[]{:S(2)}) %collective-permute-start) | collective-permute-done | bytes 24608 | tf_op jit(solution)/shard_map/ppermute | solution.py:478
  2.6 3.0 %collective-permute-start.1 = (f32[12,8,128]{2,1,0:T(8,128)S(1)}, f32[12,8,128]{2,1,0:T(8,128)S(1)}, u32[]{:S(2)}, u32[]{:S(2)}) collective-permute-start(f32[12,8,128]{2,1,0:T(8,128)S(1)} %shard_map.48), channel_id=1, source_target_pairs={{0,1},{1,0},{2,3},{3,2},{4,7},{5,6},{6,5},{7,4},{8,9},{9,8},{10,11... | collective-permute-start | bytes 147464 | tf_op jit(solution)/shard_map/ppermute | solution.py:546
  5.6 1.9 %collective-permute-start.2 = (f32[9,8,128]{2,1,0:T(8,128)S(1)}, f32[9,8,128]{2,1,0:T(8,128)S(1)}, u32[]{:S(2)}, u32[]{:S(2)}) collective-permute-start(f32[9,8,128]{2,1,0:T(8,128)S(1)} %get-tuple-element.21.face_ref.own_ref), channel_id=1, source_target_pairs={{0,4},{4,0},{8,12},{12,8},{16,20},{20,16},{24,28},{28,24},{1,5},{5... | collective-permute-start | bytes 110600 | tf_op jit(solution)/shard_map/ppermute | solution.py:478
  7.4 0.9 %collective-permute-done.2.got_ref = f32[9,8,128]{2,1,0:T(8,128)S(1)} collective-permute-done((f32[9,8,128]{2,1,0:T(8,128)S(1)}, f32[9,8,128]{2,1,0:T(8,128)S(1)}, u32[]{:S(2)}, u32[]{:S(2)}) %collective-permute-start.2) | collective-permute-done | bytes 36896 | tf_op jit(solution)/shard_map/ppermute | solution.py:478
  8.3 0.0 collective-permute-done.1.spill_ref
  8.3 0.3 %shard_map.49 = (f32[13,8,128]{2,1,0:T(8,128)S(1)}, f32[19,8,128]{2,1,0:T(8,128)S(1)}) custom-call(f32[9,8,128]{2,1,0:T(8,128)S(1)} %get-tuple-element.21.face_ref.own_ref, f32[9,8,128]{2,1,0:T(8,128)S(1)} %collective-permute-done.2.got_ref, f32[12,8,128]{2,1,0:T(8,128)S(1)} %collective-permute-done.1.spill_ref, f32[8,128]{1,0:T(8,128)S(1)} %get-tuple-element.22.meta_ref), custom_call_target="tpu_custom_call" | custom-call | tf_op jit(solution)/shard_map/pallas_call | solution.py:509
  8.6 2.5 %collective-permute-start.5 = (f32[13,8,128]{2,1,0:T(8,128)S(1)}, f32[13,8,128]{2,1,0:T(8,128)S(1)}, u32[]{:S(2)}, u32[]{:S(2)}) collective-permute-start(f32[13,8,128]{2,1,0:T(8,128)S(1)} %get-tuple-element.23.refs_0_), channel_id=1, source_target_pairs={{0,24},{4,28},{8,16},{12,20},{16,8},{20,12},{24,0},{28,4},{1,25},{... | collective-permute-start | bytes 159752 | tf_op jit(solution)/shard_map/ppermute | solution.py:478
  11.1 0.5 %collective-permute-start.4 = (f32[13,8,128]{2,1,0:T(8,128)S(1)}, f32[13,8,128]{2,1,0:T(8,128)S(1)}, u32[]{:S(2)}, u32[]{:S(2)}) collective-permute-start(f32[13,8,128]{2,1,0:T(8,128)S(1)} %get-tuple-element.23.refs_0_), channel_id=1, source_target_pairs={{0,16},{4,20},{8,24},{12,28},{16,0},{20,4},{24,8},{28,12},{1,17},{... | collective-permute-start | bytes 159752 | tf_op jit(solution)/shard_map/ppermute | solution.py:478
  11.6 0.5 %collective-permute-start.3 = (f32[13,8,128]{2,1,0:T(8,128)S(1)}, f32[13,8,128]{2,1,0:T(8,128)S(1)}, u32[]{:S(2)}, u32[]{:S(2)}) collective-permute-start(f32[13,8,128]{2,1,0:T(8,128)S(1)} %get-tuple-element.23.refs_0_), channel_id=1, source_target_pairs={{0,8},{4,12},{8,0},{12,4},{16,24},{20,28},{24,16},{28,20},{1,9},{5... | collective-permute-start | bytes 159752 | tf_op jit(solution)/shard_map/ppermute | solution.py:478
  12.1 0.0 collective-permute-start.6
  12.1 1.8 %collective-permute-done.5.refs_3_ = f32[13,8,128]{2,1,0:T(8,128)S(1)} collective-permute-done((f32[13,8,128]{2,1,0:T(8,128)S(1)}, f32[13,8,128]{2,1,0:T(8,128)S(1)}, u32[]{:S(2)}, u32[]{:S(2)}) %collective-permute-start.5) | collective-permute-done | bytes 53280 | tf_op jit(solution)/shard_map/ppermute | solution.py:478
  13.9 0.0 collective-permute-start.9
  13.9 1.3 %collective-permute-done.4.refs_2_ = f32[13,8,128]{2,1,0:T(8,128)S(1)} collective-permute-done((f32[13,8,128]{2,1,0:T(8,128)S(1)}, f32[13,8,128]{2,1,0:T(8,128)S(1)}, u32[]{:S(2)}, u32[]{:S(2)}) %collective-permute-start.4) | collective-permute-done | bytes 53280 | tf_op jit(solution)/shard_map/ppermute | solution.py:478
  15.2 0.0 collective-permute-start.8
  15.2 0.5 %collective-permute-done.3.refs_1_ = f32[13,8,128]{2,1,0:T(8,128)S(1)} collective-permute-done((f32[13,8,128]{2,1,0:T(8,128)S(1)}, f32[13,8,128]{2,1,0:T(8,128)S(1)}, u32[]{:S(2)}, u32[]{:S(2)}) %collective-permute-start.3) | collective-permute-done | bytes 53280 | tf_op jit(solution)/shard_map/ppermute | solution.py:478
  15.7 0.0 collective-permute-start.7
  15.7 0.0 collective-permute-done.6.refs_4_
  15.7 0.0 collective-permute-done.9.refs_7_
  15.7 0.7 %collective-permute-done.8.refs_6_ = f32[13,8,128]{2,1,0:T(8,128)S(1)} collective-permute-done((f32[13,8,128]{2,1,0:T(8,128)S(1)}, f32[13,8,128]{2,1,0:T(8,128)S(1)}, u32[]{:S(2)}, u32[]{:S(2)}) %collective-permute-start.8) | collective-permute-done | bytes 53280 | tf_op jit(solution)/shard_map/ppermute | solution.py:478
  16.5 0.5 %collective-permute-done.7.refs_5_ = f32[13,8,128]{2,1,0:T(8,128)S(1)} collective-permute-done((f32[13,8,128]{2,1,0:T(8,128)S(1)}, f32[13,8,128]{2,1,0:T(8,128)S(1)}, u32[]{:S(2)}, u32[]{:S(2)}) %collective-permute-start.7) | collective-permute-done | bytes 53280 | tf_op jit(solution)/shard_map/ppermute | solution.py:478
  17.0 1.2 %shard_map.50 = f32[3,1,8,1024]{3,2,1,0:T(8,128)} custom-call(f32[3,8,1024]{2,1,0:T(8,128)S(1)} %get-tuple-element.18.after_ref, f32[3,1,8,1024]{3,2,1,0:T(8,128)S(1)} %get-tuple-element.16.u_ref, f32[12,8,128]{2,1,0:T(8,128)S(1)} %collective-permute-done.1.spill_ref, f32[13,8,128]{2,1,0:T(8,128)S(1)} %get-tuple-element.23.refs_0_, ...), custom_call_target="tpu_custom_call" | custom-call | tf_op jit(solution)/shard_map/pallas_call | solution.py:509
  (1 shorter events, 0.0 us)
Async XLA Ops:
  1.2 1.4 %collective-permute-start = (f32[6,8,128]{2,1,0:T(8,128)S(1)}, f32[6,8,128]{2,1,0:T(8,128)S(1)}, u32[]{:S(2)}, u32[]{:S(2)}) collective-permute-start(f32[6,8,128]{2,1,0:T(8,128)S(1)} %get-tuple-element.20), channel_id=1, source_target_pairs={{0,4},{4,0},{8,12},{12,8},{16,20},{20,16},{24,28},{28,24},{1,5},{5... | collective-permute-start | bytes 73736 | tf_op jit(solution)/shard_map/ppermute | solution.py:478
  2.6 5.7 %collective-permute-start.1 = (f32[12,8,128]{2,1,0:T(8,128)S(1)}, f32[12,8,128]{2,1,0:T(8,128)S(1)}, u32[]{:S(2)}, u32[]{:S(2)}) collective-permute-start(f32[12,8,128]{2,1,0:T(8,128)S(1)} %shard_map.48), channel_id=1, source_target_pairs={{0,1},{1,0},{2,3},{3,2},{4,7},{5,6},{6,5},{7,4},{8,9},{9,8},{10,11... | collective-permute-start | bytes 147464 | tf_op jit(solution)/shard_map/ppermute | solution.py:546
  5.6 2.7 %collective-permute-start.2 = (f32[9,8,128]{2,1,0:T(8,128)S(1)}, f32[9,8,128]{2,1,0:T(8,128)S(1)}, u32[]{:S(2)}, u32[]{:S(2)}) collective-permute-start(f32[9,8,128]{2,1,0:T(8,128)S(1)} %get-tuple-element.21.face_ref.own_ref), channel_id=1, source_target_pairs={{0,4},{4,0},{8,12},{12,8},{16,20},{20,16},{24,28},{28,24},{1,5},{5... | collective-permute-start | bytes 110600 | tf_op jit(solution)/shard_map/ppermute | solution.py:478
  8.6 5.3 %collective-permute-start.5 = (f32[13,8,128]{2,1,0:T(8,128)S(1)}, f32[13,8,128]{2,1,0:T(8,128)S(1)}, u32[]{:S(2)}, u32[]{:S(2)}) collective-permute-start(f32[13,8,128]{2,1,0:T(8,128)S(1)} %get-tuple-element.23.refs_0_), channel_id=1, source_target_pairs={{0,24},{4,28},{8,16},{12,20},{16,8},{20,12},{24,0},{28,4},{1,25},{... | collective-permute-start | bytes 159752 | tf_op jit(solution)/shard_map/ppermute | solution.py:478
  11.1 4.1 %collective-permute-start.4 = (f32[13,8,128]{2,1,0:T(8,128)S(1)}, f32[13,8,128]{2,1,0:T(8,128)S(1)}, u32[]{:S(2)}, u32[]{:S(2)}) collective-permute-start(f32[13,8,128]{2,1,0:T(8,128)S(1)} %get-tuple-element.23.refs_0_), channel_id=1, source_target_pairs={{0,16},{4,20},{8,24},{12,28},{16,0},{20,4},{24,8},{28,12},{1,17},{... | collective-permute-start | bytes 159752 | tf_op jit(solution)/shard_map/ppermute | solution.py:478
  11.6 4.1 %collective-permute-start.3 = (f32[13,8,128]{2,1,0:T(8,128)S(1)}, f32[13,8,128]{2,1,0:T(8,128)S(1)}, u32[]{:S(2)}, u32[]{:S(2)}) collective-permute-start(f32[13,8,128]{2,1,0:T(8,128)S(1)} %get-tuple-element.23.refs_0_), channel_id=1, source_target_pairs={{0,8},{4,12},{8,0},{12,4},{16,24},{20,28},{24,16},{28,20},{1,9},{5... | collective-permute-start | bytes 159752 | tf_op jit(solution)/shard_map/ppermute | solution.py:478
  12.1 3.6 %collective-permute-start.6 = (f32[19,8,128]{2,1,0:T(8,128)S(1)}, f32[19,8,128]{2,1,0:T(8,128)S(1)}, u32[]{:S(2)}, u32[]{:S(2)}) collective-permute-start(f32[19,8,128]{2,1,0:T(8,128)S(1)} %get-tuple-element.24), channel_id=1, source_target_pairs={{0,4},{4,0},{8,12},{12,8},{16,20},{20,16},{24,28},{28,24},{1,5},{5... | collective-permute-start | bytes 233480 | tf_op jit(solution)/shard_map/ppermute | solution.py:478
  13.9 1.9 %collective-permute-start.9 = (f32[13,8,128]{2,1,0:T(8,128)S(1)}, f32[13,8,128]{2,1,0:T(8,128)S(1)}, u32[]{:S(2)}, u32[]{:S(2)}) collective-permute-start(f32[13,8,128]{2,1,0:T(8,128)S(1)} %collective-permute-done.5.refs_3_), channel_id=1, source_target_pairs={{0,4},{4,0},{8,12},{12,8},{16,20},{20,16},{24,28},{28,24},{1,5},{5... | collective-permute-start | bytes 159752 | tf_op jit(solution)/shard_map/ppermute | solution.py:478
  15.2 1.2 %collective-permute-start.8 = (f32[13,8,128]{2,1,0:T(8,128)S(1)}, f32[13,8,128]{2,1,0:T(8,128)S(1)}, u32[]{:S(2)}, u32[]{:S(2)}) collective-permute-start(f32[13,8,128]{2,1,0:T(8,128)S(1)} %collective-permute-done.4.refs_2_), channel_id=1, source_target_pairs={{0,4},{4,0},{8,12},{12,8},{16,20},{20,16},{24,28},{28,24},{1,5},{5... | collective-permute-start | bytes 159752 | tf_op jit(solution)/shard_map/ppermute | solution.py:478
  15.7 1.2 %collective-permute-start.7 = (f32[13,8,128]{2,1,0:T(8,128)S(1)}, f32[13,8,128]{2,1,0:T(8,128)S(1)}, u32[]{:S(2)}, u32[]{:S(2)}) collective-permute-start(f32[13,8,128]{2,1,0:T(8,128)S(1)} %collective-permute-done.3.refs_1_), channel_id=1, source_target_pairs={{0,4},{4,0},{8,12},{12,8},{16,20},{20,16},{24,28},{28,24},{1,5},{5... | collective-permute-start | bytes 159752 | tf_op jit(solution)/shard_map/ppermute | solution.py:478

commit v4 on v3

--- a/solution.py
+++ b/solution.py
@@ -209,7 +209,7 @@
     meta_ref[...] = meta
 
 
-def inside_kernel(slab, w_ref, u_ref, g_ref, after_ref, face_ref):
+def inside_kernel(slab, w_ref, u_ref, g_ref, meta_ref, after_ref, face_ref):
     rows, lanes = iotas()
     after = [[], [], []]
     for t in range(TILES):
@@ -229,6 +229,7 @@
     faces += [y_face(u1), z_face(u1), z_face(u2)]
     for n, face in enumerate(faces):
         face_ref[n] = face
+    face_ref[FACES] = extra_of(slab, faces, meta_ref[...])
 
 
 def pair_kernel(keep_ref, got_ref, face_ref, both_ref):
@@ -262,27 +263,36 @@
     return extra
 
 
-def middle_kernel(slab, own_ref, got_ref, spill_ref, meta_ref, sent_ref, own_sent_ref):
+def middle_kernel(slab, own_ref, got_ref, spill_ref, sent_ref, own_sent_ref):
     second = lax.axis_index("blk") % 2 == 1
-    for p, ref in enumerate((own_ref, got_ref)):
-        packed = [spill_ref[PACKED * p + j] for j in range(PACKED)]
-        for n, tile in enumerate(spills_of(slab, ref, packed)):
-            tile = jnp.where(second, packed[n], tile)
-            sent_ref[SPILLS * p + n] = tile
-            own_sent_ref[SPILLS * p + n] = tile
-            if p == 1:
-                own_sent_ref[SENT + n] = packed[n]
-    extra = extra_of(slab, own_ref, meta_ref[...])
-    sent_ref[2 * PACKED] = extra
-    own_sent_ref[2 * PACKED] = extra
-
-
-def middle_kernel_alone(slab, face_ref, near_ref, far_ref, meta_ref, sent_ref):
+    packed = [spill_ref[j] for j in range(2 * PACKED)]
+
+    def put(n, tile):
+        sent_ref[n] = tile
+        own_sent_ref[n] = tile
+
+    @pl.when(second)
+    def _():
+        for n, tile in enumerate(packed):
+            put(n, tile)
+
+    @pl.when(jnp.logical_not(second))
+    def _():
+        for p, ref in enumerate((own_ref, got_ref)):
+            for n, tile in enumerate(spills_of(slab, ref, packed[PACKED * p : PACKED * (p + 1)])):
+                put(SPILLS * p + n, tile)
+
+    for j in range(PACKED):
+        own_sent_ref[SENT + j] = packed[PACKED + j]
+    put(2 * PACKED, own_ref[FACES])
+
+
+def middle_kernel_alone(slab, face_ref, near_ref, far_ref, sent_ref):
     packed = [near_ref[j] for j in range(PACKED)]
     for n, tile in enumerate(spills_of(slab, face_ref, packed)):
         sent_ref[n] = tile
         sent_ref[SPILLS + n] = far_ref[n]
-    sent_ref[2 * PACKED] = extra_of(slab, face_ref, meta_ref[...])
+    sent_ref[2 * PACKED] = face_ref[FACES]
 
 
 def last_kernel(slab, slabs, paired, after_ref, u_ref, spill_ref, *refs):
@@ -320,7 +330,8 @@
             held, other = block_refs[slot // 2], block_refs[chips + slot // 2]
             p = slot % 2
 
-            def on_core(core, n, held=held, other=other):
+            def on_core(core, n, held=held, other=other, crossed=slot > 1):
+                core = 1 - core if crossed else core
                 mine, theirs = held[n], other[n]
                 return jnp.where(second, theirs, mine) if core == 0 else jnp.where(second, mine, theirs)
 
@@ -535,10 +546,11 @@
     )(*(pltpu.with_memory_space_constraint(a, pltpu.HBM) for a in inputs))
     after, faces = call(
         functools.partial(inside_kernel, slab),
-        (shape(3, 8, B * B), tiles(FACES)),
+        (shape(3, 8, B * B), tiles(FACES + 1)),
         vorticity,
         velocity,
         gradient,
+        meta,
     )
     if paired:
         got = swapped(give, 1, blocks)
@@ -559,15 +571,14 @@
             faces,
             got_faces,
             spill,
-            meta,
         )
-        held = [sent] + [swapped(sent, d, blocks) for d in range(2, blocks, 2)]
+        held = [sent] + [swapped(sent, d ^ 1, blocks) for d in range(2, blocks, 2)]
         arrays = held + [swapped(array, 1, blocks) for array in [own_sent] + held[1:]]
     else:
         spill = lax.ppermute(keep, "sub", [(s, near_slab(s, slabs)) for s in range(slabs)])
         far = lax.ppermute(give, "sub", [(s, far_slab(s, slabs)) for s in range(slabs)])
         sent = call(
-            functools.partial(middle_kernel_alone, slab), tiles(SENT), faces, spill, far, meta
+            functools.partial(middle_kernel_alone, slab), tiles(SENT), faces, spill, far
         )
         arrays = [lax.all_gather(sent, "blk")]
     room = (16 << 20) + (0 if paired else arrays[0].size * 4)

time: 18.3 us -> 17.7 us (0.967)
  waiting for transfers between devices: 6.34 us -> 5.14 us
  starting transfers between devices: 8.93 us -> 9.54 us
    ppermute x9, waiting for transfers between devices: 6.34 us -> 5.14 us  [swapped(): return lax.ppermute(array, 'blk', [(i, i ^ d) for i in range(blocks)])]
    ppermute x9, starting transfers between devices: 5.95 us -> 6.55 us  [swapped(): return lax.ppermute(array, 'blk', [(i, i ^ d) for i in range(blocks)])]
  transfers between devices with their start and end apart: 10 -> 10, of which waited for: 7 -> 6; matrix products, arithmetic and copies ran while one was open for 0% -> 0% of each run, Pallas kernels for 1% -> 1%
where the time goes in v4:
time: 17.7 us; the launch traced here: 17.5 us
  starting transfers between devices  9.54 us (54%)
  waiting for transfers between devices  5.14 us (29%)
  Pallas kernels  2.84 us (16%)
    ppermute x9, starting transfers between devices, swapped(): return lax.ppermute(array, 'blk', [(i, i ^ d) for i in range(blocks)])  6.55 us
    ppermute x9, waiting for transfers between devices, swapped(): return lax.ppermute(array, 'blk', [(i, i ^ d) for i in range(blocks)])  5.14 us
    ppermute x1, starting transfers between devices, shards(): lax.ppermute(both, ('blk', 'sub'), [(b * slabs + s, b * slabs + (far_slab...  2.98 us
    pallas_call x4, Pallas kernels, call(): pl.pallas_call(kernel, out_shape=out_shape, in_specs=[vmem] * len(args),...  1.65 us
    pallas_call x1, Pallas kernels, shards(): pl.pallas_call(functools.partial(spill_kernel, slab, paired), out_shape=(...  1.19 us
  transfers between devices with their start and end apart: 10, of which 6 were waited for; matrix products, arithmetic and copies ran while one was open for 0% of the time, Pallas kernels for 1%

profile of v4, /device:TPU:0, one launch (start us, length us, event | category | flops | bytes accessed | tf_op | source)
XLA Modules:
  0.0 17.5 jit_solution(17224825596488527450)
XLA Ops:
  0.0 1.2 %shard_map.46 = (f32[3,1,8,1024]{3,2,1,0:T(8,128)S(1)}, f32[3,1,8,1024]{3,2,1,0:T(8,128)S(1)}, f32[9,1,8,1024]{3,2,1,0:T(8,128)S(1)}, f32[6,8,128]{2,1,0:T(8,128...) custom-call(s32[1,6]{1,0:T(1,128)} %refs_0_.1, f32[3,1,8,1024]{3,2,1,0:T(8,128)} %refs_1_.1, ...), custom_call_target="tpu_custom_call" | custom-call | tf_op jit(solution)/shard_map/pallas_call | solution.py:529
  1.2 0.5 %collective-permute-start = (f32[6,8,128]{2,1,0:T(8,128)S(1)}, f32[6,8,128]{2,1,0:T(8,128)S(1)}, u32[]{:S(2)}, u32[]{:S(2)}) collective-permute-start(f32[6,8,128]{2,1,0:T(8,128)S(1)} %get-tuple-element.21), channel_id=1, source_target_pairs={{0,4},{4,0},{8,12},{12,8},{16,20},{20,16},{24,28},{28,24},{1,5},{5... | collective-permute-start | bytes 73736 | tf_op jit(solution)/shard_map/ppermute | solution.py:489
  1.7 0.2 %shard_map.47 = (f32[3,8,1024]{2,1,0:T(8,128)S(1)}, f32[10,8,128]{2,1,0:T(8,128)S(1)}) custom-call(f32[3,1,8,1024]{3,2,1,0:T(8,128)S(1)} %get-tuple-element.15.w_ref, f32[3,1,8,1024]{3,2,1,0:T(8,128)S(1)} %get-tuple-element.16.u_ref, f32[9,1,8,1024]{3,2,1,0:T(8,128)S(1)} %get-tuple-element.17.g_ref, f32[8,128]{1,0:T(8,128)S(1)} %get-tuple-element.18.meta_ref), custom_call_target="tpu_custom_call" | custom-call | tf_op jit(solution)/shard_map/pallas_call | solution.py:520
  1.9 0.7 %collective-permute-done.got_ref = f32[6,8,128]{2,1,0:T(8,128)S(1)} collective-permute-done((f32[6,8,128]{2,1,0:T(8,128)S(1)}, f32[6,8,128]{2,1,0:T(8,128)S(1)}, u32[]{:S(2)}, u32[]{:S(2)}) %collective-permute-start) | collective-permute-done | bytes 24608 | tf_op jit(solution)/shard_map/ppermute | solution.py:489
  2.6 3.0 %collective-permute-start.1 = (f32[12,8,128]{2,1,0:T(8,128)S(1)}, f32[12,8,128]{2,1,0:T(8,128)S(1)}, u32[]{:S(2)}, u32[]{:S(2)}) collective-permute-start(f32[12,8,128]{2,1,0:T(8,128)S(1)} %shard_map.48), channel_id=1, source_target_pairs={{0,1},{1,0},{2,3},{3,2},{4,7},{5,6},{6,5},{7,4},{8,9},{9,8},{10,11... | collective-permute-start | bytes 147464 | tf_op jit(solution)/shard_map/ppermute | solution.py:558
  5.6 1.9 %collective-permute-start.2 = (f32[10,8,128]{2,1,0:T(8,128)S(1)}, f32[10,8,128]{2,1,0:T(8,128)S(1)}, u32[]{:S(2)}, u32[]{:S(2)}) collective-permute-start(f32[10,8,128]{2,1,0:T(8,128)S(1)} %get-tuple-element.22.face_ref.own_ref), channel_id=1, source_target_pairs={{0,4},{4,0},{8,12},{12,8},{16,20},{20,16},{24,28},{28,24},{1,5},{5... | collective-permute-start | bytes 122888 | tf_op jit(solution)/shard_map/ppermute | solution.py:489
  7.4 0.9 %collective-permute-done.2.got_ref = f32[10,8,128]{2,1,0:T(8,128)S(1)} collective-permute-done((f32[10,8,128]{2,1,0:T(8,128)S(1)}, f32[10,8,128]{2,1,0:T(8,128)S(1)}, u32[]{:S(2)}, u32[]{:S(2)}) %collective-permute-start.2) | collective-permute-done | bytes 40992 | tf_op jit(solution)/shard_map/ppermute | solution.py:489
  8.3 0.0 collective-permute-done.1.spill_ref
  8.3 0.3 %shard_map.49 = (f32[13,8,128]{2,1,0:T(8,128)S(1)}, f32[19,8,128]{2,1,0:T(8,128)S(1)}) custom-call(f32[10,8,128]{2,1,0:T(8,128)S(1)} %get-tuple-element.22.face_ref.own_ref, f32[10,8,128]{2,1,0:T(8,128)S(1)} %collective-permute-done.2.got_ref, f32[12,8,128]{2,1,0:T(8,128)S(1)} %collective-permute-done.1.spill_ref), custom_call_target="tpu_custom_call" | custom-call | tf_op jit(solution)/shard_map/pallas_call | solution.py:520
  8.6 2.5 %collective-permute-start.5 = (f32[13,8,128]{2,1,0:T(8,128)S(1)}, f32[13,8,128]{2,1,0:T(8,128)S(1)}, u32[]{:S(2)}, u32[]{:S(2)}) collective-permute-start(f32[13,8,128]{2,1,0:T(8,128)S(1)} %get-tuple-element.23.refs_0_), channel_id=1, source_target_pairs={{0,28},{4,24},{8,20},{12,16},{16,12},{20,8},{24,4},{28,0},{1,29},{... | collective-permute-start | bytes 159752 | tf_op jit(solution)/shard_map/ppermute | solution.py:489
  11.0 0.3 %collective-permute-start.4 = (f32[13,8,128]{2,1,0:T(8,128)S(1)}, f32[13,8,128]{2,1,0:T(8,128)S(1)}, u32[]{:S(2)}, u32[]{:S(2)}) collective-permute-start(f32[13,8,128]{2,1,0:T(8,128)S(1)} %get-tuple-element.23.refs_0_), channel_id=1, source_target_pairs={{0,20},{4,16},{8,28},{12,24},{16,4},{20,0},{24,12},{28,8},{1,21},{... | collective-permute-start | bytes 159752 | tf_op jit(solution)/shard_map/ppermute | solution.py:489
  11.3 0.5 %collective-permute-start.3 = (f32[13,8,128]{2,1,0:T(8,128)S(1)}, f32[13,8,128]{2,1,0:T(8,128)S(1)}, u32[]{:S(2)}, u32[]{:S(2)}) collective-permute-start(f32[13,8,128]{2,1,0:T(8,128)S(1)} %get-tuple-element.23.refs_0_), channel_id=1, source_target_pairs={{0,12},{4,8},{8,4},{12,0},{16,28},{20,24},{24,20},{28,16},{1,13},{... | collective-permute-start | bytes 159752 | tf_op jit(solution)/shard_map/ppermute | solution.py:489
  11.8 0.2 collective-permute-start.6
  12.0 1.3 %collective-permute-done.5.refs_3_ = f32[13,8,128]{2,1,0:T(8,128)S(1)} collective-permute-done((f32[13,8,128]{2,1,0:T(8,128)S(1)}, f32[13,8,128]{2,1,0:T(8,128)S(1)}, u32[]{:S(2)}, u32[]{:S(2)}) %collective-permute-start.5) | collective-permute-done | bytes 53280 | tf_op jit(solution)/shard_map/ppermute | solution.py:489
  13.2 0.3 %collective-permute-start.9 = (f32[13,8,128]{2,1,0:T(8,128)S(1)}, f32[13,8,128]{2,1,0:T(8,128)S(1)}, u32[]{:S(2)}, u32[]{:S(2)}) collective-permute-start(f32[13,8,128]{2,1,0:T(8,128)S(1)} %collective-permute-done.5.refs_3_), channel_id=1, source_target_pairs={{0,4},{4,0},{8,12},{12,8},{16,20},{20,16},{24,28},{28,24},{1,5},{5... | collective-permute-start | bytes 159752 | tf_op jit(solution)/shard_map/ppermute | solution.py:489
  13.5 1.4 %collective-permute-done.4.refs_2_ = f32[13,8,128]{2,1,0:T(8,128)S(1)} collective-permute-done((f32[13,8,128]{2,1,0:T(8,128)S(1)}, f32[13,8,128]{2,1,0:T(8,128)S(1)}, u32[]{:S(2)}, u32[]{:S(2)}) %collective-permute-start.4) | collective-permute-done | bytes 53280 | tf_op jit(solution)/shard_map/ppermute | solution.py:489
  14.9 0.2 %collective-permute-start.8 = (f32[13,8,128]{2,1,0:T(8,128)S(1)}, f32[13,8,128]{2,1,0:T(8,128)S(1)}, u32[]{:S(2)}, u32[]{:S(2)}) collective-permute-start(f32[13,8,128]{2,1,0:T(8,128)S(1)} %collective-permute-done.4.refs_2_), channel_id=1, source_target_pairs={{0,4},{4,0},{8,12},{12,8},{16,20},{20,16},{24,28},{28,24},{1,5},{5... | collective-permute-start | bytes 159752 | tf_op jit(solution)/shard_map/ppermute | solution.py:489
  15.1 0.0 collective-permute-done.3.refs_1_
  15.1 0.3 %collective-permute-start.7 = (f32[13,8,128]{2,1,0:T(8,128)S(1)}, f32[13,8,128]{2,1,0:T(8,128)S(1)}, u32[]{:S(2)}, u32[]{:S(2)}) collective-permute-start(f32[13,8,128]{2,1,0:T(8,128)S(1)} %collective-permute-done.3.refs_1_), channel_id=1, source_target_pairs={{0,4},{4,0},{8,12},{12,8},{16,20},{20,16},{24,28},{28,24},{1,5},{5... | collective-permute-start | bytes 159752 | tf_op jit(solution)/shard_map/ppermute | solution.py:489
  15.4 0.0 collective-permute-done.6.refs_4_
  15.4 0.0 collective-permute-done.9.refs_7_
  15.4 0.7 %collective-permute-done.8.refs_6_ = f32[13,8,128]{2,1,0:T(8,128)S(1)} collective-permute-done((f32[13,8,128]{2,1,0:T(8,128)S(1)}, f32[13,8,128]{2,1,0:T(8,128)S(1)}, u32[]{:S(2)}, u32[]{:S(2)}) %collective-permute-start.8) | collective-permute-done | bytes 53280 | tf_op jit(solution)/shard_map/ppermute | solution.py:489
  16.2 0.2 %collective-permute-done.7.refs_5_ = f32[13,8,128]{2,1,0:T(8,128)S(1)} collective-permute-done((f32[13,8,128]{2,1,0:T(8,128)S(1)}, f32[13,8,128]{2,1,0:T(8,128)S(1)}, u32[]{:S(2)}, u32[]{:S(2)}) %collective-permute-start.7) | collective-permute-done | bytes 53280 | tf_op jit(solution)/shard_map/ppermute | solution.py:489
  16.4 1.2 %shard_map.50 = f32[3,1,8,1024]{3,2,1,0:T(8,128)} custom-call(f32[3,8,1024]{2,1,0:T(8,128)S(1)} %get-tuple-element.19.after_ref, f32[3,1,8,1024]{3,2,1,0:T(8,128)S(1)} %get-tuple-element.16.u_ref, f32[12,8,128]{2,1,0:T(8,128)S(1)} %collective-permute-done.1.spill_ref, f32[13,8,128]{2,1,0:T(8,128)S(1)} %get-tuple-element.23.refs_0_, ...), custom_call_target="tpu_custom_call" | custom-call | tf_op jit(solution)/shard_map/pallas_call | solution.py:520
  (1 shorter events, 0.0 us)
Async XLA Ops:
  1.2 1.4 %collective-permute-start = (f32[6,8,128]{2,1,0:T(8,128)S(1)}, f32[6,8,128]{2,1,0:T(8,128)S(1)}, u32[]{:S(2)}, u32[]{:S(2)}) collective-permute-start(f32[6,8,128]{2,1,0:T(8,128)S(1)} %get-tuple-element.21), channel_id=1, source_target_pairs={{0,4},{4,0},{8,12},{12,8},{16,20},{20,16},{24,28},{28,24},{1,5},{5... | collective-permute-start | bytes 73736 | tf_op jit(solution)/shard_map/ppermute | solution.py:489
  2.6 5.7 %collective-permute-start.1 = (f32[12,8,128]{2,1,0:T(8,128)S(1)}, f32[12,8,128]{2,1,0:T(8,128)S(1)}, u32[]{:S(2)}, u32[]{:S(2)}) collective-permute-start(f32[12,8,128]{2,1,0:T(8,128)S(1)} %shard_map.48), channel_id=1, source_target_pairs={{0,1},{1,0},{2,3},{3,2},{4,7},{5,6},{6,5},{7,4},{8,9},{9,8},{10,11... | collective-permute-start | bytes 147464 | tf_op jit(solution)/shard_map/ppermute | solution.py:558
  5.6 2.7 %collective-permute-start.2 = (f32[10,8,128]{2,1,0:T(8,128)S(1)}, f32[10,8,128]{2,1,0:T(8,128)S(1)}, u32[]{:S(2)}, u32[]{:S(2)}) collective-permute-start(f32[10,8,128]{2,1,0:T(8,128)S(1)} %get-tuple-element.22.face_ref.own_ref), channel_id=1, source_target_pairs={{0,4},{4,0},{8,12},{12,8},{16,20},{20,16},{24,28},{28,24},{1,5},{5... | collective-permute-start | bytes 122888 | tf_op jit(solution)/shard_map/ppermute | solution.py:489
  8.6 4.6 %collective-permute-start.5 = (f32[13,8,128]{2,1,0:T(8,128)S(1)}, f32[13,8,128]{2,1,0:T(8,128)S(1)}, u32[]{:S(2)}, u32[]{:S(2)}) collective-permute-start(f32[13,8,128]{2,1,0:T(8,128)S(1)} %get-tuple-element.23.refs_0_), channel_id=1, source_target_pairs={{0,28},{4,24},{8,20},{12,16},{16,12},{20,8},{24,4},{28,0},{1,29},{... | collective-permute-start | bytes 159752 | tf_op jit(solution)/shard_map/ppermute | solution.py:489
  11.0 3.9 %collective-permute-start.4 = (f32[13,8,128]{2,1,0:T(8,128)S(1)}, f32[13,8,128]{2,1,0:T(8,128)S(1)}, u32[]{:S(2)}, u32[]{:S(2)}) collective-permute-start(f32[13,8,128]{2,1,0:T(8,128)S(1)} %get-tuple-element.23.refs_0_), channel_id=1, source_target_pairs={{0,20},{4,16},{8,28},{12,24},{16,4},{20,0},{24,12},{28,8},{1,21},{... | collective-permute-start | bytes 159752 | tf_op jit(solution)/shard_map/ppermute | solution.py:489
  11.3 3.8 %collective-permute-start.3 = (f32[13,8,128]{2,1,0:T(8,128)S(1)}, f32[13,8,128]{2,1,0:T(8,128)S(1)}, u32[]{:S(2)}, u32[]{:S(2)}) collective-permute-start(f32[13,8,128]{2,1,0:T(8,128)S(1)} %get-tuple-element.23.refs_0_), channel_id=1, source_target_pairs={{0,12},{4,8},{8,4},{12,0},{16,28},{20,24},{24,20},{28,16},{1,13},{... | collective-permute-start | bytes 159752 | tf_op jit(solution)/shard_map/ppermute | solution.py:489
  11.8 3.6 %collective-permute-start.6 = (f32[19,8,128]{2,1,0:T(8,128)S(1)}, f32[19,8,128]{2,1,0:T(8,128)S(1)}, u32[]{:S(2)}, u32[]{:S(2)}) collective-permute-start(f32[19,8,128]{2,1,0:T(8,128)S(1)} %get-tuple-element.24), channel_id=1, source_target_pairs={{0,4},{4,0},{8,12},{12,8},{16,20},{20,16},{24,28},{28,24},{1,5},{5... | collective-permute-start | bytes 233480 | tf_op jit(solution)/shard_map/ppermute | solution.py:489
  13.2 2.2 %collective-permute-start.9 = (f32[13,8,128]{2,1,0:T(8,128)S(1)}, f32[13,8,128]{2,1,0:T(8,128)S(1)}, u32[]{:S(2)}, u32[]{:S(2)}) collective-permute-start(f32[13,8,128]{2,1,0:T(8,128)S(1)} %collective-permute-done.5.refs_3_), channel_id=1, source_target_pairs={{0,4},{4,0},{8,12},{12,8},{16,20},{20,16},{24,28},{28,24},{1,5},{5... | collective-permute-start | bytes 159752 | tf_op jit(solution)/shard_map/ppermute | solution.py:489
  14.9 1.2 %collective-permute-start.8 = (f32[13,8,128]{2,1,0:T(8,128)S(1)}, f32[13,8,128]{2,1,0:T(8,128)S(1)}, u32[]{:S(2)}, u32[]{:S(2)}) collective-permute-start(f32[13,8,128]{2,1,0:T(8,128)S(1)} %collective-permute-done.4.refs_2_), channel_id=1, source_target_pairs={{0,4},{4,0},{8,12},{12,8},{16,20},{20,16},{24,28},{28,24},{1,5},{5... | collective-permute-start | bytes 159752 | tf_op jit(solution)/shard_map/ppermute | solution.py:489
  15.1 1.2 %collective-permute-start.7 = (f32[13,8,128]{2,1,0:T(8,128)S(1)}, f32[13,8,128]{2,1,0:T(8,128)S(1)}, u32[]{:S(2)}, u32[]{:S(2)}) collective-permute-start(f32[13,8,128]{2,1,0:T(8,128)S(1)} %collective-permute-done.3.refs_1_), channel_id=1, source_target_pairs={{0,4},{4,0},{8,12},{12,8},{16,20},{20,16},{24,28},{28,24},{1,5},{5... | collective-permute-start | bytes 159752 | tf_op jit(solution)/shard_map/ppermute | solution.py:489

commit v5 on v3

--- a/solution.py
+++ b/solution.py
@@ -13,11 +13,12 @@
 
 AFTER_Y, AFTER_Z, U1_Y, U1_Z, U2_Z = 0, 3, 6, 7, 8
 FACES = 9
+EXTRA = FACES
 SPILLS = 6
 KEPT = (0, 1, 2, 5, 6, 7)
 PACKED = len(KEPT)
 ROW_U1_Y, ROW_U1_Z, ROW_U2_Z, ROW_CORNER, ROW_BESIDE = 0, 2, 4, 6, 7
-SENT = 2 * PACKED + 1
+SENT = SPILLS + 1 + PACKED
 
 
 def iotas():
@@ -168,8 +169,8 @@
     ]
 
 
-def spill_kernel(slab, paired, *refs):
-    here, (w_ref, u_ref, g_ref, give_ref, keep_ref, meta_ref) = refs[:4], refs[4:10]
+def spill_kernel(slab, *refs):
+    here, (w_ref, u_ref, g_ref, up_ref, down_ref, meta_ref) = refs[:4], refs[4:10]
     nb_ref, sems = refs[10:]
     copies = [
         pltpu.make_async_copy(source, target, sems.at[n])
@@ -180,8 +181,7 @@
     for copy in copies:
         copy.wait()
     rows, lanes = iotas()
-    odd = lax.axis_index("sub") % 2 == 1
-    near, far = [], []
+    ups, downs = [], []
     for t in range(TILES):
         q = stretched(w_ref, g_ref, t)
         u = u_ref[0, 0, :, lane(t)]
@@ -193,23 +193,19 @@
             bottom = jnp.where(mine, pltpu.roll(q[c], 2 * c, 0) if c else q[c], bottom)
         weight = weights(pair_rows(u, slab - 2))
         edge = jnp.where(rows & 1 == 0, pltpu.roll(top * weight[1], 7, 0), 0.0)
-        up = top * weight[2] + edge
+        ups.append(top * weight[2] + edge)
         weight = weights(pair_rows(u, 0))
         edge = jnp.where(rows & 1 == 1, pltpu.roll(bottom * weight[-1], 1, 0), 0.0)
-        down = bottom * weight[-2] + edge
-        near.append(jnp.where(odd, down, up))
-        far.append(jnp.where(odd, up, down))
-    second = lax.axis_index("blk") % 2 == 1
-    for j, (n, f) in enumerate(zip(pack(near), pack(far))):
-        give_ref[j] = jnp.where(second, n, f) if paired else f
-        keep_ref[j] = jnp.where(second, f, n) if paired else n
+        downs.append(bottom * weight[-2] + edge)
+    for j, (up, down) in enumerate(zip(pack(ups), pack(downs))):
+        up_ref[j], down_ref[j] = up, down
     meta = jnp.zeros((8, 128), jnp.float32)
     for j in range(6):
         meta = jnp.where(lanes == j, nb_ref[0, j].astype(jnp.float32), meta)
     meta_ref[...] = meta
 
 
-def inside_kernel(slab, w_ref, u_ref, g_ref, after_ref, face_ref):
+def inside_kernel(slab, slabs, w_ref, u_ref, g_ref, meta_ref, after_ref, face_ref):
     rows, lanes = iotas()
     after = [[], [], []]
     for t in range(TILES):
@@ -227,75 +223,109 @@
     u2 = [u_ref[2, 0, :, lane(t)] for t in range(TILES)]
     faces = [y_face(after[c]) for c in range(3)] + [z_face(after[c]) for c in range(3)]
     faces += [y_face(u1), z_face(u1), z_face(u2)]
+    faces.append(extra_of(slab, slabs, faces, meta_ref[...]))
     for n, face in enumerate(faces):
         face_ref[n] = face
 
 
-def pair_kernel(keep_ref, got_ref, face_ref, both_ref):
-    second = lax.axis_index("blk") % 2 == 1
-    for j in range(PACKED):
-        both_ref[j] = jnp.where(second, got_ref[j], keep_ref[j])
-        both_ref[PACKED + j] = jnp.where(second, keep_ref[j], got_ref[j])
-
-
-def spills_of(slab, face_ref, packed):
-    near_row = jnp.where(lax.axis_index("sub") % 2 == 1, 0, slab - 2)
-    near = unpack(packed)
-    near_y, near_z = y_face(near), z_face(near)
-    in_y = [face_ref[AFTER_Y + c] + placed(near_y, c, near_row) for c in range(3)]
-    in_z = [face_ref[AFTER_Z + c] + placed(near_z, c, near_row) for c in range(3)]
+def extra_of(slab, slabs, faces, meta):
+    rows, lanes = iotas()
+    far_row = jnp.where(lax.axis_index("sub") == slabs - 1, slab - 2, 0)
+    corner = gathered(faces[U2_Z], 4 * z_of((lanes >> 2) & 3) + (lanes & 3))
+    corner = jnp.sum(jnp.where(rows == lanes >> 4, corner, 0.0), axis=0, keepdims=True)
+    extra = jnp.where(rows < ROW_BESIDE, jnp.broadcast_to(corner, (8, 128)), meta)
+    for tile, row in ((U2_Z, ROW_U2_Z), (U1_Z, ROW_U1_Z), (U1_Y, ROW_U1_Y)):
+        moved = pltpu.roll(faces[tile], (row - far_row + 8) % 8, 0)
+        extra = jnp.where(rows < row + 2, moved, extra)
+    return extra
+
+
+def spills_of(slab, face_ref, up, down):
+    up, down = unpack(up), unpack(down)
+    up_y, up_z, down_y, down_z = y_face(up), z_face(up), y_face(down), z_face(down)
+    in_y, in_z = [], []
+    for c in range(3):
+        q = face_ref[AFTER_Y + c] + placed(up_y, c, 0) + placed(down_y, c, slab - 2)
+        in_y.append(q)
+        q = face_ref[AFTER_Z + c] + placed(up_z, c, 0) + placed(down_z, c, slab - 2)
+        in_z.append(q)
     weight = weights(face_ref[U1_Z])
     in_z = [y_pass_of_z_face(q, weight) for q in in_z]
     return y_spill(in_y, face_ref[U1_Y]) + z_spill(in_z, face_ref[U2_Z])
 
 
-def extra_of(slab, face_ref, meta):
-    rows, lanes = iotas()
-    far_row = jnp.where(lax.axis_index("sub") % 2 == 1, slab - 2, 0)
-    extra = meta
-    corner = gathered(face_ref[U2_Z], 4 * z_of((lanes >> 2) & 3) + (lanes & 3))
-    corner = jnp.sum(jnp.where(rows == lanes >> 4, corner, 0.0), axis=0, keepdims=True)
-    extra = jnp.where(rows < ROW_BESIDE, jnp.broadcast_to(corner, (8, 128)), extra)
-    for tile, row in ((U2_Z, ROW_U2_Z), (U1_Z, ROW_U1_Z), (U1_Y, ROW_U1_Y)):
-        moved = pltpu.roll(face_ref[tile], (row - far_row + 8) % 8, 0)
-        extra = jnp.where(rows < row + 2, moved, extra)
-    return extra
-
-
-def middle_kernel(slab, own_ref, got_ref, spill_ref, meta_ref, sent_ref, own_sent_ref):
-    second = lax.axis_index("blk") % 2 == 1
-    for p, ref in enumerate((own_ref, got_ref)):
-        packed = [spill_ref[PACKED * p + j] for j in range(PACKED)]
-        for n, tile in enumerate(spills_of(slab, ref, packed)):
-            tile = jnp.where(second, packed[n], tile)
-            sent_ref[SPILLS * p + n] = tile
-            own_sent_ref[SPILLS * p + n] = tile
-            if p == 1:
-                own_sent_ref[SENT + n] = packed[n]
-    extra = extra_of(slab, own_ref, meta_ref[...])
-    sent_ref[2 * PACKED] = extra
-    own_sent_ref[2 * PACKED] = extra
-
-
-def middle_kernel_alone(slab, face_ref, near_ref, far_ref, meta_ref, sent_ref):
-    packed = [near_ref[j] for j in range(PACKED)]
-    for n, tile in enumerate(spills_of(slab, face_ref, packed)):
+def middle_kernel(slab, slabs, face_ref, own_face_ref, up_ref, down_ref, sent_ref, own_sent_ref):
+    first, last = lax.axis_index("sub") == 0, lax.axis_index("sub") == slabs - 1
+    up, down, far = [], [], []
+    for j in range(PACKED):
+        up.append(jnp.where(first, 0.0, up_ref[j]))
+        down.append(jnp.where(last, 0.0, down_ref[j]))
+        far.append(jnp.where(first, up_ref[j], jnp.where(last, down_ref[j], 0.0)))
+    sent = spills_of(slab, face_ref, up, down) + [own_face_ref[EXTRA]] + far
+    for n, tile in enumerate(sent):
         sent_ref[n] = tile
-        sent_ref[SPILLS + n] = far_ref[n]
-    sent_ref[2 * PACKED] = extra_of(slab, face_ref, meta_ref[...])
-
-
-def last_kernel(slab, slabs, paired, after_ref, u_ref, spill_ref, *refs):
+    for n, tile in enumerate(sent + up + down):
+        own_sent_ref[n] = tile
+
+
+def y_pass(fields, weight):
+    _, lanes = iotas()
+    results = []
+    for tiles in fields:
+        moved = {
+            (t, k): pltpu.roll(tiles[t] * weight[t][k], (32 * k) % 128, 1)
+            for t in range(TILES)
+            for k in (-2, -1, 1, 2)
+        }
+        result = []
+        for t in range(TILES):
+            total = tiles[t] * weight[t][0]
+            for k in (1, 2):
+                other = moved[t - 1, k] if t > 0 else 0.0
+                total = total + jnp.where(lanes < 32 * k, other, moved[t, k])
+                other = moved[t + 1, -k] if t < TILES - 1 else 0.0
+                total = total + jnp.where(lanes >= 128 - 32 * k, other, moved[t, -k])
+            result.append(total)
+        results.append(result)
+    return results
+
+
+def z_pass(q, weight):
+    _, lanes = iotas()
+    z = lanes & 31
+    total = q * weight[0]
+    for k in (1, 2):
+        total = total + jnp.where(z >= k, pltpu.roll(q * weight[k], k, 1), 0.0)
+        total = total + jnp.where(z < B - k, pltpu.roll(q * weight[-k], 128 - k, 1), 0.0)
+    return total
+
+
+def own_kernel(slab, after_ref, u_ref, near_ref, own_ref):
+    up = unpack([near_ref[SENT + j] for j in range(PACKED)])
+    down = unpack([near_ref[SENT + PACKED + j] for j in range(PACKED)])
+    after = [
+        [
+            after_ref[c, :, lane(t)] + placed(up[t], c, 0) + placed(down[t], c, slab - 2)
+            for t in range(TILES)
+        ]
+        for c in range(3)
+    ]
+    after = y_pass(after, [weights(u_ref[1, 0, :, lane(t)]) for t in range(TILES)])
+    for t in range(TILES):
+        weight = weights(u_ref[2, 0, :, lane(t)])
+        for c in range(3):
+            own_ref[c, :, lane(t)] = z_pass(after[c][t], weight)
+
+
+def last_kernel(slab, slabs, paired, own_ref, u_ref, *refs):
     block_refs, out_ref = refs[:-1], refs[-1]
     rows, lanes = iotas()
     here = lax.axis_index("blk")
     place_in = lax.axis_index("sub")
-    odd = place_in % 2 == 1
-    near_row = jnp.where(odd, 0, slab - 2)
-    far_row = jnp.where(odd, slab - 2, 0)
     below_x = place_in == 0
     above_x = place_in == slabs - 1
     at_end = below_x | above_x
+    far_row = jnp.where(above_x, slab - 2, 0)
     x_face = jnp.where(above_x, 1, 0)
     second = here % 2 == 1
     base = here - here % 2 if paired else 0
@@ -309,41 +339,38 @@
                 lambda slot, c: step(
                     slot,
                     lambda n: ref[slot, n],
-                    lambda j: ref[slot, SPILLS + j],
-                    lambda: ref[slot, 2 * PACKED],
+                    lambda j: ref[slot, SPILLS + 1 + j],
+                    lambda: ref[slot, SPILLS],
                     c,
                 ),
                 carry,
             )
-        chips = len(block_refs) // 2
         for slot in range(2 * chips):
-            held, other = block_refs[slot // 2], block_refs[chips + slot // 2]
-            p = slot % 2
-
-            def on_core(core, n, held=held, other=other):
-                mine, theirs = held[n], other[n]
-                return jnp.where(second, theirs, mine) if core == 0 else jnp.where(second, mine, theirs)
-
+            n, p = slot // 2, slot % 2
             carry = step(
                 slot,
-                lambda n, p=p, get=on_core: get(0, SPILLS * p + n),
-                lambda j, p=p, get=on_core: get(1, PACKED * p + j),
-                lambda p=p, get=on_core: get(p, 2 * PACKED),
+                lambda i, n=n, p=p: prepared(n, p, i),
+                lambda j, n=n, p=p: prepared(n, p, SPILLS + 1 + j),
+                lambda n=n, p=p: prepared(n, p, SPILLS),
                 carry,
             )
         return carry
 
-    packed = [spill_ref[j] for j in range(PACKED)]
-    if paired:
-        other = block_refs[len(block_refs) // 2]
-        packed = [jnp.where(second, other[SENT + j], packed[j]) for j in range(PACKED)]
-    near = unpack(packed)
+    chips = len(block_refs) // 2
+
+    def prepared(n, p, tile):
+        held, other = block_refs[n][tile], block_refs[chips + n][tile]
+        held_by_second = (p == 1) == (2 * n not in (2, 4))
+        if tile > SPILLS:
+            held_by_second = not held_by_second
+        return jnp.where(second, held, other) if held_by_second else jnp.where(second, other, held)
+
+    own_extra = block_refs[0][SPILLS] if paired else block_refs[0][here, SPILLS]
 
     def beside(extra, face):
         index = jnp.full((8, 128), face, jnp.int32)
         return gathered(row_of(extra, ROW_BESIDE), index).astype(jnp.int32) ^ base
 
-    own_extra = block_refs[0][2 * PACKED] if paired else block_refs[0][here, 2 * PACKED]
     ym, yp, zm, zp = (beside(own_extra, face) for face in (2, 3, 4, 5))
     outer = jnp.where(at_end, beside(own_extra, x_face), here ^ base)
 
@@ -433,57 +460,26 @@
     by_corner = z_spill([jnp.where(at_edge, y_edges(q), 0.0) for q in into_corner], u2)
     into_z = [into_z[c] + by_corner[c] + placed(by_far, c, far_row) for c in range(3)]
 
-    after_y = [[None] * TILES for c in range(3)]
-    moved = {}
+    def far_rows(c, t):
+        u = pltpu.roll(u_ref[c, 0, :, lane(t)], (8 - far_row) % 8, 0)
+        return weights(pair_rows(u, 0))
+
+    packed = y_pass([far_own], [far_rows(1, t) for t in range(TILES)])[0]
+    packed = [z_pass(packed[t], far_rows(2, t)) for t in range(TILES)]
+    u2 = y_face([u_ref[2, 0, :, lane(t)] for t in range(TILES)])
+    weight = weights(u2)
+    into_y = [z_pass(q, weight) for q in into_y]
+    at_face = (z_cell < 2) | (z_cell >= B - 2)
+    place = jnp.where(z_cell < 2, z_cell, jnp.where(z_cell >= B - 2, z_cell - (B - 4), 0))
     for t in range(TILES):
-        weight = weights(u_ref[1, 0, :, lane(t)])
+        index = 16 * t + 4 * (lanes >> 5) + place
         for c in range(3):
-            q = after_ref[c, :, lane(t)] + placed(near[t], c, near_row) + placed(far_own[t], c, far_row)
-            after_y[c][t] = q * weight[0]
-            for k in (-2, -1, 1, 2):
-                moved[c, t, k] = pltpu.roll(q * weight[k], (32 * k) % 128, 1)
-    for t in range(TILES):
-        for c in range(3):
-            total = after_y[c][t]
-            for k in (1, 2):
-                cut = lanes < 32 * k
-                other = moved[c, t - 1, k] if t > 0 else 0.0
-                total = total + jnp.where(cut, other, moved[c, t, k])
-                cut = lanes >= 128 - 32 * k
-                other = moved[c, t + 1, -k] if t < TILES - 1 else 0.0
-                total = total + jnp.where(cut, other, moved[c, t, -k])
+            total = own_ref[c, :, lane(t)] + placed(packed[t], c, far_row)
             if t == 0:
                 total = total + jnp.where(y_low, into_y[c], 0.0)
             if t == TILES - 1:
                 total = total + jnp.where(y_low, 0.0, into_y[c])
-            after_y[c][t] = total
-
-    at_face = (z_cell < 2) | (z_cell >= B - 2)
-    place = jnp.where(z_cell < 2, z_cell, jnp.where(z_cell >= B - 2, z_cell - (B - 4), 0))
-    for t in range(TILES):
-        weight = weights(u_ref[2, 0, :, lane(t)])
-        index = 16 * t + 4 * (lanes >> 5) + place
-        for c in range(3):
-            q = after_y[c][t]
-            total = q * weight[0]
-            for k in (1, 2):
-                shifted = pltpu.roll(q * weight[k], k, 1)
-                total = total + jnp.where(z_cell >= k, shifted, 0.0)
-                shifted = pltpu.roll(q * weight[-k], 128 - k, 1)
-                total = total + jnp.where(z_cell < B - k, shifted, 0.0)
             out_ref[c, 0, :, lane(t)] = total + jnp.where(at_face, gathered(into_z[c], index), 0.0)
-
-
-def swapped(array, d, blocks):
-    return lax.ppermute(array, "blk", [(i, i ^ d) for i in range(blocks)])
-
-
-def near_slab(s, slabs):
-    return s ^ 1
-
-
-def far_slab(s, slabs):
-    return (s + 1 if s % 2 else s - 1) % slabs
 
 
 def shards(slabs, vorticity, velocity, gradient, neighbour):
@@ -515,8 +511,8 @@
         )(*args)
 
     inputs = (neighbour, vorticity, velocity, gradient)
-    vorticity, velocity, gradient, give, keep, meta = pl.pallas_call(
-        functools.partial(spill_kernel, slab, paired),
+    vorticity, velocity, gradient, up, down, meta = pl.pallas_call(
+        functools.partial(spill_kernel, slab),
         out_shape=(
             shape(*vorticity.shape),
             shape(*velocity.shape),
@@ -534,49 +530,48 @@
         compiler_params=small,
     )(*(pltpu.with_memory_space_constraint(a, pltpu.HBM) for a in inputs))
     after, faces = call(
-        functools.partial(inside_kernel, slab),
-        (shape(3, 8, B * B), tiles(FACES)),
+        functools.partial(inside_kernel, slab, slabs),
+        (shape(3, 8, B * B), tiles(FACES + 1)),
         vorticity,
         velocity,
         gradient,
+        meta,
+    )
+
+    def moved(array, d, step=0):
+        pairs = []
+        for b in range(blocks):
+            for s in range(slabs):
+                c = b ^ d ^ (1 if paired and not 0 <= s + step < slabs else 0)
+                pairs.append((b * slabs + s, c * slabs + (s + step) % slabs))
+        return lax.ppermute(array, ("blk", "sub"), pairs)
+
+    cross = 0
+    up = moved(up, cross, 1)
+    down = moved(down, cross, -1)
+    their_faces = faces
+    sent, near = call(
+        functools.partial(middle_kernel, slab, slabs),
+        (tiles(SENT), tiles(SENT + 2 * PACKED)),
+        their_faces,
+        faces,
+        up,
+        down,
     )
     if paired:
-        got = swapped(give, 1, blocks)
-        both = call(pair_kernel, tiles(2 * PACKED), keep, got, faces)
-        spill = lax.ppermute(
-            both,
-            ("blk", "sub"),
-            [
-                (b * slabs + s, b * slabs + (far_slab if b % 2 else near_slab)(s, slabs))
-                for b in range(blocks)
-                for s in range(slabs)
-            ],
-        )
-        got_faces = swapped(faces, 1, blocks)
-        sent, own_sent = call(
-            functools.partial(middle_kernel, slab),
-            (tiles(SENT), tiles(SENT + PACKED)),
-            faces,
-            got_faces,
-            spill,
-            meta,
-        )
-        held = [sent] + [swapped(sent, d, blocks) for d in range(2, blocks, 2)]
-        arrays = held + [swapped(array, 1, blocks) for array in [own_sent] + held[1:]]
+        held = [sent] + [moved(sent, d ^ (d in (2, 4))) for d in range(2, blocks, 2)]
+        arrays = held + [moved(array, 1) for array in held]
     else:
-        spill = lax.ppermute(keep, "sub", [(s, near_slab(s, slabs)) for s in range(slabs)])
-        far = lax.ppermute(give, "sub", [(s, far_slab(s, slabs)) for s in range(slabs)])
-        sent = call(
-            functools.partial(middle_kernel_alone, slab), tiles(SENT), faces, spill, far, meta
-        )
         arrays = [lax.all_gather(sent, "blk")]
+    own = call(
+        functools.partial(own_kernel, slab), shape(3, 8, B * B), after, velocity, near
+    )
     room = (16 << 20) + (0 if paired else arrays[0].size * 4)
     out = call(
         functools.partial(last_kernel, slab, slabs, paired),
         shape(3, 1, 8, B * B),
-        after,
+        own,
         velocity,
-        spill,
         *arrays,
         params=pltpu.CompilerParams(vmem_limit_bytes=room),
     )

time: 18.3 us -> 17.6 us (0.962)
  starting transfers between devices: 8.93 us -> 8.41 us
  waiting for transfers between devices: 6.34 us -> 5.89 us
  Pallas kernels: 2.85 us -> 3.1 us
    ppermute x10 -> x9, starting transfers between devices: 8.93 us -> 8.41 us  [moved(): return lax.ppermute(array, ('blk', 'sub'), pairs)]
    ppermute x10 -> x9, waiting for transfers between devices: 6.34 us -> 5.89 us  [moved(): return lax.ppermute(array, ('blk', 'sub'), pairs)]
    pallas_call x4, Pallas kernels: 1.65 us -> 1.91 us  [call(): pl.pallas_call(kernel, out_shape=out_shape, in_specs=[vmem] * len(args),...]
  transfers between devices with their start and end apart: 10 -> 9, of which waited for: 7 -> 6; matrix products, arithmetic and copies ran while one was open for 0% -> 0% of each run, Pallas kernels for 1% -> 3%
where the time goes in v5:
time: 17.6 us; the launch traced here: 17.4 us
  starting transfers between devices  8.41 us (48%)
  waiting for transfers between devices  5.89 us (33%)
  Pallas kernels  3.1 us (18%)
    ppermute x9, starting transfers between devices, moved(): return lax.ppermute(array, ('blk', 'sub'), pairs)  8.41 us
    ppermute x9, waiting for transfers between devices, moved(): return lax.ppermute(array, ('blk', 'sub'), pairs)  5.89 us
    pallas_call x4, Pallas kernels, call(): pl.pallas_call(kernel, out_shape=out_shape, in_specs=[vmem] * len(args),...  1.91 us
    pallas_call x1, Pallas kernels, shards(): pl.pallas_call(functools.partial(spill_kernel, slab), out_shape=(shape(*v...  1.19 us
  transfers between devices with their start and end apart: 9, of which 6 were waited for; matrix products, arithmetic and copies ran while one was open for 0% of the time, Pallas kernels for 3%

profile of v5, /device:TPU:0, one launch (start us, length us, event | category | flops | bytes accessed | tf_op | source)
XLA Modules:
  0.0 17.4 jit_solution(6920092288864738479)
XLA Ops:
  0.0 1.2 %shard_map.46 = (f32[3,1,8,1024]{3,2,1,0:T(8,128)S(1)}, f32[3,1,8,1024]{3,2,1,0:T(8,128)S(1)}, f32[9,1,8,1024]{3,2,1,0:T(8,128)S(1)}, f32[6,8,128]{2,1,0:T(8,128...) custom-call(s32[1,6]{1,0:T(1,128)} %refs_0_.1, f32[3,1,8,1024]{3,2,1,0:T(8,128)} %refs_1_.1, ...), custom_call_target="tpu_custom_call" | custom-call | tf_op jit(solution)/shard_map/pallas_call | solution.py:514
  1.2 3.1 %collective-permute-start = (f32[6,8,128]{2,1,0:T(8,128)S(1)}, f32[6,8,128]{2,1,0:T(8,128)S(1)}, u32[]{:S(2)}, u32[]{:S(2)}) collective-permute-start(f32[6,8,128]{2,1,0:T(8,128)S(1)} %get-tuple-element.21), channel_id=1, source_target_pairs={{0,1},{1,2},{2,3},{3,4},{4,5},{5,6},{6,7},{7,0},{8,9},{9,10},{10,1... | collective-permute-start | bytes 73736 | tf_op jit(solution)/shard_map/ppermute | solution.py:547
  4.3 1.5 %collective-permute-start.1 = (f32[6,8,128]{2,1,0:T(8,128)S(1)}, f32[6,8,128]{2,1,0:T(8,128)S(1)}, u32[]{:S(2)}, u32[]{:S(2)}) collective-permute-start(f32[6,8,128]{2,1,0:T(8,128)S(1)} %get-tuple-element.22), channel_id=1, source_target_pairs={{0,7},{1,0},{2,1},{3,2},{4,3},{5,4},{6,5},{7,6},{8,15},{9,8},{10,9... | collective-permute-start | bytes 73736 | tf_op jit(solution)/shard_map/ppermute | solution.py:547
  5.8 0.2 %shard_map.47 = (f32[3,8,1024]{2,1,0:T(8,128)S(1)}, f32[10,8,128]{2,1,0:T(8,128)S(1)}) custom-call(f32[3,1,8,1024]{3,2,1,0:T(8,128)S(1)} %get-tuple-element.15.w_ref, f32[3,1,8,1024]{3,2,1,0:T(8,128)S(1)} %get-tuple-element.16.u_ref, f32[9,1,8,1024]{3,2,1,0:T(8,128)S(1)} %get-tuple-element.17.g_ref, f32[8,128]{1,0:T(8,128)S(1)} %get-tuple-element.18.meta_ref), custom_call_target="tpu_custom_call" | custom-call | tf_op jit(solution)/shard_map/pallas_call | solution.py:505
  6.0 1.3 %collective-permute-done.up_ref = f32[6,8,128]{2,1,0:T(8,128)S(1)} collective-permute-done((f32[6,8,128]{2,1,0:T(8,128)S(1)}, f32[6,8,128]{2,1,0:T(8,128)S(1)}, u32[]{:S(2)}, u32[]{:S(2)}) %collective-permute-start) | collective-permute-done | bytes 24608 | tf_op jit(solution)/shard_map/ppermute | solution.py:547
  7.3 1.1 %collective-permute-done.1.down_ref = f32[6,8,128]{2,1,0:T(8,128)S(1)} collective-permute-done((f32[6,8,128]{2,1,0:T(8,128)S(1)}, f32[6,8,128]{2,1,0:T(8,128)S(1)}, u32[]{:S(2)}, u32[]{:S(2)}) %collective-permute-start.1) | collective-permute-done | bytes 24608 | tf_op jit(solution)/shard_map/ppermute | solution.py:547
  8.4 0.2 %shard_map.48 = (f32[13,8,128]{2,1,0:T(8,128)S(1)}, f32[25,8,128]{2,1,0:T(8,128)S(1)}) custom-call(f32[10,8,128]{2,1,0:T(8,128)S(1)} %get-tuple-element.20.face_ref.own_face_ref, f32[10,8,128]{2,1,0:T(8,128)S(1)} %get-tuple-element.20.face_ref.own_face_ref, f32[6,8,128]{2,1,0:T(8,128)S(1)} %collective-permute-done.up_ref, ...), custom_call_target="tpu_custom_call" | custom-call | tf_op jit(solution)/shard_map/pallas_call | solution.py:505
  8.6 2.5 %collective-permute-start.4 = (f32[13,8,128]{2,1,0:T(8,128)S(1)}, f32[13,8,128]{2,1,0:T(8,128)S(1)}, u32[]{:S(2)}, u32[]{:S(2)}) collective-permute-start(f32[13,8,128]{2,1,0:T(8,128)S(1)} %get-tuple-element.24.refs_0_), channel_id=1, source_target_pairs={{0,24},{1,25},{2,26},{3,27},{4,28},{5,29},{6,30},{7,31},{8,16},{9,... | collective-permute-start | bytes 159752 | tf_op jit(solution)/shard_map/ppermute | solution.py:547
  11.2 0.0 collective-permute-start.3
  11.2 0.7 %collective-permute-start.2 = (f32[13,8,128]{2,1,0:T(8,128)S(1)}, f32[13,8,128]{2,1,0:T(8,128)S(1)}, u32[]{:S(2)}, u32[]{:S(2)}) collective-permute-start(f32[13,8,128]{2,1,0:T(8,128)S(1)} %get-tuple-element.24.refs_0_), channel_id=1, source_target_pairs={{0,12},{1,13},{2,14},{3,15},{4,8},{5,9},{6,10},{7,11},{8,4},{9,5},... | collective-permute-start | bytes 159752 | tf_op jit(solution)/shard_map/ppermute | solution.py:547
  11.9 0.0 collective-permute-start.5
  11.9 1.8 %collective-permute-done.4.refs_3_ = f32[13,8,128]{2,1,0:T(8,128)S(1)} collective-permute-done((f32[13,8,128]{2,1,0:T(8,128)S(1)}, f32[13,8,128]{2,1,0:T(8,128)S(1)}, u32[]{:S(2)}, u32[]{:S(2)}) %collective-permute-start.4) | collective-permute-done | bytes 53280 | tf_op jit(solution)/shard_map/ppermute | solution.py:547
  13.7 0.0 collective-permute-start.8
  13.7 1.1 %collective-permute-done.3.refs_2_ = f32[13,8,128]{2,1,0:T(8,128)S(1)} collective-permute-done((f32[13,8,128]{2,1,0:T(8,128)S(1)}, f32[13,8,128]{2,1,0:T(8,128)S(1)}, u32[]{:S(2)}, u32[]{:S(2)}) %collective-permute-start.3) | collective-permute-done | bytes 53280 | tf_op jit(solution)/shard_map/ppermute | solution.py:547
  14.9 0.0 collective-permute-start.7
  14.9 0.0 collective-permute-done.2.refs_1_
  14.9 0.5 %collective-permute-start.6 = (f32[13,8,128]{2,1,0:T(8,128)S(1)}, f32[13,8,128]{2,1,0:T(8,128)S(1)}, u32[]{:S(2)}, u32[]{:S(2)}) collective-permute-start(f32[13,8,128]{2,1,0:T(8,128)S(1)} %collective-permute-done.2.refs_1_), channel_id=1, source_target_pairs={{0,4},{1,5},{2,6},{3,7},{4,0},{5,1},{6,2},{7,3},{8,12},{9,13},{10,... | collective-permute-start | bytes 159752 | tf_op jit(solution)/shard_map/ppermute | solution.py:547
  15.4 0.3 %shard_map.49.own_ref = f32[3,8,1024]{2,1,0:T(8,128)S(1)} custom-call(f32[3,8,1024]{2,1,0:T(8,128)S(1)} %get-tuple-element.19.after_ref, f32[3,1,8,1024]{3,2,1,0:T(8,128)S(1)} %get-tuple-element.16.u_ref, f32[25,8,128]{2,1,0:T(8,128)S(1)} %get-tuple-element.23.near_ref), custom_call_target="tpu_custom_call" | custom-call | tf_op jit(solution)/shard_map/pallas_call | solution.py:505
  15.7 0.0 collective-permute-done.5.refs_4_
  15.7 0.0 collective-permute-done.8.refs_7_
  15.7 0.4 %collective-permute-done.7.refs_6_ = f32[13,8,128]{2,1,0:T(8,128)S(1)} collective-permute-done((f32[13,8,128]{2,1,0:T(8,128)S(1)}, f32[13,8,128]{2,1,0:T(8,128)S(1)}, u32[]{:S(2)}, u32[]{:S(2)}) %collective-permute-start.7) | collective-permute-done | bytes 53280 | tf_op jit(solution)/shard_map/ppermute | solution.py:547
  16.1 0.2 collective-permute-done.6.refs_5_
  16.3 1.2 %shard_map.50 = f32[3,1,8,1024]{3,2,1,0:T(8,128)} custom-call(f32[3,8,1024]{2,1,0:T(8,128)S(1)} %shard_map.49.own_ref, f32[3,1,8,1024]{3,2,1,0:T(8,128)S(1)} %get-tuple-element.16.u_ref, f32[13,8,128]{2,1,0:T(8,128)S(1)} %get-tuple-element.24.refs_0_, f32[13,8,128]{2,1,0:T(8,128)S(1)} %collective-permute-done.2.refs_1_, ...), custom_call_target="tpu_custom_call" | custom-call | tf_op jit(solution)/shard_map/pallas_call | solution.py:505
Async XLA Ops:
  1.2 6.1 %collective-permute-start = (f32[6,8,128]{2,1,0:T(8,128)S(1)}, f32[6,8,128]{2,1,0:T(8,128)S(1)}, u32[]{:S(2)}, u32[]{:S(2)}) collective-permute-start(f32[6,8,128]{2,1,0:T(8,128)S(1)} %get-tuple-element.21), channel_id=1, source_target_pairs={{0,1},{1,2},{2,3},{3,4},{4,5},{5,6},{6,7},{7,0},{8,9},{9,10},{10,1... | collective-permute-start | bytes 73736 | tf_op jit(solution)/shard_map/ppermute | solution.py:547
  4.3 4.1 %collective-permute-start.1 = (f32[6,8,128]{2,1,0:T(8,128)S(1)}, f32[6,8,128]{2,1,0:T(8,128)S(1)}, u32[]{:S(2)}, u32[]{:S(2)}) collective-permute-start(f32[6,8,128]{2,1,0:T(8,128)S(1)} %get-tuple-element.22), channel_id=1, source_target_pairs={{0,7},{1,0},{2,1},{3,2},{4,3},{5,4},{6,5},{7,6},{8,15},{9,8},{10,9... | collective-permute-start | bytes 73736 | tf_op jit(solution)/shard_map/ppermute | solution.py:547
  8.6 5.1 %collective-permute-start.4 = (f32[13,8,128]{2,1,0:T(8,128)S(1)}, f32[13,8,128]{2,1,0:T(8,128)S(1)}, u32[]{:S(2)}, u32[]{:S(2)}) collective-permute-start(f32[13,8,128]{2,1,0:T(8,128)S(1)} %get-tuple-element.24.refs_0_), channel_id=1, source_target_pairs={{0,24},{1,25},{2,26},{3,27},{4,28},{5,29},{6,30},{7,31},{8,16},{9,... | collective-permute-start | bytes 159752 | tf_op jit(solution)/shard_map/ppermute | solution.py:547
  11.2 3.7 %collective-permute-start.3 = (f32[13,8,128]{2,1,0:T(8,128)S(1)}, f32[13,8,128]{2,1,0:T(8,128)S(1)}, u32[]{:S(2)}, u32[]{:S(2)}) collective-permute-start(f32[13,8,128]{2,1,0:T(8,128)S(1)} %get-tuple-element.24.refs_0_), channel_id=1, source_target_pairs={{0,20},{1,21},{2,22},{3,23},{4,16},{5,17},{6,18},{7,19},{8,28},{9,... | collective-permute-start | bytes 159752 | tf_op jit(solution)/shard_map/ppermute | solution.py:547
  11.2 3.7 %collective-permute-start.2 = (f32[13,8,128]{2,1,0:T(8,128)S(1)}, f32[13,8,128]{2,1,0:T(8,128)S(1)}, u32[]{:S(2)}, u32[]{:S(2)}) collective-permute-start(f32[13,8,128]{2,1,0:T(8,128)S(1)} %get-tuple-element.24.refs_0_), channel_id=1, source_target_pairs={{0,12},{1,13},{2,14},{3,15},{4,8},{5,9},{6,10},{7,11},{8,4},{9,5},... | collective-permute-start | bytes 159752 | tf_op jit(solution)/shard_map/ppermute | solution.py:547
  11.9 3.8 %collective-permute-start.5 = (f32[13,8,128]{2,1,0:T(8,128)S(1)}, f32[13,8,128]{2,1,0:T(8,128)S(1)}, u32[]{:S(2)}, u32[]{:S(2)}) collective-permute-start(f32[13,8,128]{2,1,0:T(8,128)S(1)} %get-tuple-element.24.refs_0_), channel_id=1, source_target_pairs={{0,4},{1,5},{2,6},{3,7},{4,0},{5,1},{6,2},{7,3},{8,12},{9,13},{10,... | collective-permute-start | bytes 159752 | tf_op jit(solution)/shard_map/ppermute | solution.py:547
  13.7 2.0 %collective-permute-start.8 = (f32[13,8,128]{2,1,0:T(8,128)S(1)}, f32[13,8,128]{2,1,0:T(8,128)S(1)}, u32[]{:S(2)}, u32[]{:S(2)}) collective-permute-start(f32[13,8,128]{2,1,0:T(8,128)S(1)} %collective-permute-done.4.refs_3_), channel_id=1, source_target_pairs={{0,4},{1,5},{2,6},{3,7},{4,0},{5,1},{6,2},{7,3},{8,12},{9,13},{10,... | collective-permute-start | bytes 159752 | tf_op jit(solution)/shard_map/ppermute | solution.py:547
  14.9 1.2 %collective-permute-start.7 = (f32[13,8,128]{2,1,0:T(8,128)S(1)}, f32[13,8,128]{2,1,0:T(8,128)S(1)}, u32[]{:S(2)}, u32[]{:S(2)}) collective-permute-start(f32[13,8,128]{2,1,0:T(8,128)S(1)} %collective-permute-done.3.refs_2_), channel_id=1, source_target_pairs={{0,4},{1,5},{2,6},{3,7},{4,0},{5,1},{6,2},{7,3},{8,12},{9,13},{10,... | collective-permute-start | bytes 159752 | tf_op jit(solution)/shard_map/ppermute | solution.py:547
  14.9 1.4 %collective-permute-start.6 = (f32[13,8,128]{2,1,0:T(8,128)S(1)}, f32[13,8,128]{2,1,0:T(8,128)S(1)}, u32[]{:S(2)}, u32[]{:S(2)}) collective-permute-start(f32[13,8,128]{2,1,0:T(8,128)S(1)} %collective-permute-done.2.refs_1_), channel_id=1, source_target_pairs={{0,4},{1,5},{2,6},{3,7},{4,0},{5,1},{6,2},{7,3},{8,12},{9,13},{10,... | collective-permute-start | bytes 159752 | tf_op jit(solution)/shard_map/ppermute | solution.py:547

commit v6 on v5

--- a/solution.py
+++ b/solution.py
@@ -19,6 +19,7 @@
 PACKED = len(KEPT)
 ROW_U1_Y, ROW_U1_Z, ROW_U2_Z, ROW_CORNER, ROW_BESIDE = 0, 2, 4, 6, 7
 SENT = SPILLS + 1 + PACKED
+CROSSED = (2, 6)
 
 
 def iotas():
@@ -360,9 +361,7 @@
 
     def prepared(n, p, tile):
         held, other = block_refs[n][tile], block_refs[chips + n][tile]
-        held_by_second = (p == 1) == (2 * n not in (2, 4))
-        if tile > SPILLS:
-            held_by_second = not held_by_second
+        held_by_second = (p == 1) == (2 * n not in CROSSED)
         return jnp.where(second, held, other) if held_by_second else jnp.where(second, other, held)
 
     own_extra = block_refs[0][SPILLS] if paired else block_refs[0][here, SPILLS]
@@ -542,7 +541,7 @@
         pairs = []
         for b in range(blocks):
             for s in range(slabs):
-                c = b ^ d ^ (1 if paired and not 0 <= s + step < slabs else 0)
+                c = b ^ d
                 pairs.append((b * slabs + s, c * slabs + (s + step) % slabs))
         return lax.ppermute(array, ("blk", "sub"), pairs)
 
@@ -559,8 +558,11 @@
         down,
     )
     if paired:
-        held = [sent] + [moved(sent, d ^ (d in (2, 4))) for d in range(2, blocks, 2)]
-        arrays = held + [moved(array, 1) for array in held]
+        held, theirs = [sent], [moved(sent, 1)]
+        for d in range(2, blocks, 2):
+            held.append(moved(sent, d ^ (d in CROSSED)))
+            theirs.append(moved(sent, d ^ (d not in CROSSED)) if d == 2 else moved(held[-1], 1))
+        arrays = held + theirs
     else:
         arrays = [lax.all_gather(sent, "blk")]
     own = call(

time: 17.6 us -> 17.3 us (0.983)
  waiting for transfers between devices: 5.89 us -> 4.39 us
  starting transfers between devices: 8.41 us -> 9.59 us
    ppermute x9, waiting for transfers between devices: 5.89 us -> 4.39 us  [moved(): return lax.ppermute(array, ('blk', 'sub'), pairs)]
    ppermute x9, starting transfers between devices: 8.41 us -> 9.59 us  [moved(): return lax.ppermute(array, ('blk', 'sub'), pairs)]
where the time goes in v6:
time: 17.3 us; the launch traced here: 17.1 us
  starting transfers between devices  9.59 us (55%)
  waiting for transfers between devices  4.39 us (25%)
  Pallas kernels  3.1 us (18%)
    ppermute x9, starting transfers between devices, moved(): return lax.ppermute(array, ('blk', 'sub'), pairs)  9.59 us
    ppermute x9, waiting for transfers between devices, moved(): return lax.ppermute(array, ('blk', 'sub'), pairs)  4.39 us
    pallas_call x4, Pallas kernels, call(): pl.pallas_call(kernel, out_shape=out_shape, in_specs=[vmem] * len(args),...  1.91 us
    pallas_call x1, Pallas kernels, shards(): pl.pallas_call(functools.partial(spill_kernel, slab), out_shape=(shape(*v...  1.19 us
  transfers between devices with their start and end apart: 9, of which 6 were waited for; matrix products, arithmetic and copies ran while one was open for 0% of the time, Pallas kernels for 3%

profile of v6, /device:TPU:0, one launch (start us, length us, event | category | flops | bytes accessed | tf_op | source)
XLA Modules:
  0.0 17.1 jit_solution(15702265497797085742)
XLA Ops:
  0.0 1.2 %shard_map.46 = (f32[3,1,8,1024]{3,2,1,0:T(8,128)S(1)}, f32[3,1,8,1024]{3,2,1,0:T(8,128)S(1)}, f32[9,1,8,1024]{3,2,1,0:T(8,128)S(1)}, f32[6,8,128]{2,1,0:T(8,128...) custom-call(s32[1,6]{1,0:T(1,128)} %refs_0_.1, f32[3,1,8,1024]{3,2,1,0:T(8,128)} %refs_1_.1, ...), custom_call_target="tpu_custom_call" | custom-call | tf_op jit(solution)/shard_map/pallas_call | solution.py:513
  1.2 3.1 %collective-permute-start = (f32[6,8,128]{2,1,0:T(8,128)S(1)}, f32[6,8,128]{2,1,0:T(8,128)S(1)}, u32[]{:S(2)}, u32[]{:S(2)}) collective-permute-start(f32[6,8,128]{2,1,0:T(8,128)S(1)} %get-tuple-element.21), channel_id=1, source_target_pairs={{0,1},{1,2},{2,3},{3,0},{4,5},{5,6},{6,7},{7,4},{8,9},{9,10},{10,1... | collective-permute-start | bytes 73736 | tf_op jit(solution)/shard_map/ppermute | solution.py:546
  4.3 2.1 %collective-permute-start.1 = (f32[6,8,128]{2,1,0:T(8,128)S(1)}, f32[6,8,128]{2,1,0:T(8,128)S(1)}, u32[]{:S(2)}, u32[]{:S(2)}) collective-permute-start(f32[6,8,128]{2,1,0:T(8,128)S(1)} %get-tuple-element.22), channel_id=1, source_target_pairs={{0,3},{1,0},{2,1},{3,2},{4,7},{5,4},{6,5},{7,6},{8,11},{9,8},{10,9... | collective-permute-start | bytes 73736 | tf_op jit(solution)/shard_map/ppermute | solution.py:546
  6.4 0.2 %shard_map.47 = (f32[3,8,1024]{2,1,0:T(8,128)S(1)}, f32[10,8,128]{2,1,0:T(8,128)S(1)}) custom-call(f32[3,1,8,1024]{3,2,1,0:T(8,128)S(1)} %get-tuple-element.15.w_ref, f32[3,1,8,1024]{3,2,1,0:T(8,128)S(1)} %get-tuple-element.16.u_ref, f32[9,1,8,1024]{3,2,1,0:T(8,128)S(1)} %get-tuple-element.17.g_ref, f32[8,128]{1,0:T(8,128)S(1)} %get-tuple-element.18.meta_ref), custom_call_target="tpu_custom_call" | custom-call | tf_op jit(solution)/shard_map/pallas_call | solution.py:504
  6.5 1.7 %collective-permute-done.up_ref = f32[6,8,128]{2,1,0:T(8,128)S(1)} collective-permute-done((f32[6,8,128]{2,1,0:T(8,128)S(1)}, f32[6,8,128]{2,1,0:T(8,128)S(1)}, u32[]{:S(2)}, u32[]{:S(2)}) %collective-permute-start) | collective-permute-done | bytes 24608 | tf_op jit(solution)/shard_map/ppermute | solution.py:546
  8.2 0.2 collective-permute-done.1.down_ref
  8.4 0.2 %shard_map.48 = (f32[13,8,128]{2,1,0:T(8,128)S(1)}, f32[25,8,128]{2,1,0:T(8,128)S(1)}) custom-call(f32[10,8,128]{2,1,0:T(8,128)S(1)} %get-tuple-element.20.face_ref.own_face_ref, f32[10,8,128]{2,1,0:T(8,128)S(1)} %get-tuple-element.20.face_ref.own_face_ref, f32[6,8,128]{2,1,0:T(8,128)S(1)} %collective-permute-done.up_ref, ...), custom_call_target="tpu_custom_call" | custom-call | tf_op jit(solution)/shard_map/pallas_call | solution.py:504
  8.6 0.8 %collective-permute-start.4 = (f32[13,8,128]{2,1,0:T(8,128)S(1)}, f32[13,8,128]{2,1,0:T(8,128)S(1)}, u32[]{:S(2)}, u32[]{:S(2)}) collective-permute-start(f32[13,8,128]{2,1,0:T(8,128)S(1)} %get-tuple-element.24.refs_0_), channel_id=1, source_target_pairs={{0,28},{1,29},{2,30},{3,31},{4,24},{5,25},{6,26},{7,27},{8,20},{9,... | collective-permute-start | bytes 159752 | tf_op jit(solution)/shard_map/ppermute | solution.py:546
  9.4 0.8 %collective-permute-start.3 = (f32[13,8,128]{2,1,0:T(8,128)S(1)}, f32[13,8,128]{2,1,0:T(8,128)S(1)}, u32[]{:S(2)}, u32[]{:S(2)}) collective-permute-start(f32[13,8,128]{2,1,0:T(8,128)S(1)} %get-tuple-element.24.refs_0_), channel_id=1, source_target_pairs={{0,16},{1,17},{2,18},{3,19},{4,20},{5,21},{6,22},{7,23},{8,24},{9,... | collective-permute-start | bytes 159752 | tf_op jit(solution)/shard_map/ppermute | solution.py:546
  10.3 1.5 %collective-permute-start.6 = (f32[13,8,128]{2,1,0:T(8,128)S(1)}, f32[13,8,128]{2,1,0:T(8,128)S(1)}, u32[]{:S(2)}, u32[]{:S(2)}) collective-permute-start(f32[13,8,128]{2,1,0:T(8,128)S(1)} %get-tuple-element.24.refs_0_), channel_id=1, source_target_pairs={{0,8},{1,9},{2,10},{3,11},{4,12},{5,13},{6,14},{7,15},{8,0},{9,1},... | collective-permute-start | bytes 159752 | tf_op jit(solution)/shard_map/ppermute | solution.py:546
  11.8 0.0 collective-permute-start.5
  11.8 1.1 %collective-permute-start.2 = (f32[13,8,128]{2,1,0:T(8,128)S(1)}, f32[13,8,128]{2,1,0:T(8,128)S(1)}, u32[]{:S(2)}, u32[]{:S(2)}) collective-permute-start(f32[13,8,128]{2,1,0:T(8,128)S(1)} %get-tuple-element.24.refs_0_), channel_id=1, source_target_pairs={{0,12},{1,13},{2,14},{3,15},{4,8},{5,9},{6,10},{7,11},{8,4},{9,5},... | collective-permute-start | bytes 159752 | tf_op jit(solution)/shard_map/ppermute | solution.py:546
  12.8 0.8 %collective-permute-done.4.refs_3_ = f32[13,8,128]{2,1,0:T(8,128)S(1)} collective-permute-done((f32[13,8,128]{2,1,0:T(8,128)S(1)}, f32[13,8,128]{2,1,0:T(8,128)S(1)}, u32[]{:S(2)}, u32[]{:S(2)}) %collective-permute-start.4) | collective-permute-done | bytes 53280 | tf_op jit(solution)/shard_map/ppermute | solution.py:546
  13.7 0.1 collective-permute-start.8
  13.7 1.0 %collective-permute-done.3.refs_2_ = f32[13,8,128]{2,1,0:T(8,128)S(1)} collective-permute-done((f32[13,8,128]{2,1,0:T(8,128)S(1)}, f32[13,8,128]{2,1,0:T(8,128)S(1)}, u32[]{:S(2)}, u32[]{:S(2)}) %collective-permute-start.3) | collective-permute-done | bytes 53280 | tf_op jit(solution)/shard_map/ppermute | solution.py:546
  14.7 0.2 collective-permute-start.7
  14.9 0.3 %shard_map.49.own_ref = f32[3,8,1024]{2,1,0:T(8,128)S(1)} custom-call(f32[3,8,1024]{2,1,0:T(8,128)S(1)} %get-tuple-element.19.after_ref, f32[3,1,8,1024]{3,2,1,0:T(8,128)S(1)} %get-tuple-element.16.u_ref, f32[25,8,128]{2,1,0:T(8,128)S(1)} %get-tuple-element.23.near_ref), custom_call_target="tpu_custom_call" | custom-call | tf_op jit(solution)/shard_map/pallas_call | solution.py:504
  15.2 0.0 collective-permute-done.6.refs_5_
  15.2 0.0 collective-permute-done.5.refs_4_
  15.2 0.4 %collective-permute-done.2.refs_1_ = f32[13,8,128]{2,1,0:T(8,128)S(1)} collective-permute-done((f32[13,8,128]{2,1,0:T(8,128)S(1)}, f32[13,8,128]{2,1,0:T(8,128)S(1)}, u32[]{:S(2)}, u32[]{:S(2)}) %collective-permute-start.2) | collective-permute-done | bytes 53280 | tf_op jit(solution)/shard_map/ppermute | solution.py:546
  15.6 0.0 collective-permute-done.8.refs_7_
  15.6 0.3 %collective-permute-done.7.refs_6_ = f32[13,8,128]{2,1,0:T(8,128)S(1)} collective-permute-done((f32[13,8,128]{2,1,0:T(8,128)S(1)}, f32[13,8,128]{2,1,0:T(8,128)S(1)}, u32[]{:S(2)}, u32[]{:S(2)}) %collective-permute-start.7) | collective-permute-done | bytes 53280 | tf_op jit(solution)/shard_map/ppermute | solution.py:546
  16.0 1.2 %shard_map.50 = f32[3,1,8,1024]{3,2,1,0:T(8,128)} custom-call(f32[3,8,1024]{2,1,0:T(8,128)S(1)} %shard_map.49.own_ref, f32[3,1,8,1024]{3,2,1,0:T(8,128)S(1)} %get-tuple-element.16.u_ref, f32[13,8,128]{2,1,0:T(8,128)S(1)} %get-tuple-element.24.refs_0_, f32[13,8,128]{2,1,0:T(8,128)S(1)} %collective-permute-done.2.refs_1_, ...), custom_call_target="tpu_custom_call" | custom-call | tf_op jit(solution)/shard_map/pallas_call | solution.py:504
Async XLA Ops:
  1.2 7.0 %collective-permute-start = (f32[6,8,128]{2,1,0:T(8,128)S(1)}, f32[6,8,128]{2,1,0:T(8,128)S(1)}, u32[]{:S(2)}, u32[]{:S(2)}) collective-permute-start(f32[6,8,128]{2,1,0:T(8,128)S(1)} %get-tuple-element.21), channel_id=1, source_target_pairs={{0,1},{1,2},{2,3},{3,0},{4,5},{5,6},{6,7},{7,4},{8,9},{9,10},{10,1... | collective-permute-start | bytes 73736 | tf_op jit(solution)/shard_map/ppermute | solution.py:546
  4.3 4.1 %collective-permute-start.1 = (f32[6,8,128]{2,1,0:T(8,128)S(1)}, f32[6,8,128]{2,1,0:T(8,128)S(1)}, u32[]{:S(2)}, u32[]{:S(2)}) collective-permute-start(f32[6,8,128]{2,1,0:T(8,128)S(1)} %get-tuple-element.22), channel_id=1, source_target_pairs={{0,3},{1,0},{2,1},{3,2},{4,7},{5,4},{6,5},{7,6},{8,11},{9,8},{10,9... | collective-permute-start | bytes 73736 | tf_op jit(solution)/shard_map/ppermute | solution.py:546
  8.6 5.0 %collective-permute-start.4 = (f32[13,8,128]{2,1,0:T(8,128)S(1)}, f32[13,8,128]{2,1,0:T(8,128)S(1)}, u32[]{:S(2)}, u32[]{:S(2)}) collective-permute-start(f32[13,8,128]{2,1,0:T(8,128)S(1)} %get-tuple-element.24.refs_0_), channel_id=1, source_target_pairs={{0,28},{1,29},{2,30},{3,31},{4,24},{5,25},{6,26},{7,27},{8,20},{9,... | collective-permute-start | bytes 159752 | tf_op jit(solution)/shard_map/ppermute | solution.py:546
  9.4 5.3 %collective-permute-start.3 = (f32[13,8,128]{2,1,0:T(8,128)S(1)}, f32[13,8,128]{2,1,0:T(8,128)S(1)}, u32[]{:S(2)}, u32[]{:S(2)}) collective-permute-start(f32[13,8,128]{2,1,0:T(8,128)S(1)} %get-tuple-element.24.refs_0_), channel_id=1, source_target_pairs={{0,16},{1,17},{2,18},{3,19},{4,20},{5,21},{6,22},{7,23},{8,24},{9,... | collective-permute-start | bytes 159752 | tf_op jit(solution)/shard_map/ppermute | solution.py:546
  10.3 4.9 %collective-permute-start.6 = (f32[13,8,128]{2,1,0:T(8,128)S(1)}, f32[13,8,128]{2,1,0:T(8,128)S(1)}, u32[]{:S(2)}, u32[]{:S(2)}) collective-permute-start(f32[13,8,128]{2,1,0:T(8,128)S(1)} %get-tuple-element.24.refs_0_), channel_id=1, source_target_pairs={{0,8},{1,9},{2,10},{3,11},{4,12},{5,13},{6,14},{7,15},{8,0},{9,1},... | collective-permute-start | bytes 159752 | tf_op jit(solution)/shard_map/ppermute | solution.py:546
  11.8 3.4 %collective-permute-start.5 = (f32[13,8,128]{2,1,0:T(8,128)S(1)}, f32[13,8,128]{2,1,0:T(8,128)S(1)}, u32[]{:S(2)}, u32[]{:S(2)}) collective-permute-start(f32[13,8,128]{2,1,0:T(8,128)S(1)} %get-tuple-element.24.refs_0_), channel_id=1, source_target_pairs={{0,4},{1,5},{2,6},{3,7},{4,0},{5,1},{6,2},{7,3},{8,12},{9,13},{10,... | collective-permute-start | bytes 159752 | tf_op jit(solution)/shard_map/ppermute | solution.py:546
  11.8 3.8 %collective-permute-start.2 = (f32[13,8,128]{2,1,0:T(8,128)S(1)}, f32[13,8,128]{2,1,0:T(8,128)S(1)}, u32[]{:S(2)}, u32[]{:S(2)}) collective-permute-start(f32[13,8,128]{2,1,0:T(8,128)S(1)} %get-tuple-element.24.refs_0_), channel_id=1, source_target_pairs={{0,12},{1,13},{2,14},{3,15},{4,8},{5,9},{6,10},{7,11},{8,4},{9,5},... | collective-permute-start | bytes 159752 | tf_op jit(solution)/shard_map/ppermute | solution.py:546
  13.7 2.0 %collective-permute-start.8 = (f32[13,8,128]{2,1,0:T(8,128)S(1)}, f32[13,8,128]{2,1,0:T(8,128)S(1)}, u32[]{:S(2)}, u32[]{:S(2)}) collective-permute-start(f32[13,8,128]{2,1,0:T(8,128)S(1)} %collective-permute-done.4.refs_3_), channel_id=1, source_target_pairs={{0,4},{1,5},{2,6},{3,7},{4,0},{5,1},{6,2},{7,3},{8,12},{9,13},{10,... | collective-permute-start | bytes 159752 | tf_op jit(solution)/shard_map/ppermute | solution.py:546
  14.7 1.2 %collective-permute-start.7 = (f32[13,8,128]{2,1,0:T(8,128)S(1)}, f32[13,8,128]{2,1,0:T(8,128)S(1)}, u32[]{:S(2)}, u32[]{:S(2)}) collective-permute-start(f32[13,8,128]{2,1,0:T(8,128)S(1)} %collective-permute-done.3.refs_2_), channel_id=1, source_target_pairs={{0,4},{1,5},{2,6},{3,7},{4,0},{5,1},{6,2},{7,3},{8,12},{9,13},{10,... | collective-permute-start | bytes 159752 | tf_op jit(solution)/shard_map/ppermute | solution.py:546

commit v7 on v6

--- a/solution.py
+++ b/solution.py
@@ -225,6 +225,9 @@
     faces = [y_face(after[c]) for c in range(3)] + [z_face(after[c]) for c in range(3)]
     faces += [y_face(u1), z_face(u1), z_face(u2)]
     faces.append(extra_of(slab, slabs, faces, meta_ref[...]))
+    weight = weights(faces[U1_Z])
+    in_z = [y_pass_of_z_face(q, weight) for q in faces[AFTER_Z : AFTER_Z + 3]]
+    faces[:SPILLS] = y_spill(faces[:AFTER_Z], faces[U1_Y]) + z_spill(in_z, faces[U2_Z])
     for n, face in enumerate(faces):
         face_ref[n] = face
 
@@ -242,17 +245,16 @@
 
 
 def spills_of(slab, face_ref, up, down):
-    up, down = unpack(up), unpack(down)
-    up_y, up_z, down_y, down_z = y_face(up), z_face(up), y_face(down), z_face(down)
-    in_y, in_z = [], []
-    for c in range(3):
-        q = face_ref[AFTER_Y + c] + placed(up_y, c, 0) + placed(down_y, c, slab - 2)
-        in_y.append(q)
-        q = face_ref[AFTER_Z + c] + placed(up_z, c, 0) + placed(down_z, c, slab - 2)
-        in_z.append(q)
-    weight = weights(face_ref[U1_Z])
-    in_z = [y_pass_of_z_face(q, weight) for q in in_z]
-    return y_spill(in_y, face_ref[U1_Y]) + z_spill(in_z, face_ref[U2_Z])
+    spilt = [face_ref[n] for n in range(SPILLS)]
+    for packed, row in ((up, 0), (down, slab - 2)):
+        tiles = unpack(packed)
+        u1_y, u1_z, u2_z = (pair_rows(face_ref[n], row) for n in (U1_Y, U1_Z, U2_Z))
+        (by_y,) = y_spill([y_face(tiles)], u1_y)
+        (by_z,) = z_spill([y_pass_of_z_face(z_face(tiles), weights(u1_z))], u2_z)
+        for c in range(3):
+            spilt[c] = spilt[c] + placed(by_y, c, row)
+            spilt[3 + c] = spilt[3 + c] + placed(by_z, c, row)
+    return spilt
 
 
 def middle_kernel(slab, slabs, face_ref, own_face_ref, up_ref, down_ref, sent_ref, own_sent_ref):

time: 17.3 us -> 17.3 us (level)
  transfers between devices with their start and end apart: 9 -> 9, of which waited for: 6 -> 6; matrix products, arithmetic and copies ran while one was open for 0% -> 0% of each run, Pallas kernels for 3% -> 4%
where the time goes in v7:
time: 17.3 us; the launch traced here: 17.1 us
  starting transfers between devices  9.59 us (55%)
  waiting for transfers between devices  4.24 us (25%)
  Pallas kernels  3.25 us (19%)
    ppermute x9, starting transfers between devices, moved(): return lax.ppermute(array, ('blk', 'sub'), pairs)  9.59 us
    ppermute x9, waiting for transfers between devices, moved(): return lax.ppermute(array, ('blk', 'sub'), pairs)  4.24 us
    pallas_call x4, Pallas kernels, call(): pl.pallas_call(kernel, out_shape=out_shape, in_specs=[vmem] * len(args),...  2.06 us
    pallas_call x1, Pallas kernels, shards(): pl.pallas_call(functools.partial(spill_kernel, slab), out_shape=(shape(*v...  1.19 us
  transfers between devices with their start and end apart: 9, of which 6 were waited for; matrix products, arithmetic and copies ran while one was open for 0% of the time, Pallas kernels for 4%

profile of v7, /device:TPU:0, one launch (start us, length us, event | category | flops | bytes accessed | tf_op | source)
XLA Modules:
  0.0 17.1 jit_solution(11201415113952233822)
XLA Ops:
  0.0 1.2 %shard_map.46 = (f32[3,1,8,1024]{3,2,1,0:T(8,128)S(1)}, f32[3,1,8,1024]{3,2,1,0:T(8,128)S(1)}, f32[9,1,8,1024]{3,2,1,0:T(8,128)S(1)}, f32[6,8,128]{2,1,0:T(8,128...) custom-call(s32[1,6]{1,0:T(1,128)} %refs_0_.1, f32[3,1,8,1024]{3,2,1,0:T(8,128)} %refs_1_.1, ...), custom_call_target="tpu_custom_call" | custom-call | tf_op jit(solution)/shard_map/pallas_call | solution.py:515
  1.2 3.1 %collective-permute-start = (f32[6,8,128]{2,1,0:T(8,128)S(1)}, f32[6,8,128]{2,1,0:T(8,128)S(1)}, u32[]{:S(2)}, u32[]{:S(2)}) collective-permute-start(f32[6,8,128]{2,1,0:T(8,128)S(1)} %get-tuple-element.21), channel_id=1, source_target_pairs={{0,1},{1,2},{2,3},{3,0},{4,5},{5,6},{6,7},{7,4},{8,9},{9,10},{10,1... | collective-permute-start | bytes 73736 | tf_op jit(solution)/shard_map/ppermute | solution.py:548
  4.3 2.1 %collective-permute-start.1 = (f32[6,8,128]{2,1,0:T(8,128)S(1)}, f32[6,8,128]{2,1,0:T(8,128)S(1)}, u32[]{:S(2)}, u32[]{:S(2)}) collective-permute-start(f32[6,8,128]{2,1,0:T(8,128)S(1)} %get-tuple-element.22), channel_id=1, source_target_pairs={{0,3},{1,0},{2,1},{3,2},{4,7},{5,4},{6,5},{7,6},{8,11},{9,8},{10,9... | collective-permute-start | bytes 73736 | tf_op jit(solution)/shard_map/ppermute | solution.py:548
  6.4 0.3 %shard_map.47 = (f32[3,8,1024]{2,1,0:T(8,128)S(1)}, f32[10,8,128]{2,1,0:T(8,128)S(1)}) custom-call(f32[3,1,8,1024]{3,2,1,0:T(8,128)S(1)} %get-tuple-element.15.w_ref, f32[3,1,8,1024]{3,2,1,0:T(8,128)S(1)} %get-tuple-element.16.u_ref, f32[9,1,8,1024]{3,2,1,0:T(8,128)S(1)} %get-tuple-element.17.g_ref, f32[8,128]{1,0:T(8,128)S(1)} %get-tuple-element.18.meta_ref), custom_call_target="tpu_custom_call" | custom-call | tf_op jit(solution)/shard_map/pallas_call | solution.py:506
  6.7 1.5 %collective-permute-done.up_ref = f32[6,8,128]{2,1,0:T(8,128)S(1)} collective-permute-done((f32[6,8,128]{2,1,0:T(8,128)S(1)}, f32[6,8,128]{2,1,0:T(8,128)S(1)}, u32[]{:S(2)}, u32[]{:S(2)}) %collective-permute-start) | collective-permute-done | bytes 24608 | tf_op jit(solution)/shard_map/ppermute | solution.py:548
  8.2 0.2 collective-permute-done.1.down_ref
  8.4 0.2 %shard_map.48 = (f32[13,8,128]{2,1,0:T(8,128)S(1)}, f32[25,8,128]{2,1,0:T(8,128)S(1)}) custom-call(f32[10,8,128]{2,1,0:T(8,128)S(1)} %get-tuple-element.20.face_ref.own_face_ref, f32[10,8,128]{2,1,0:T(8,128)S(1)} %get-tuple-element.20.face_ref.own_face_ref, f32[6,8,128]{2,1,0:T(8,128)S(1)} %collective-permute-done.up_ref, ...), custom_call_target="tpu_custom_call" | custom-call | tf_op jit(solution)/shard_map/pallas_call | solution.py:506
  8.6 0.8 %collective-permute-start.4 = (f32[13,8,128]{2,1,0:T(8,128)S(1)}, f32[13,8,128]{2,1,0:T(8,128)S(1)}, u32[]{:S(2)}, u32[]{:S(2)}) collective-permute-start(f32[13,8,128]{2,1,0:T(8,128)S(1)} %get-tuple-element.24.refs_0_), channel_id=1, source_target_pairs={{0,28},{1,29},{2,30},{3,31},{4,24},{5,25},{6,26},{7,27},{8,20},{9,... | collective-permute-start | bytes 159752 | tf_op jit(solution)/shard_map/ppermute | solution.py:548
  9.4 0.8 %collective-permute-start.3 = (f32[13,8,128]{2,1,0:T(8,128)S(1)}, f32[13,8,128]{2,1,0:T(8,128)S(1)}, u32[]{:S(2)}, u32[]{:S(2)}) collective-permute-start(f32[13,8,128]{2,1,0:T(8,128)S(1)} %get-tuple-element.24.refs_0_), channel_id=1, source_target_pairs={{0,16},{1,17},{2,18},{3,19},{4,20},{5,21},{6,22},{7,23},{8,24},{9,... | collective-permute-start | bytes 159752 | tf_op jit(solution)/shard_map/ppermute | solution.py:548
  10.3 1.5 %collective-permute-start.6 = (f32[13,8,128]{2,1,0:T(8,128)S(1)}, f32[13,8,128]{2,1,0:T(8,128)S(1)}, u32[]{:S(2)}, u32[]{:S(2)}) collective-permute-start(f32[13,8,128]{2,1,0:T(8,128)S(1)} %get-tuple-element.24.refs_0_), channel_id=1, source_target_pairs={{0,8},{1,9},{2,10},{3,11},{4,12},{5,13},{6,14},{7,15},{8,0},{9,1},... | collective-permute-start | bytes 159752 | tf_op jit(solution)/shard_map/ppermute | solution.py:548
  11.8 0.0 collective-permute-start.5
  11.8 1.1 %collective-permute-start.2 = (f32[13,8,128]{2,1,0:T(8,128)S(1)}, f32[13,8,128]{2,1,0:T(8,128)S(1)}, u32[]{:S(2)}, u32[]{:S(2)}) collective-permute-start(f32[13,8,128]{2,1,0:T(8,128)S(1)} %get-tuple-element.24.refs_0_), channel_id=1, source_target_pairs={{0,12},{1,13},{2,14},{3,15},{4,8},{5,9},{6,10},{7,11},{8,4},{9,5},... | collective-permute-start | bytes 159752 | tf_op jit(solution)/shard_map/ppermute | solution.py:548
  12.8 0.8 %collective-permute-done.4.refs_3_ = f32[13,8,128]{2,1,0:T(8,128)S(1)} collective-permute-done((f32[13,8,128]{2,1,0:T(8,128)S(1)}, f32[13,8,128]{2,1,0:T(8,128)S(1)}, u32[]{:S(2)}, u32[]{:S(2)}) %collective-permute-start.4) | collective-permute-done | bytes 53280 | tf_op jit(solution)/shard_map/ppermute | solution.py:548
  13.7 0.1 collective-permute-start.8
  13.7 1.0 %collective-permute-done.3.refs_2_ = f32[13,8,128]{2,1,0:T(8,128)S(1)} collective-permute-done((f32[13,8,128]{2,1,0:T(8,128)S(1)}, f32[13,8,128]{2,1,0:T(8,128)S(1)}, u32[]{:S(2)}, u32[]{:S(2)}) %collective-permute-start.3) | collective-permute-done | bytes 53280 | tf_op jit(solution)/shard_map/ppermute | solution.py:548
  14.7 0.2 collective-permute-start.7
  14.9 0.3 %shard_map.49.own_ref = f32[3,8,1024]{2,1,0:T(8,128)S(1)} custom-call(f32[3,8,1024]{2,1,0:T(8,128)S(1)} %get-tuple-element.19.after_ref, f32[3,1,8,1024]{3,2,1,0:T(8,128)S(1)} %get-tuple-element.16.u_ref, f32[25,8,128]{2,1,0:T(8,128)S(1)} %get-tuple-element.23.near_ref), custom_call_target="tpu_custom_call" | custom-call | tf_op jit(solution)/shard_map/pallas_call | solution.py:506
  15.2 0.0 collective-permute-done.6.refs_5_
  15.2 0.0 collective-permute-done.5.refs_4_
  15.2 0.4 %collective-permute-done.2.refs_1_ = f32[13,8,128]{2,1,0:T(8,128)S(1)} collective-permute-done((f32[13,8,128]{2,1,0:T(8,128)S(1)}, f32[13,8,128]{2,1,0:T(8,128)S(1)}, u32[]{:S(2)}, u32[]{:S(2)}) %collective-permute-start.2) | collective-permute-done | bytes 53280 | tf_op jit(solution)/shard_map/ppermute | solution.py:548
  15.6 0.0 collective-permute-done.8.refs_7_
  15.6 0.3 %collective-permute-done.7.refs_6_ = f32[13,8,128]{2,1,0:T(8,128)S(1)} collective-permute-done((f32[13,8,128]{2,1,0:T(8,128)S(1)}, f32[13,8,128]{2,1,0:T(8,128)S(1)}, u32[]{:S(2)}, u32[]{:S(2)}) %collective-permute-start.7) | collective-permute-done | bytes 53280 | tf_op jit(solution)/shard_map/ppermute | solution.py:548
  16.0 1.2 %shard_map.50 = f32[3,1,8,1024]{3,2,1,0:T(8,128)} custom-call(f32[3,8,1024]{2,1,0:T(8,128)S(1)} %shard_map.49.own_ref, f32[3,1,8,1024]{3,2,1,0:T(8,128)S(1)} %get-tuple-element.16.u_ref, f32[13,8,128]{2,1,0:T(8,128)S(1)} %get-tuple-element.24.refs_0_, f32[13,8,128]{2,1,0:T(8,128)S(1)} %collective-permute-done.2.refs_1_, ...), custom_call_target="tpu_custom_call" | custom-call | tf_op jit(solution)/shard_map/pallas_call | solution.py:506
Async XLA Ops:
  1.2 7.0 %collective-permute-start = (f32[6,8,128]{2,1,0:T(8,128)S(1)}, f32[6,8,128]{2,1,0:T(8,128)S(1)}, u32[]{:S(2)}, u32[]{:S(2)}) collective-permute-start(f32[6,8,128]{2,1,0:T(8,128)S(1)} %get-tuple-element.21), channel_id=1, source_target_pairs={{0,1},{1,2},{2,3},{3,0},{4,5},{5,6},{6,7},{7,4},{8,9},{9,10},{10,1... | collective-permute-start | bytes 73736 | tf_op jit(solution)/shard_map/ppermute | solution.py:548
  4.3 4.1 %collective-permute-start.1 = (f32[6,8,128]{2,1,0:T(8,128)S(1)}, f32[6,8,128]{2,1,0:T(8,128)S(1)}, u32[]{:S(2)}, u32[]{:S(2)}) collective-permute-start(f32[6,8,128]{2,1,0:T(8,128)S(1)} %get-tuple-element.22), channel_id=1, source_target_pairs={{0,3},{1,0},{2,1},{3,2},{4,7},{5,4},{6,5},{7,6},{8,11},{9,8},{10,9... | collective-permute-start | bytes 73736 | tf_op jit(solution)/shard_map/ppermute | solution.py:548
  8.6 5.0 %collective-permute-start.4 = (f32[13,8,128]{2,1,0:T(8,128)S(1)}, f32[13,8,128]{2,1,0:T(8,128)S(1)}, u32[]{:S(2)}, u32[]{:S(2)}) collective-permute-start(f32[13,8,128]{2,1,0:T(8,128)S(1)} %get-tuple-element.24.refs_0_), channel_id=1, source_target_pairs={{0,28},{1,29},{2,30},{3,31},{4,24},{5,25},{6,26},{7,27},{8,20},{9,... | collective-permute-start | bytes 159752 | tf_op jit(solution)/shard_map/ppermute | solution.py:548
  9.4 5.3 %collective-permute-start.3 = (f32[13,8,128]{2,1,0:T(8,128)S(1)}, f32[13,8,128]{2,1,0:T(8,128)S(1)}, u32[]{:S(2)}, u32[]{:S(2)}) collective-permute-start(f32[13,8,128]{2,1,0:T(8,128)S(1)} %get-tuple-element.24.refs_0_), channel_id=1, source_target_pairs={{0,16},{1,17},{2,18},{3,19},{4,20},{5,21},{6,22},{7,23},{8,24},{9,... | collective-permute-start | bytes 159752 | tf_op jit(solution)/shard_map/ppermute | solution.py:548
  10.3 4.9 %collective-permute-start.6 = (f32[13,8,128]{2,1,0:T(8,128)S(1)}, f32[13,8,128]{2,1,0:T(8,128)S(1)}, u32[]{:S(2)}, u32[]{:S(2)}) collective-permute-start(f32[13,8,128]{2,1,0:T(8,128)S(1)} %get-tuple-element.24.refs_0_), channel_id=1, source_target_pairs={{0,8},{1,9},{2,10},{3,11},{4,12},{5,13},{6,14},{7,15},{8,0},{9,1},... | collective-permute-start | bytes 159752 | tf_op jit(solution)/shard_map/ppermute | solution.py:548
  11.8 3.4 %collective-permute-start.5 = (f32[13,8,128]{2,1,0:T(8,128)S(1)}, f32[13,8,128]{2,1,0:T(8,128)S(1)}, u32[]{:S(2)}, u32[]{:S(2)}) collective-permute-start(f32[13,8,128]{2,1,0:T(8,128)S(1)} %get-tuple-element.24.refs_0_), channel_id=1, source_target_pairs={{0,4},{1,5},{2,6},{3,7},{4,0},{5,1},{6,2},{7,3},{8,12},{9,13},{10,... | collective-permute-start | bytes 159752 | tf_op jit(solution)/shard_map/ppermute | solution.py:548
  11.8 3.8 %collective-permute-start.2 = (f32[13,8,128]{2,1,0:T(8,128)S(1)}, f32[13,8,128]{2,1,0:T(8,128)S(1)}, u32[]{:S(2)}, u32[]{:S(2)}) collective-permute-start(f32[13,8,128]{2,1,0:T(8,128)S(1)} %get-tuple-element.24.refs_0_), channel_id=1, source_target_pairs={{0,12},{1,13},{2,14},{3,15},{4,8},{5,9},{6,10},{7,11},{8,4},{9,5},... | collective-permute-start | bytes 159752 | tf_op jit(solution)/shard_map/ppermute | solution.py:548
  13.7 2.0 %collective-permute-start.8 = (f32[13,8,128]{2,1,0:T(8,128)S(1)}, f32[13,8,128]{2,1,0:T(8,128)S(1)}, u32[]{:S(2)}, u32[]{:S(2)}) collective-permute-start(f32[13,8,128]{2,1,0:T(8,128)S(1)} %collective-permute-done.4.refs_3_), channel_id=1, source_target_pairs={{0,4},{1,5},{2,6},{3,7},{4,0},{5,1},{6,2},{7,3},{8,12},{9,13},{10,... | collective-permute-start | bytes 159752 | tf_op jit(solution)/shard_map/ppermute | solution.py:548
  14.7 1.2 %collective-permute-start.7 = (f32[13,8,128]{2,1,0:T(8,128)S(1)}, f32[13,8,128]{2,1,0:T(8,128)S(1)}, u32[]{:S(2)}, u32[]{:S(2)}) collective-permute-start(f32[13,8,128]{2,1,0:T(8,128)S(1)} %collective-permute-done.3.refs_2_), channel_id=1, source_target_pairs={{0,4},{1,5},{2,6},{3,7},{4,0},{5,1},{6,2},{7,3},{8,12},{9,13},{10,... | collective-permute-start | bytes 159752 | tf_op jit(solution)/shard_map/ppermute | solution.py:548

commit v8 on v7

--- a/solution.py
+++ b/solution.py
@@ -177,7 +177,7 @@
         pltpu.make_async_copy(source, target, sems.at[n])
         for n, (source, target) in enumerate(zip(here, (nb_ref, w_ref, u_ref, g_ref)))
     ]
-    for copy in copies:
+    for copy in copies[::-1]:
         copy.start()
     for copy in copies:
         copy.wait()

time: 17.3 us -> 17.2 us (level)
  no operation moved by 1% of the time
where the time goes in v8:
time: 17.2 us; the launch traced here: 17.1 us
  starting transfers between devices  9.59 us (56%)
  waiting for transfers between devices  4.24 us (25%)
  Pallas kernels  3.22 us (19%)
    ppermute x9, starting transfers between devices, moved(): return lax.ppermute(array, ('blk', 'sub'), pairs)  9.59 us
    ppermute x9, waiting for transfers between devices, moved(): return lax.ppermute(array, ('blk', 'sub'), pairs)  4.24 us
    pallas_call x4, Pallas kernels, call(): pl.pallas_call(kernel, out_shape=out_shape, in_specs=[vmem] * len(args),...  2.06 us
    pallas_call x1, Pallas kernels, shards(): pl.pallas_call(functools.partial(spill_kernel, slab), out_shape=(shape(*v...  1.16 us
  transfers between devices with their start and end apart: 9, of which 6 were waited for; matrix products, arithmetic and copies ran while one was open for 0% of the time, Pallas kernels for 4%

profile of v8, /device:TPU:0, one launch (start us, length us, event | category | flops | bytes accessed | tf_op | source)
XLA Modules:
  0.0 17.1 jit_solution(7309150314011795250)
XLA Ops:
  0.0 1.2 %shard_map.46 = (f32[3,1,8,1024]{3,2,1,0:T(8,128)S(1)}, f32[3,1,8,1024]{3,2,1,0:T(8,128)S(1)}, f32[9,1,8,1024]{3,2,1,0:T(8,128)S(1)}, f32[6,8,128]{2,1,0:T(8,128...) custom-call(s32[1,6]{1,0:T(1,128)} %refs_0_.1, f32[3,1,8,1024]{3,2,1,0:T(8,128)} %refs_1_.1, ...), custom_call_target="tpu_custom_call" | custom-call | tf_op jit(solution)/shard_map/pallas_call | solution.py:515
  1.2 3.1 %collective-permute-start = (f32[6,8,128]{2,1,0:T(8,128)S(1)}, f32[6,8,128]{2,1,0:T(8,128)S(1)}, u32[]{:S(2)}, u32[]{:S(2)}) collective-permute-start(f32[6,8,128]{2,1,0:T(8,128)S(1)} %get-tuple-element.21), channel_id=1, source_target_pairs={{0,1},{1,2},{2,3},{3,0},{4,5},{5,6},{6,7},{7,4},{8,9},{9,10},{10,1... | collective-permute-start | bytes 73736 | tf_op jit(solution)/shard_map/ppermute | solution.py:548
  4.2 2.1 %collective-permute-start.1 = (f32[6,8,128]{2,1,0:T(8,128)S(1)}, f32[6,8,128]{2,1,0:T(8,128)S(1)}, u32[]{:S(2)}, u32[]{:S(2)}) collective-permute-start(f32[6,8,128]{2,1,0:T(8,128)S(1)} %get-tuple-element.22), channel_id=1, source_target_pairs={{0,3},{1,0},{2,1},{3,2},{4,7},{5,4},{6,5},{7,6},{8,11},{9,8},{10,9... | collective-permute-start | bytes 73736 | tf_op jit(solution)/shard_map/ppermute | solution.py:548
  6.3 0.3 %shard_map.47 = (f32[3,8,1024]{2,1,0:T(8,128)S(1)}, f32[10,8,128]{2,1,0:T(8,128)S(1)}) custom-call(f32[3,1,8,1024]{3,2,1,0:T(8,128)S(1)} %get-tuple-element.15.w_ref, f32[3,1,8,1024]{3,2,1,0:T(8,128)S(1)} %get-tuple-element.16.u_ref, f32[9,1,8,1024]{3,2,1,0:T(8,128)S(1)} %get-tuple-element.17.g_ref, f32[8,128]{1,0:T(8,128)S(1)} %get-tuple-element.18.meta_ref), custom_call_target="tpu_custom_call" | custom-call | tf_op jit(solution)/shard_map/pallas_call | solution.py:506
  6.7 1.5 %collective-permute-done.up_ref = f32[6,8,128]{2,1,0:T(8,128)S(1)} collective-permute-done((f32[6,8,128]{2,1,0:T(8,128)S(1)}, f32[6,8,128]{2,1,0:T(8,128)S(1)}, u32[]{:S(2)}, u32[]{:S(2)}) %collective-permute-start) | collective-permute-done | bytes 24608 | tf_op jit(solution)/shard_map/ppermute | solution.py:548
  8.2 0.2 collective-permute-done.1.down_ref
  8.3 0.2 %shard_map.48 = (f32[13,8,128]{2,1,0:T(8,128)S(1)}, f32[25,8,128]{2,1,0:T(8,128)S(1)}) custom-call(f32[10,8,128]{2,1,0:T(8,128)S(1)} %get-tuple-element.20.face_ref.own_face_ref, f32[10,8,128]{2,1,0:T(8,128)S(1)} %get-tuple-element.20.face_ref.own_face_ref, f32[6,8,128]{2,1,0:T(8,128)S(1)} %collective-permute-done.up_ref, ...), custom_call_target="tpu_custom_call" | custom-call | tf_op jit(solution)/shard_map/pallas_call | solution.py:506
  8.6 0.8 %collective-permute-start.4 = (f32[13,8,128]{2,1,0:T(8,128)S(1)}, f32[13,8,128]{2,1,0:T(8,128)S(1)}, u32[]{:S(2)}, u32[]{:S(2)}) collective-permute-start(f32[13,8,128]{2,1,0:T(8,128)S(1)} %get-tuple-element.24.refs_0_), channel_id=1, source_target_pairs={{0,28},{1,29},{2,30},{3,31},{4,24},{5,25},{6,26},{7,27},{8,20},{9,... | collective-permute-start | bytes 159752 | tf_op jit(solution)/shard_map/ppermute | solution.py:548
  9.4 0.8 %collective-permute-start.3 = (f32[13,8,128]{2,1,0:T(8,128)S(1)}, f32[13,8,128]{2,1,0:T(8,128)S(1)}, u32[]{:S(2)}, u32[]{:S(2)}) collective-permute-start(f32[13,8,128]{2,1,0:T(8,128)S(1)} %get-tuple-element.24.refs_0_), channel_id=1, source_target_pairs={{0,16},{1,17},{2,18},{3,19},{4,20},{5,21},{6,22},{7,23},{8,24},{9,... | collective-permute-start | bytes 159752 | tf_op jit(solution)/shard_map/ppermute | solution.py:548
  10.3 1.5 %collective-permute-start.6 = (f32[13,8,128]{2,1,0:T(8,128)S(1)}, f32[13,8,128]{2,1,0:T(8,128)S(1)}, u32[]{:S(2)}, u32[]{:S(2)}) collective-permute-start(f32[13,8,128]{2,1,0:T(8,128)S(1)} %get-tuple-element.24.refs_0_), channel_id=1, source_target_pairs={{0,8},{1,9},{2,10},{3,11},{4,12},{5,13},{6,14},{7,15},{8,0},{9,1},... | collective-permute-start | bytes 159752 | tf_op jit(solution)/shard_map/ppermute | solution.py:548
  11.7 0.0 collective-permute-start.5
  11.7 1.1 %collective-permute-start.2 = (f32[13,8,128]{2,1,0:T(8,128)S(1)}, f32[13,8,128]{2,1,0:T(8,128)S(1)}, u32[]{:S(2)}, u32[]{:S(2)}) collective-permute-start(f32[13,8,128]{2,1,0:T(8,128)S(1)} %get-tuple-element.24.refs_0_), channel_id=1, source_target_pairs={{0,12},{1,13},{2,14},{3,15},{4,8},{5,9},{6,10},{7,11},{8,4},{9,5},... | collective-permute-start | bytes 159752 | tf_op jit(solution)/shard_map/ppermute | solution.py:548
  12.8 0.8 %collective-permute-done.4.refs_3_ = f32[13,8,128]{2,1,0:T(8,128)S(1)} collective-permute-done((f32[13,8,128]{2,1,0:T(8,128)S(1)}, f32[13,8,128]{2,1,0:T(8,128)S(1)}, u32[]{:S(2)}, u32[]{:S(2)}) %collective-permute-start.4) | collective-permute-done | bytes 53280 | tf_op jit(solution)/shard_map/ppermute | solution.py:548
  13.6 0.1 collective-permute-start.8
  13.7 1.0 %collective-permute-done.3.refs_2_ = f32[13,8,128]{2,1,0:T(8,128)S(1)} collective-permute-done((f32[13,8,128]{2,1,0:T(8,128)S(1)}, f32[13,8,128]{2,1,0:T(8,128)S(1)}, u32[]{:S(2)}, u32[]{:S(2)}) %collective-permute-start.3) | collective-permute-done | bytes 53280 | tf_op jit(solution)/shard_map/ppermute | solution.py:548
  14.7 0.2 collective-permute-start.7
  14.8 0.3 %shard_map.49.own_ref = f32[3,8,1024]{2,1,0:T(8,128)S(1)} custom-call(f32[3,8,1024]{2,1,0:T(8,128)S(1)} %get-tuple-element.19.after_ref, f32[3,1,8,1024]{3,2,1,0:T(8,128)S(1)} %get-tuple-element.16.u_ref, f32[25,8,128]{2,1,0:T(8,128)S(1)} %get-tuple-element.23.near_ref), custom_call_target="tpu_custom_call" | custom-call | tf_op jit(solution)/shard_map/pallas_call | solution.py:506
  15.2 0.0 collective-permute-done.6.refs_5_
  15.2 0.0 collective-permute-done.5.refs_4_
  15.2 0.4 %collective-permute-done.2.refs_1_ = f32[13,8,128]{2,1,0:T(8,128)S(1)} collective-permute-done((f32[13,8,128]{2,1,0:T(8,128)S(1)}, f32[13,8,128]{2,1,0:T(8,128)S(1)}, u32[]{:S(2)}, u32[]{:S(2)}) %collective-permute-start.2) | collective-permute-done | bytes 53280 | tf_op jit(solution)/shard_map/ppermute | solution.py:548
  15.6 0.0 collective-permute-done.8.refs_7_
  15.6 0.3 %collective-permute-done.7.refs_6_ = f32[13,8,128]{2,1,0:T(8,128)S(1)} collective-permute-done((f32[13,8,128]{2,1,0:T(8,128)S(1)}, f32[13,8,128]{2,1,0:T(8,128)S(1)}, u32[]{:S(2)}, u32[]{:S(2)}) %collective-permute-start.7) | collective-permute-done | bytes 53280 | tf_op jit(solution)/shard_map/ppermute | solution.py:548
  15.9 1.2 %shard_map.50 = f32[3,1,8,1024]{3,2,1,0:T(8,128)} custom-call(f32[3,8,1024]{2,1,0:T(8,128)S(1)} %shard_map.49.own_ref, f32[3,1,8,1024]{3,2,1,0:T(8,128)S(1)} %get-tuple-element.16.u_ref, f32[13,8,128]{2,1,0:T(8,128)S(1)} %get-tuple-element.24.refs_0_, f32[13,8,128]{2,1,0:T(8,128)S(1)} %collective-permute-done.2.refs_1_, ...), custom_call_target="tpu_custom_call" | custom-call | tf_op jit(solution)/shard_map/pallas_call | solution.py:506
Async XLA Ops:
  1.2 7.0 %collective-permute-start = (f32[6,8,128]{2,1,0:T(8,128)S(1)}, f32[6,8,128]{2,1,0:T(8,128)S(1)}, u32[]{:S(2)}, u32[]{:S(2)}) collective-permute-start(f32[6,8,128]{2,1,0:T(8,128)S(1)} %get-tuple-element.21), channel_id=1, source_target_pairs={{0,1},{1,2},{2,3},{3,0},{4,5},{5,6},{6,7},{7,4},{8,9},{9,10},{10,1... | collective-permute-start | bytes 73736 | tf_op jit(solution)/shard_map/ppermute | solution.py:548
  4.2 4.1 %collective-permute-start.1 = (f32[6,8,128]{2,1,0:T(8,128)S(1)}, f32[6,8,128]{2,1,0:T(8,128)S(1)}, u32[]{:S(2)}, u32[]{:S(2)}) collective-permute-start(f32[6,8,128]{2,1,0:T(8,128)S(1)} %get-tuple-element.22), channel_id=1, source_target_pairs={{0,3},{1,0},{2,1},{3,2},{4,7},{5,4},{6,5},{7,6},{8,11},{9,8},{10,9... | collective-permute-start | bytes 73736 | tf_op jit(solution)/shard_map/ppermute | solution.py:548
  8.6 5.0 %collective-permute-start.4 = (f32[13,8,128]{2,1,0:T(8,128)S(1)}, f32[13,8,128]{2,1,0:T(8,128)S(1)}, u32[]{:S(2)}, u32[]{:S(2)}) collective-permute-start(f32[13,8,128]{2,1,0:T(8,128)S(1)} %get-tuple-element.24.refs_0_), channel_id=1, source_target_pairs={{0,28},{1,29},{2,30},{3,31},{4,24},{5,25},{6,26},{7,27},{8,20},{9,... | collective-permute-start | bytes 159752 | tf_op jit(solution)/shard_map/ppermute | solution.py:548
  9.4 5.3 %collective-permute-start.3 = (f32[13,8,128]{2,1,0:T(8,128)S(1)}, f32[13,8,128]{2,1,0:T(8,128)S(1)}, u32[]{:S(2)}, u32[]{:S(2)}) collective-permute-start(f32[13,8,128]{2,1,0:T(8,128)S(1)} %get-tuple-element.24.refs_0_), channel_id=1, source_target_pairs={{0,16},{1,17},{2,18},{3,19},{4,20},{5,21},{6,22},{7,23},{8,24},{9,... | collective-permute-start | bytes 159752 | tf_op jit(solution)/shard_map/ppermute | solution.py:548
  10.3 4.9 %collective-permute-start.6 = (f32[13,8,128]{2,1,0:T(8,128)S(1)}, f32[13,8,128]{2,1,0:T(8,128)S(1)}, u32[]{:S(2)}, u32[]{:S(2)}) collective-permute-start(f32[13,8,128]{2,1,0:T(8,128)S(1)} %get-tuple-element.24.refs_0_), channel_id=1, source_target_pairs={{0,8},{1,9},{2,10},{3,11},{4,12},{5,13},{6,14},{7,15},{8,0},{9,1},... | collective-permute-start | bytes 159752 | tf_op jit(solution)/shard_map/ppermute | solution.py:548
  11.7 3.4 %collective-permute-start.5 = (f32[13,8,128]{2,1,0:T(8,128)S(1)}, f32[13,8,128]{2,1,0:T(8,128)S(1)}, u32[]{:S(2)}, u32[]{:S(2)}) collective-permute-start(f32[13,8,128]{2,1,0:T(8,128)S(1)} %get-tuple-element.24.refs_0_), channel_id=1, source_target_pairs={{0,4},{1,5},{2,6},{3,7},{4,0},{5,1},{6,2},{7,3},{8,12},{9,13},{10,... | collective-permute-start | bytes 159752 | tf_op jit(solution)/shard_map/ppermute | solution.py:548
  11.7 3.8 %collective-permute-start.2 = (f32[13,8,128]{2,1,0:T(8,128)S(1)}, f32[13,8,128]{2,1,0:T(8,128)S(1)}, u32[]{:S(2)}, u32[]{:S(2)}) collective-permute-start(f32[13,8,128]{2,1,0:T(8,128)S(1)} %get-tuple-element.24.refs_0_), channel_id=1, source_target_pairs={{0,12},{1,13},{2,14},{3,15},{4,8},{5,9},{6,10},{7,11},{8,4},{9,5},... | collective-permute-start | bytes 159752 | tf_op jit(solution)/shard_map/ppermute | solution.py:548
  13.6 2.0 %collective-permute-start.8 = (f32[13,8,128]{2,1,0:T(8,128)S(1)}, f32[13,8,128]{2,1,0:T(8,128)S(1)}, u32[]{:S(2)}, u32[]{:S(2)}) collective-permute-start(f32[13,8,128]{2,1,0:T(8,128)S(1)} %collective-permute-done.4.refs_3_), channel_id=1, source_target_pairs={{0,4},{1,5},{2,6},{3,7},{4,0},{5,1},{6,2},{7,3},{8,12},{9,13},{10,... | collective-permute-start | bytes 159752 | tf_op jit(solution)/shard_map/ppermute | solution.py:548
  14.7 1.2 %collective-permute-start.7 = (f32[13,8,128]{2,1,0:T(8,128)S(1)}, f32[13,8,128]{2,1,0:T(8,128)S(1)}, u32[]{:S(2)}, u32[]{:S(2)}) collective-permute-start(f32[13,8,128]{2,1,0:T(8,128)S(1)} %collective-permute-done.3.refs_2_), channel_id=1, source_target_pairs={{0,4},{1,5},{2,6},{3,7},{4,0},{5,1},{6,2},{7,3},{8,12},{9,13},{10,... | collective-permute-start | bytes 159752 | tf_op jit(solution)/shard_map/ppermute | solution.py:548
